TPU v7x, 32 devices: a whole 2x2x4 slice. The times are simulated.
32 devices in a mesh: groups: 2 (over y), ctx: 4 (over z), head: 2 (over x), sub: 2 (over core).
Axes of the slice: x: 2, y: 2, z: 4, core: 2. Of those that a mesh axis runs over, the one named last changes fastest.
Arguments:
- queries: bfloat16 [16384, 4096], P(('groups', 'ctx', 'sub'), 'head'), parts along dimension 0, may hold values from -6 to 6
- keys: bfloat16 [16384, 4096], P(('groups', 'ctx', 'sub'), 'head'), parts along dimension 0, may hold values from -6 to 6
- values: bfloat16 [16384, 4096], P(('groups', 'ctx', 'sub'), 'head'), parts along dimension 0, may hold values from -6 to 6
- out_weight: bfloat16 [4096, 4096], P('head', ('ctx', 'sub')), may hold values from -0.09375 to 0.09375
- norm_gain: float32 [4096], P('head'), may hold values from 0.1 to 1.9
Outputs:
- layer_out: bfloat16 [16384, 4096], P(('groups', 'ctx', 'sub'), 'head'), parts along dimension 0
There are 2 independent parts, one for each index of `groups`. A program takes and returns all parts, laid end to end along the dimension named above; an argument that names none is the same for every part. Nothing has to cross between parts.
All inputs are finite; a program needn't handle non-finite values.
Results may differ from a plain program's by a relative error of at most 0.0052.
Values may be sent and summed in bfloat16 or wider, within the bound.
No kernel may reach another device: no remote copies, remote signals or barrier semaphores. Data moves between devices by JAX's collectives and lax.ppermute only.
A program may use at most 128 MiB of HBM per device.

v0:
```python
import jax
import jax.numpy as jnp
from jax import lax
from jax.sharding import PartitionSpec as P

DH = 128


def local(queries, keys, values, out_weight, norm_gain):
    tok_rows = queries.shape[0]
    head_count = queries.shape[1] // DH
    query_blk = queries.reshape(tok_rows, head_count, DH)
    key_blk = keys.reshape(tok_rows, head_count, DH)
    value_blk = values.reshape(tok_rows, head_count, DH)
    local_state = jnp.einsum("khd,khe->hde", key_blk, value_blk, preferred_element_type=jnp.float32)
    my_block = lax.axis_index(("ctx", "sub"))
    piece = lax.all_gather(local_state[None], ("ctx", "sub"), axis=0, tiled=True)
    count = piece.shape[0]
    earlier = jnp.arange(count, dtype=jnp.int32) < my_block
    prefix_state = jnp.sum(jnp.where(earlier[:, None, None, None], piece, 0.0), axis=0)
    scores = jnp.einsum("qhd,khd->hqk", query_blk, key_blk, preferred_element_type=jnp.float32)
    row_ids = lax.broadcasted_iota(jnp.int32, (tok_rows, tok_rows), 0)
    col_ids = lax.broadcasted_iota(jnp.int32, (tok_rows, tok_rows), 1)
    causal = (col_ids <= row_ids)[None, :, :]
    weights = jnp.where(causal, scores, 0.0).astype(jnp.bfloat16)
    intra = jnp.einsum("hqk,khd->qhd", weights, value_blk, preferred_element_type=jnp.float32)
    inter = jnp.einsum(
        "qhd,hde->qhe", query_blk.astype(jnp.float32), prefix_state, precision=lax.Precision.HIGHEST
    )
    mixed = intra + inter
    mean_sq = jnp.mean(mixed * mixed, axis=-1, keepdims=True)
    gain = norm_gain.reshape(head_count, DH)
    normed = (mixed * lax.rsqrt(mean_sq + 1e-06) * gain).astype(jnp.bfloat16)
    normed = normed.reshape(tok_rows, head_count * DH)
    partial_out = jnp.dot(
        normed,
        lax.all_gather(out_weight, ("ctx", "sub"), axis=1, tiled=True),
        preferred_element_type=jnp.float32,
    )
    return lax.psum_scatter(partial_out, "head", scatter_dimension=1, tiled=True).astype(
        jnp.bfloat16
    )


def solution(mesh):
    return jax.shard_map(
        local,
        mesh=mesh,
        in_specs=(
            P(("groups", "ctx", "sub"), "head"),
            P(("groups", "ctx", "sub"), "head"),
            P(("groups", "ctx", "sub"), "head"),
            P("head", ("ctx", "sub")),
            P("head"),
        ),
        out_specs=P(("groups", "ctx", "sub"), "head"),
        check_vma=False,
    )
```

profile of v0, /device:TPU:16, one launch (start us, length us, event | category | flops | bytes accessed | tf_op | source)
XLA Modules:
  0.0 477.1 jit_solution(2654471461920297784)
XLA Ops:
  6.5 0.0 all-gather.6.cloned.1.call-start
  6.5 6.4 %copy.16 = bf16[1024,2048]{0,1:T(8,128)(2,1)} copy(bf16[1024,2048]{1,0:T(8,128)(2,1)} %param.6) | data formatting | bytes 8388608 | tf_op jit(solution)/shard_map/reshape | solution.py:13
  12.9 5.8 %fusion.6 = f32[16,128,128]{2,1,0:T(8,128)} fusion(bf16[1024,16,128]{0,2,1:T(8,128)(2,1)} %bitcast.51, bf16[1024,2048]{1,0:T(8,128)(2,1)} %param.7), kind=kOutput, calls=%fused_computation.10 | convolution fusion | flops 536870912 | bytes 9437184 | tf_op jit(solution)/shard_map/khd,khe->hde/dot_general | solution.py:15
  18.7 0.0 all-gather.6.cloned.1.call-update
  18.8 0.0 all-gather.4.cloned.1.call-start
  18.8 0.7 all-gather.4.cloned.1.call-update
  19.5 0.0 reduce-scatter.2.cloned.1.call-start
  19.6 0.3 iota_compare_fusion
  19.9 23.5 %fusion = f32[16,1024,128]{1,2,0:T(8,128)} fusion(pred[1024,1024]{1,0:T(8,128)(4,1)S(1)} %iota_compare_fusion, bf16[1024,16,128]{0,2,1:T(8,128)(2,1)} %bitcast.52, bf16[1024,2048]{1,0:T(8,128)(2,1)} %param.7, bf16[1024,2048]{1,0:T(8,128)(2,1)} %param.5), kind=kOutput, calls=%fused_computation.1 | convolution fusion | flops 8623489024 | bytes 22020096 | tf_op jit(solution)/shard_map/hqk,khd->qhd/dot_general | solution.py:26
  43.4 57.2 %all-gather.6.cloned.1.call-done = f32[128,128,128]{2,1,0:T(8,128)} async-done(((f32[16,128,128]{2,1,0:T(8,128)}), f32[128,128,128]{2,1,0:T(8,128)}) %all-gather.6.cloned.1.call-update) | async-done | bytes 8388624 | tf_op jit(solution)/shard_map/all_gather | solution.py:17
  100.6 0.0 copy-start
  100.6 4.8 select_reduce_fusion
  105.3 1.0 copy-done
  106.4 0.0 copy-start.1
  106.4 6.5 %multiply_reduce_fusion = (f32[1024,16]{0,1:T(8,128)S(1)}, f32[16,128,1024]{2,1,0:T(8,128)S(1)}) fusion(f32[16,1024,128]{1,2,0:T(8,128)S(1)} %copy-done, f32[16,128,128]{2,1,0:T(8,128)S(1)} %select_reduce_fusion, bf16[1024,2048]{1,0:T(8,128)(2,1)} %param.5), kind=kOutput, calls=%fused_computation.7 | convolution fusion | flops 3227500544 | bytes 22085632 | tf_op jit(solution)/shard_map/qhd,hde->qhe/dot_general | solution.py:27
  112.9 0.0 copy-done.1
  112.9 2.9 multiply_convert_fusion
  115.8 135.8 %all-gather.4.cloned.1.call-done = bf16[2048,4096]{1,0:T(8,128)(2,1)} async-done(((bf16[2048,512]{1,0:T(8,128)(2,1)}), bf16[2048,4096]{1,0:T(8,128)(2,1)}) %all-gather.4.cloned.1.call-update) | async-done | bytes 16777232 | tf_op jit(solution)/shard_map/all_gather | solution.py:37
  251.6 23.7 %fusion.18 = f32[1024,4096]{1,0:T(8,128)} fusion(bf16[1024,2048]{0,1:T(8,128)(2,1)} %bitcast.50, bf16[2048,4096]{1,0:T(8,128)(2,1)} %all-gather.4.cloned.1.call-done), kind=kOutput, calls=%fused_computation.23 | convolution fusion | flops 17179869184 | bytes 37748736 | tf_op jit(solution)/shard_map/dot_general | solution.py:35
  275.3 0.0 reduce-scatter.2.cloned.1.call-update
  275.3 189.2 %reduce-scatter.2.cloned.1.call-done = f32[1024,2048]{1,0:T(8,128)} async-done(((f32[1024,4096]{1,0:T(8,128)}), f32[1024,2048]{1,0:T(8,128)}) %reduce-scatter.2.cloned.1.call-update) | async-done | bytes 8388624 | tf_op jit(solution)/shard_map/reduce_scatter | solution.py:40
  464.5 6.0 %convert_element_type.12 = bf16[1024,2048]{1,0:T(8,128)(2,1)} convert(f32[1024,2048]{1,0:T(8,128)} %reduce-scatter.2.cloned.1.call-done) | non-fusion elementwise | flops 2097152 | bytes 12582912 | tf_op jit(solution)/shard_map/convert_element_type | solution.py:40
  (2 shorter events, 0.0 us)
Async XLA Ops:
  6.5 94.0 %all-gather.6.cloned.1.call-start = ((), (), s32[]{:S(2)}) async-start(), calls=%async_computation.3 | async-start | bytes 9437184 | tf_op jit(solution)/shard_map/all_gather | solution.py:17
  18.8 232.8 %all-gather.4.cloned.1.call-start = ((), (), s32[]{:S(2)}) async-start(), calls=%async_computation.1 | async-start | bytes 18874368 | tf_op jit(solution)/shard_map/all_gather | solution.py:37
  19.5 445.0 %reduce-scatter.2.cloned.1.call-start = ((), (), s32[]{:S(2)}) async-start(), calls=%async_computation.2 | async-start | bytes 25165824 | tf_op jit(solution)/shard_map/reduce_scatter | solution.py:40
  100.6 5.8 %copy-start = (f32[16,1024,128]{1,2,0:T(8,128)S(1)}, f32[16,1024,128]{1,2,0:T(8,128)}, u32[]{:S(2)}) copy-start(f32[16,1024,128]{1,2,0:T(8,128)} %fusion) | copy-start | bytes 25165828
  106.4 6.5 %copy-start.1 = (f32[2048]{0:T(1024)S(1)}, f32[2048]{0:T(1024)}, u32[]{:S(2)}) copy-start(f32[2048]{0:T(1024)} %param.9) | copy-start | bytes 24580
Sparse Core Ops, SparseCore 0:
  18.9 81.6 all-gather.5
  102.2 149.3 all-gather.3
  275.4 189.0 reduce-scatter.1
where the time goes:
time: 479 us; the launch traced here: 477 us
  waiting for transfers between devices  383 us (80%)
  matrix products  59.5 us (12%)
  other arithmetic  14.1 us (3%)
  between operations  13.2 us (3%)
  local copies, waits for them, and re-layouts  7.4 us (2%)
    reduce_scatter x1, waiting for transfers between devices, local(): lax.psum_scatter(partial_out, 'head', scatter_dimension=1, tiled=True)  189 us
    all_gather x1, waiting for transfers between devices, local(): lax.all_gather(out_weight, ('ctx', 'sub'), axis=1, tiled=True)  136 us
    all_gather x1, waiting for transfers between devices, local(): lax.all_gather(local_state[None], ('ctx', 'sub'), axis=0, tiled=True)  57.2 us
    dot_general x1, matrix products, local(): jnp.dot(normed, lax.all_gather(out_weight, ('ctx', 'sub'), axis=1, tiled=...  23.7 us
    dot_general x1, matrix products, local(): jnp.einsum('hqk,khd->qhd', weights, value_blk, preferred_element_type=jnp...  23.5 us
  transfers between devices with their start and end apart: 3, of which 3 were waited for; matrix products, arithmetic and copies ran while one was open for 8% of the time, Pallas kernels for 0%

commit v1 on v0

v1 whole, which is shorter than its diff:
```python
import functools

import jax
import jax.numpy as jnp
from jax import lax
from jax.experimental import pallas as pl
from jax.experimental.pallas import tpu as pltpu
from jax.sharding import PartitionSpec as P

DH = 128
LANES = 128
EPS = 1e-06
F32 = jnp.float32
BF16 = jnp.bfloat16
MIB = 1 << 20


def params(mib=32):
    return pltpu.CompilerParams(vmem_limit_bytes=mib * MIB)


def dot(a, b):
    return lax.dot_general(a, b, (((1,), (0,)), ((), ())), preferred_element_type=F32)


def dot_nt(a, b):
    return lax.dot_general(a, b, (((1,), (1,)), ((), ())), preferred_element_type=F32)


def dot_tn(a, b):
    return lax.dot_general(a, b, (((0,), (0,)), ((), ())), preferred_element_type=F32)


def state_kernel(per, k_ref, v_ref, out_ref):
    for i in range(per):
        cols = slice(i * DH, (i + 1) * DH)
        out_ref[i] = dot_tn(k_ref[:, cols], v_ref[:, cols]).astype(BF16)


def block_states(keys, values, heads):
    rows = keys.shape[0]
    per = 4 if heads % 4 == 0 else 1
    spec = pl.BlockSpec((rows, per * DH), lambda i: (0, i))
    return pl.pallas_call(
        functools.partial(state_kernel, per),
        grid=(heads // per,),
        in_specs=[spec, spec],
        out_specs=pl.BlockSpec((per, DH, DH), lambda i: (i, 0, 0)),
        out_shape=jax.ShapeDtypeStruct((heads, DH, DH), BF16),
        compiler_params=params(),
        cost_estimate=pl.CostEstimate(
            flops=8 * rows * heads * DH * DH, bytes_accessed=4 * keys.size, transcendentals=0
        ),
        name="block_states",
    )(keys, values)


def intra_kernel(per, chunk, q_ref, k_ref, v_ref, out_ref):
    rows = q_ref.shape[0]
    row_ids = lax.broadcasted_iota(jnp.int32, (chunk, chunk), 0)
    col_ids = lax.broadcasted_iota(jnp.int32, (chunk, chunk), 1)
    causal = col_ids <= row_ids
    for i in range(per):
        cols = slice(i * DH, (i + 1) * DH)
        state = None
        for at in range(0, rows, chunk):
            part = slice(at, at + chunk)
            q, k, v = q_ref[part, cols], k_ref[part, cols], v_ref[part, cols]
            scores = jnp.where(causal, dot_nt(q, k), 0.0).astype(BF16)
            mixed = dot(scores, v)
            if state is not None:
                mixed = mixed + dot(q, state.astype(BF16))
            out_ref[part, cols] = mixed
            if at + chunk < rows:
                step = dot_tn(k, v)
                state = step if state is None else state + step


def intra_block(queries, keys, values, heads):
    rows = queries.shape[0]
    per = 2 if heads % 2 == 0 else 1
    chunk = 256 if rows % 256 == 0 else rows
    spec = pl.BlockSpec((rows, per * DH), lambda i: (0, i))
    return pl.pallas_call(
        functools.partial(intra_kernel, per, chunk),
        grid=(heads // per,),
        in_specs=[spec, spec, spec],
        out_specs=spec,
        out_shape=jax.ShapeDtypeStruct(queries.shape, F32),
        compiler_params=params(),
        cost_estimate=pl.CostEstimate(
            flops=16 * rows * heads * DH * DH, bytes_accessed=10 * queries.size, transcendentals=0
        ),
        name="intra_block",
    )(queries, keys, values)


def norm_kernel(n_sib, table, q_ref, a_ref, p_ref, g_ref, *refs):
    sib_refs, out_ref = refs[:n_sib], refs[-1]
    state = p_ref[0].astype(F32)
    for o in range(n_sib):
        state = state + jnp.where(table[2 + o] > 0, sib_refs[o][0].astype(F32), 0.0)
    mixed = a_ref[...] + dot(q_ref[...], state.astype(BF16))
    mean_sq = jnp.mean(mixed * mixed, axis=-1, keepdims=True)
    out_ref[...] = (mixed * lax.rsqrt(mean_sq + EPS) * g_ref[0]).astype(BF16)


def norm_part(table, queries, intra, prefix, gain, sibs, normed):
    rows, width = queries.shape
    part = prefix.shape[0]
    cols = pl.BlockSpec((rows, DH), lambda i, t: (0, t[0] * part + i))
    mat = pl.BlockSpec((1, DH, DH), lambda i, t: (t[0] * part + i, 0, 0))
    in_specs = [
        cols,
        cols,
        pl.BlockSpec((1, DH, DH), lambda i, t: (i, 0, 0)),
        pl.BlockSpec((1, 1, DH), lambda i, t: (t[0] * part + i, 0, 0)),
    ] + [mat] * len(sibs)
    operands = [queries, intra, prefix, gain, *sibs]
    aliases = {}
    if normed is not None:
        in_specs.append(pl.BlockSpec(memory_space=pl.ANY))
        operands.append(normed)
        aliases = {len(operands): 0}
    return pl.pallas_call(
        functools.partial(norm_kernel, len(sibs)),
        grid_spec=pltpu.PrefetchScalarGridSpec(
            num_scalar_prefetch=1, grid=(part,), in_specs=in_specs, out_specs=cols
        ),
        out_shape=jax.ShapeDtypeStruct((rows, width), BF16),
        input_output_aliases=aliases,
        compiler_params=params(),
        cost_estimate=pl.CostEstimate(
            flops=4 * rows * part * DH * DH, bytes_accessed=8 * rows * part * DH, transcendentals=0
        ),
        name="norm_part",
    )(table, *operands)


def project_kernel(n_head, n_sub, table, x_ref, *refs):
    w_refs, outs = refs[: n_head * n_sub], refs[n_head * n_sub :]
    own = table[0]
    for kh in range(n_head):
        for j in range(n_sub):
            res = dot(x_ref[...], w_refs[kh * n_sub + j][...])
            at = slice(j * LANES, (j + 1) * LANES)
            for o in range(n_head):

                @pl.when(jnp.bitwise_xor(own, kh) == o)
                def _(res=res, at=at, o=o):
                    outs[o][:, at] = res.astype(outs[o].dtype)


def project(table, normed, pieces, n_head, n_sub):
    rows, depth = normed.shape
    tile = 256 if rows % 256 == 0 else rows
    width = n_sub * LANES
    out_spec = pl.BlockSpec((tile, width), lambda i, t: (i, 0))
    return pl.pallas_call(
        functools.partial(project_kernel, n_head, n_sub),
        grid_spec=pltpu.PrefetchScalarGridSpec(
            num_scalar_prefetch=1,
            grid=(rows // tile,),
            in_specs=[pl.BlockSpec((tile, depth), lambda i, t: (i, 0))]
            + [pl.BlockSpec((depth, LANES), lambda i, t: (0, 0))] * len(pieces),
            out_specs=[out_spec] * n_head,
        ),
        out_shape=[jax.ShapeDtypeStruct((rows, width), F32)]
        + [jax.ShapeDtypeStruct((rows, width), BF16)] * (n_head - 1),
        compiler_params=params(),
        cost_estimate=pl.CostEstimate(
            flops=2 * rows * depth * width * n_head,
            bytes_accessed=2 * rows * depth + 2 * depth * width * n_head + 6 * rows * width,
            transcendentals=0,
        ),
        name="project",
    )(table, normed, *pieces)


def combine_kernel(n_recv, table, keep_ref, *refs):
    total = keep_ref[...]
    for r in refs[:n_recv]:
        total = total + r[...].astype(F32)
    refs[-1][...] = total.astype(BF16)


def combine(table, keep, recvs, out, shape):
    rows = shape[0]
    n_sub = keep.shape[1] // LANES
    block = pl.BlockSpec((rows, LANES), lambda i, t: (0, i))
    in_specs = [block] * (1 + len(recvs))
    operands = [keep, *recvs]
    aliases = {}
    if out is not None:
        in_specs.append(pl.BlockSpec(memory_space=pl.ANY))
        operands.append(out)
        aliases = {len(operands): 0}
    return pl.pallas_call(
        functools.partial(combine_kernel, len(recvs)),
        grid_spec=pltpu.PrefetchScalarGridSpec(
            num_scalar_prefetch=1,
            grid=(n_sub,),
            in_specs=in_specs,
            out_specs=pl.BlockSpec((rows, LANES), lambda i, t: (0, t[i])),
        ),
        out_shape=jax.ShapeDtypeStruct(shape, BF16),
        input_output_aliases=aliases,
        compiler_params=params(),
        cost_estimate=pl.CostEstimate(
            flops=2 * keep.size, bytes_accessed=8 * keep.size, transcendentals=0
        ),
        name="combine",
    )(table, *operands)


def shift(x, axis, size, o):
    return lax.ppermute(x, axis, [(i, (i + o) % size) for i in range(size)])


def swap(x, axis, size, k):
    return lax.ppermute(x, axis, [(i, i ^ k) for i in range(size)])


def table(*entries):
    return jnp.stack([jnp.asarray(e, jnp.int32) for e in entries])


def local(sizes, queries, keys, values, out_weight, norm_gain):
    n_group, n_ctx, n_head, n_sub = (sizes[a] for a in ("groups", "ctx", "head", "sub"))
    g, c, h, s = (lax.axis_index(a) for a in ("groups", "ctx", "head", "sub"))
    rows, width = queries.shape
    heads = width // DH
    depth, cols = out_weight.shape
    near = n_ctx // n_head
    split = n_group if cols % (n_group * LANES) == 0 else 1
    rounds = cols // (split * LANES)
    low, own = c % near, (c // near) ^ h

    def mine(o, r):
        return ((g - o) % split) * rounds + r

    def cut(o, r):
        return lax.dynamic_slice(out_weight, (0, mine(o, r) * LANES), (depth, LANES))

    first = {(o, r): cut(o, r) for o in range(split) for r in range(rounds)}
    pieces = {}

    def fetch(r, k):
        for o in range(split):
            if k == 0:
                piece = first[o, r]
            elif o == 0:
                piece = swap(first[0, r], "ctx", n_ctx, k)
            else:
                piece = shift(pieces[r, k, 0][0], "groups", n_group, o)
            pieces[r, k, o] = [piece] + [shift(piece, "sub", n_sub, j) for j in range(1, n_sub)]

    part = heads // n_sub
    states = block_states(keys, values, heads)
    sibs = [shift(states, "sub", n_sub, o) for o in range(1, n_sub)]
    total = sum(
        lax.dynamic_slice_in_dim(x, s * part, part).astype(F32) for x in [states, *sibs]
    )
    prefix = jnp.zeros((part, DH, DH), BF16)
    for i in range(n_ctx - 1):
        prefix = prefix + lax.ppermute(
            (prefix.astype(F32) + total).astype(BF16), "ctx", [(i, i + 1)]
        )
    intra = intra_block(queries, keys, values, heads)
    gain = norm_gain.reshape(heads, 1, DH)
    normed = None
    for o in range(n_sub):
        mat = prefix if o == 0 else shift(prefix, "sub", n_sub, o)
        at = table((s - o) % n_sub, 0, *[s >= j for j in range(1, n_sub)])
        normed = norm_part(at, queries, intra, mat, gain, sibs, normed)

    for r in range(rounds):
        for kl in range(near):
            for kh in range(n_head):
                fetch(r, kh * near + kl)
    out = None
    for r in range(rounds):
        for kl in range(near):
            for o in range(split):
                use = [p for kh in range(n_head) for p in pieces[r, kh * near + kl, o]]
                keep, *sends = project(table(own), normed, use, n_head, n_sub)
                recvs = [swap(x, "head", n_head, i + 1) for i, x in enumerate(sends)]
                places = [
                    (((low ^ kl) * n_sub + (s - j) % n_sub) * split * rounds + mine(o, r))
                    for j in range(n_sub)
                ]
                out = combine(table(*places), keep, recvs, out, (rows, n_sub * near * cols))
    return out


def solution(mesh):
    return jax.shard_map(
        functools.partial(local, dict(mesh.shape)),
        mesh=mesh,
        in_specs=(
            P(("groups", "ctx", "sub"), "head"),
            P(("groups", "ctx", "sub"), "head"),
            P(("groups", "ctx", "sub"), "head"),
            P("head", ("ctx", "sub")),
            P("head"),
        ),
        out_specs=P(("groups", "ctx", "sub"), "head"),
        check_vma=False,
    )
```

time: 479 us -> 295 us (0.62)
  waiting for transfers between devices: 383 us -> 132 us
  Pallas kernels: 0 us -> 100 us
  matrix products: 59.5 us -> 0 us
  starting transfers between devices: 0.08 us -> 33.6 us
  local copies, waits for them, and re-layouts: 7.4 us -> 26.3 us
  between operations: 13.2 us -> 0.52 us
  other arithmetic: 14.1 us -> 2.04 us
    all_gather x2 -> x0, waiting for transfers between devices: 193 us -> none  [the longest x1 136 us: local(): lax.all_gather(out_weight, ('ctx', 'sub'), axis=1, tiled=True)]
    reduce_scatter x1 -> x0, waiting for transfers between devices: 189 us -> none  [local(): lax.psum_scatter(partial_out, 'head', scatter_dimension=1, tiled=True)]
    ppermute x0 -> x41, waiting for transfers between devices: none -> 132 us  [the longest x14 113 us: swap(): return lax.ppermute(x, axis, [(i, i ^ k) for i in range(size)])]
    pallas_call x0 -> x20, Pallas kernels: none -> 100 us  [the longest x8 62.7 us: project(): pl.pallas_call(functools.partial(project_kernel, n_head, n_sub), grid_spe...]
    dot_general x4 -> x0, matrix products: 59.5 us -> none  [the longest x1 23.7 us: local(): jnp.dot(normed, lax.all_gather(out_weight, ('ctx', 'sub'), axis=1, tiled=...]
    ppermute x0 -> x41, starting transfers between devices: none -> 33.6 us  [the longest x14 19.1 us: swap(): return lax.ppermute(x, axis, [(i, i ^ k) for i in range(size)])]
    unnamed x4 -> x52, local copies, waits for them, and re-layouts: 1.01 us -> 24.6 us
    convert_element_type x2 -> x3, other arithmetic: 8.96 us -> 0.34 us  [local(): (prefix.astype(F32) + total).astype(BF16)]
  transfers between devices with their start and end apart: 3 -> 41, of which waited for: 3 -> 12; matrix products, arithmetic and copies ran while one was open for 8% -> 1% of each run, Pallas kernels for 0% -> 33%
where the time goes in v1:
time: 295 us
  waiting for transfers between devices  132 us (45%)
  Pallas kernels  100 us (34%)
  starting transfers between devices  33.6 us (11%)
  local copies, waits for them, and re-layouts  26.3 us (9%)
    ppermute x14, waiting for transfers between devices, swap(): return lax.ppermute(x, axis, [(i, i ^ k) for i in range(size)])  113 us
    pallas_call x8, Pallas kernels, project(): pl.pallas_call(functools.partial(project_kernel, n_head, n_sub), grid_spe...  62.7 us
    unnamed x52, local copies, waits for them, and re-layouts  24.6 us
    ppermute x14, starting transfers between devices, swap(): return lax.ppermute(x, axis, [(i, i ^ k) for i in range(size)])  19.1 us
    ppermute x3, waiting for transfers between devices, local(): lax.ppermute((prefix.astype(F32) + total).astype(BF16), 'ctx', [(i, i + 1)])  17.3 us
    pallas_call x8, Pallas kernels, combine(): pl.pallas_call(functools.partial(combine_kernel, len(recvs)), grid_spec=p...  12.6 us
    pallas_call x1, Pallas kernels, intra_block(): pl.pallas_call(functools.partial(intra_kernel, per, chunk), grid=(heads /...  11.6 us
    ppermute x24, starting transfers between devices, shift(): return lax.ppermute(x, axis, [(i, (i + o) % size) for i in range(size)])  11.1 us
  transfers between devices with their start and end apart: 41, of which 12 were waited for; matrix products, arithmetic and copies ran while one was open for 1% of the time, Pallas kernels for 33%

profile of v1, /device:TPU:16, one launch (start us, length us, event | category | flops | bytes accessed | tf_op | source)
XLA Modules:
  0.0 294.7 jit_solution(3560456304155948146)
XLA Ops:
  0.0 2.2 copy-done.4
  2.2 2.2 copy-done.6
  4.4 2.6 block_states.1
  7.1 1.7 constant_dynamic-slice_fusion
  9.1 0.7 collective-permute-start.1
  10.3 1.9 collective-permute-start.23
  12.2 20.1 %collective-permute-done.34.refs_2_ = bf16[2048,128]{1,0:T(8,128)(2,1)} collective-permute-done((bf16[2048,128]{1,0:T(8,128)(2,1)S(1)}, bf16[2048,128]{1,0:T(8,128)(2,1)}, u32[]{:S(2)}, u32[]{:S(2)}) %collective-permute-start.34) | collective-permute-done | bytes 524320 | tf_op jit(solution)/shard_map/ppermute | solution.py:221
  32.3 2.7 collective-permute-start.26
  35.0 4.4 %collective-permute-start.16 = (bf16[2048,128]{1,0:T(8,128)(2,1)S(1)}, bf16[2048,128]{1,0:T(8,128)(2,1)S(1)}, u32[]{:S(2)}, u32[]{:S(2)}) collective-permute-start(bf16[2048,128]{1,0:T(8,128)(2,1)S(1)} %get-tuple-element.41.refs_0_), channel_id=1, source_target_pairs={{0,8},{4,12},{8,0},{12,4},{1,9},{5,13},{9,1},{13,5},{2,10},{6,14},... | collective-permute-start | bytes 1572872 | tf_op jit(solution)/shard_map/ppermute | solution.py:221
  39.5 0.8 copy-done.21
  40.3 1.3 collective-permute-start.2
  41.6 0.8 copy-done.19
  43.0 27.3 %collective-permute-done.26.refs_2_ = bf16[2048,128]{1,0:T(8,128)(2,1)} collective-permute-done((bf16[2048,128]{1,0:T(8,128)(2,1)S(1)}, bf16[2048,128]{1,0:T(8,128)(2,1)}, u32[]{:S(2)}, u32[]{:S(2)}) %collective-permute-start.26) | collective-permute-done | bytes 524320 | tf_op jit(solution)/shard_map/ppermute | solution.py:221
  70.2 9.9 %collective-permute-done.16.refs_2_ = bf16[2048,128]{1,0:T(8,128)(2,1)S(1)} collective-permute-done((bf16[2048,128]{1,0:T(8,128)(2,1)S(1)}, bf16[2048,128]{1,0:T(8,128)(2,1)S(1)}, u32[]{:S(2)}, u32[]{:S(2)}) %collective-permute-start.16) | collective-permute-done | bytes 524320 | tf_op jit(solution)/shard_map/ppermute | solution.py:221
  80.1 0.9 collective-permute-start.8
  81.0 17.3 %collective-permute-done.2 = bf16[8,128,128]{2,1,0:T(8,128)(2,1)S(1)} collective-permute-done((bf16[8,128,128]{2,1,0:T(8,128)(2,1)S(1)}, bf16[8,128,128]{2,1,0:T(8,128)(2,1)S(1)}, u32[]{:S(2)}, u32[]{:S(2)}) %collective-permute-start.2) | collective-permute-done | bytes 262176 | tf_op jit(solution)/shard_map/ppermute | solution.py:266
  98.5 0.8 copy-done.17
  99.3 1.5 collective-permute-start.3
  100.8 0.8 copy-done.9
  101.6 1.5 collective-permute-start.35
  103.3 5.6 %collective-permute-done.8.refs_2_ = bf16[2048,128]{1,0:T(8,128)(2,1)S(1)} collective-permute-done((bf16[2048,128]{1,0:T(8,128)(2,1)S(1)}, bf16[2048,128]{1,0:T(8,128)(2,1)S(1)}, u32[]{:S(2)}, u32[]{:S(2)}) %collective-permute-start.8) | collective-permute-done | bytes 524320 | tf_op jit(solution)/shard_map/ppermute | solution.py:221
  108.9 1.5 collective-permute-start.24
  110.5 0.8 copy-done.23
  111.3 0.7 copy-done.25
  112.5 2.2 copy-done.2
  114.7 2.2 copy-done.5
  116.9 2.2 copy-done.7
  119.1 11.6 %intra_block.1.a_ref = f32[1024,2048]{1,0:T(8,128)S(1)} custom-call(bf16[1024,2048]{1,0:T(8,128)(2,1)S(1)} %copy-done.2, bf16[1024,2048]{1,0:T(8,128)(2,1)S(1)} %copy-done.5, bf16[1024,2048]{1,0:T(8,128)(2,1)S(1)} %copy-done.7), custom_call_target="tpu_custom_call" | custom-call | flops 4294967296 | bytes 20971520 | tf_op jit(solution)/shard_map/intra_block/pallas_call | solution.py:84
  130.7 3.3 %copy-done = f32[1024,2048]{1,0:T(8,128)} copy-done((f32[1024,2048]{1,0:T(8,128)}, f32[1024,2048]{1,0:T(8,128)S(1)}, u32[]{:S(2)}) %copy-start) | copy-done | bytes 8388632
  134.0 1.0 add.185.p_ref
  136.1 1.5 collective-permute-start.17
  137.6 1.1 collective-permute-done.27.refs_2_
  139.3 3.4 %copy-done.1 = f32[1024,2048]{1,0:T(8,128)S(1)} copy-done((f32[1024,2048]{1,0:T(8,128)S(1)}, f32[1024,2048]{1,0:T(8,128)}, u32[]{:S(2)}) %copy-start.1) | copy-done | bytes 8388632
  142.7 2.2 copy-done.3
  144.8 5.4 %norm_part.2.refs_1_ = bf16[1024,2048]{1,0:T(8,128)(2,1)S(1)} custom-call(s32[3]{0:T(128)S(1)} %fusion.2.table, bf16[1024,2048]{1,0:T(8,128)(2,1)S(1)} %copy-done.3, f32[1024,2048]{1,0:T(8,128)S(1)} %copy-done.1, bf16[8,128,128]{2,1,0:T(8,128)(2,1)S(1)} %add.185.p_ref, f32[16,1,128]{2,1,0:T(1,128)S(1)} %bitcast.21, ...), custom_call_target="tpu_custom_call" | custom-call | flops 536870912 | bytes 8388608 | tf_op jit(solution)/shard_map/norm_part/pallas_call | solution.py:125
  150.2 5.4 %norm_part.3.x_ref = bf16[1024,2048]{1,0:T(8,128)(2,1)S(1)} custom-call(s32[3]{0:T(128)S(1)} %fusion.1.table, bf16[1024,2048]{1,0:T(8,128)(2,1)S(1)} %copy-done.3, f32[1024,2048]{1,0:T(8,128)S(1)} %copy-done.1, bf16[8,128,128]{2,1,0:T(8,128)(2,1)S(1)} %collective-permute-done.4.p_ref, f32[16,1,128]{2,1,0:T(1,128)S(1)} %bitcast.22, ...), custom_call_target="tpu_custom_call", output_to_operand_aliasing={{}: (6, {})} | custom-call | flops 536870912 | bytes 8388608 | tf_op jit(solution)/shard_map/norm_part/pallas_call | solution.py:125
  155.6 8.1 %project.15 = (f32[1024,256]{1,0:T(8,128)S(1)}, bf16[1024,256]{1,0:T(8,128)(2,1)S(1)}) custom-call(s32[1]{0:T(128)} %bitcast.2.table, bf16[1024,2048]{1,0:T(8,128)(2,1)S(1)} %norm_part.3.x_ref, bf16[2048,128]{1,0:T(8,128)(2,1)S(1)} %get-tuple-element.42.refs_0_, bf16[2048,128]{1,0:T(8,128)(2,1)S(1)} %copy-done.22, ...), custom_call_target="tpu_custom_call" | custom-call | flops 2147483648 | bytes 7864320 | tf_op jit(solution)/shard_map/project/pallas_call | solution.py:159
  163.7 1.6 collective-permute-start.9
  165.8 8.1 %project.14 = (f32[1024,256]{1,0:T(8,128)S(1)}, bf16[1024,256]{1,0:T(8,128)(2,1)S(1)}) custom-call(s32[1]{0:T(128)} %bitcast.2.table, bf16[1024,2048]{1,0:T(8,128)(2,1)S(1)} %norm_part.3.x_ref, bf16[2048,128]{1,0:T(8,128)(2,1)S(1)} %get-tuple-element.39.refs_0_, bf16[2048,128]{1,0:T(8,128)(2,1)S(1)} %copy-done.20, ...), custom_call_target="tpu_custom_call" | custom-call | flops 2147483648 | bytes 7864320 | tf_op jit(solution)/shard_map/project/pallas_call | solution.py:159
  174.6 8.4 %project.13 = (f32[1024,256]{1,0:T(8,128)S(1)}, bf16[1024,256]{1,0:T(8,128)(2,1)S(1)}) custom-call(s32[1]{0:T(128)} %bitcast.2.table, bf16[1024,2048]{1,0:T(8,128)(2,1)S(1)} %norm_part.3.x_ref, bf16[2048,128]{1,0:T(8,128)(2,1)} %collective-permute-done.23.refs_0_, bf16[2048,128]{1,0:T(8,128)(2,1)} %collective-permute-done.30.refs_1_, ...), custom_call_target="tpu_custom_call" | custom-call | flops 2147483648 | bytes 7864320 | tf_op jit(solution)/shard_map/project/pallas_call | solution.py:159
  183.1 8.5 %project.12 = (f32[1024,256]{1,0:T(8,128)S(1)}, bf16[1024,256]{1,0:T(8,128)(2,1)S(1)}) custom-call(s32[1]{0:T(128)} %bitcast.2.table, bf16[1024,2048]{1,0:T(8,128)(2,1)S(1)} %norm_part.3.x_ref, bf16[2048,128]{1,0:T(8,128)(2,1)} %collective-permute-done.24.refs_0_, bf16[2048,128]{1,0:T(8,128)(2,1)} %collective-permute-done.25.refs_1_, ...), custom_call_target="tpu_custom_call" | custom-call | flops 2147483648 | bytes 7864320 | tf_op jit(solution)/shard_map/project/pallas_call | solution.py:159
  192.2 7.9 %project.11 = (f32[1024,256]{1,0:T(8,128)S(1)}, bf16[1024,256]{1,0:T(8,128)(2,1)S(1)}) custom-call(s32[1]{0:T(128)} %bitcast.2.table, bf16[1024,2048]{1,0:T(8,128)(2,1)S(1)} %norm_part.3.x_ref, bf16[2048,128]{1,0:T(8,128)(2,1)S(1)} %get-tuple-element.41.refs_0_, bf16[2048,128]{1,0:T(8,128)(2,1)S(1)} %copy-done.18, bf16[2048,128]{1,0:T(8,128)(2,1)S(1)} %copy-done.14, ...), custom_call_target="tpu_custom_call" | custom-call | flops 2147483648 | bytes 7864320 | tf_op jit(solution)/shard_map/project/pallas_call | solution.py:159
  200.1 1.5 collective-permute-start.40
  202.2 1.4 collective-permute-start.32
  203.7 7.9 %project.10 = (f32[1024,256]{1,0:T(8,128)S(1)}, bf16[1024,256]{1,0:T(8,128)(2,1)S(1)}) custom-call(s32[1]{0:T(128)} %bitcast.2.table, bf16[1024,2048]{1,0:T(8,128)(2,1)S(1)} %norm_part.3.x_ref, bf16[2048,128]{1,0:T(8,128)(2,1)S(1)} %get-tuple-element.40.refs_0_, bf16[2048,128]{1,0:T(8,128)(2,1)S(1)} %copy-done.10, ...), custom_call_target="tpu_custom_call" | custom-call | flops 2147483648 | bytes 7864320 | tf_op jit(solution)/shard_map/project/pallas_call | solution.py:159
  211.6 6.9 %project.9 = (f32[1024,256]{1,0:T(8,128)S(1)}, bf16[1024,256]{1,0:T(8,128)(2,1)S(1)}) custom-call(s32[1]{0:T(128)} %bitcast.2.table, bf16[1024,2048]{1,0:T(8,128)(2,1)S(1)} %norm_part.3.x_ref, bf16[2048,128]{1,0:T(8,128)(2,1)S(1)} %copy-done.12, bf16[2048,128]{1,0:T(8,128)(2,1)S(1)} %collective-permute-done.12.refs_1_, bf16[2048,128]{1,0:T(8,128)(2,1)S(1)} %copy-done.16, ...), custom_call_target="tpu_custom_call" | custom-call | flops 2147483648 | bytes 7864320 | tf_op jit(solution)/shard_map/project/pallas_call | solution.py:159
  219.2 1.5 collective-permute-start.22
  220.6 6.9 %project.8 = (f32[1024,256]{1,0:T(8,128)S(1)}, bf16[1024,256]{1,0:T(8,128)(2,1)S(1)}) custom-call(s32[1]{0:T(128)} %bitcast.2.table, bf16[1024,2048]{1,0:T(8,128)(2,1)S(1)} %norm_part.3.x_ref, bf16[2048,128]{1,0:T(8,128)(2,1)S(1)} %collective-permute-done.6.refs_0_, bf16[2048,128]{1,0:T(8,128)(2,1)S(1)} %collective-permute-done.7.refs_1_, ...), custom_call_target="tpu_custom_call" | custom-call | flops 2147483648 | bytes 7864320 | tf_op jit(solution)/shard_map/project/pallas_call | solution.py:159
  228.2 1.5 collective-permute-start.14
  229.6 7.8 %collective-permute-done.32.refs_0_ = bf16[1024,256]{1,0:T(8,128)(2,1)S(1)} collective-permute-done((bf16[1024,256]{1,0:T(8,128)(2,1)S(1)}, bf16[1024,256]{1,0:T(8,128)(2,1)S(1)}, u32[]{:S(2)}, u32[]{:S(2)}) %collective-permute-start.32) | collective-permute-done | bytes 524320 | tf_op jit(solution)/shard_map/ppermute | solution.py:221
  237.4 1.4 collective-permute-start.11
  239.2 1.6 combine.8.refs_1_
  240.8 1.6 combine.9.refs_1_
  242.4 1.6 combine.10.refs_1_
  244.0 4.7 %collective-permute-done.29.refs_0_ = bf16[1024,256]{1,0:T(8,128)(2,1)S(1)} collective-permute-done((bf16[1024,256]{1,0:T(8,128)(2,1)S(1)}, bf16[1024,256]{1,0:T(8,128)(2,1)S(1)}, u32[]{:S(2)}, u32[]{:S(2)}) %collective-permute-start.29) | collective-permute-done | bytes 524320 | tf_op jit(solution)/shard_map/ppermute | solution.py:221
  248.6 1.6 combine.11.refs_1_
  250.2 9.7 %collective-permute-done.22.refs_0_ = bf16[1024,256]{1,0:T(8,128)(2,1)S(1)} collective-permute-done((bf16[1024,256]{1,0:T(8,128)(2,1)S(1)}, bf16[1024,256]{1,0:T(8,128)(2,1)S(1)}, u32[]{:S(2)}, u32[]{:S(2)}) %collective-permute-start.22) | collective-permute-done | bytes 524320 | tf_op jit(solution)/shard_map/ppermute | solution.py:221
  259.9 1.6 combine.12.refs_1_
  261.5 9.7 %collective-permute-done.19.refs_0_ = bf16[1024,256]{1,0:T(8,128)(2,1)S(1)} collective-permute-done((bf16[1024,256]{1,0:T(8,128)(2,1)S(1)}, bf16[1024,256]{1,0:T(8,128)(2,1)S(1)}, u32[]{:S(2)}, u32[]{:S(2)}) %collective-permute-start.19) | collective-permute-done | bytes 524320 | tf_op jit(solution)/shard_map/ppermute | solution.py:221
  271.1 1.6 combine.13.refs_1_
  272.7 9.7 %collective-permute-done.14.refs_0_ = bf16[1024,256]{1,0:T(8,128)(2,1)S(1)} collective-permute-done((bf16[1024,256]{1,0:T(8,128)(2,1)S(1)}, bf16[1024,256]{1,0:T(8,128)(2,1)S(1)}, u32[]{:S(2)}, u32[]{:S(2)}) %collective-permute-start.14) | collective-permute-done | bytes 524320 | tf_op jit(solution)/shard_map/ppermute | solution.py:221
  282.4 1.6 combine.14.refs_1_
  283.9 9.2 %collective-permute-done.11.refs_0_ = bf16[1024,256]{1,0:T(8,128)(2,1)S(1)} collective-permute-done((bf16[1024,256]{1,0:T(8,128)(2,1)S(1)}, bf16[1024,256]{1,0:T(8,128)(2,1)S(1)}, u32[]{:S(2)}, u32[]{:S(2)}) %collective-permute-start.11) | collective-permute-done | bytes 524320 | tf_op jit(solution)/shard_map/ppermute | solution.py:221
  293.1 1.6 combine.15
  (104 shorter events, 8.0 us)
Async XLA Ops:
  0.0 2.2 copy-start.4
  2.2 2.2 copy-start.6
  7.0 2.0 collective-permute-start
  8.9 23.4 %collective-permute-start.34 = (bf16[2048,128]{1,0:T(8,128)(2,1)S(1)}, bf16[2048,128]{1,0:T(8,128)(2,1)}, u32[]{:S(2)}, u32[]{:S(2)}) collective-permute-start(bf16[2048,128]{1,0:T(8,128)(2,1)S(1)} %get-tuple-element.42.refs_0_), channel_id=1, source_target_pairs={{0,8},{4,12},{8,0},{12,4},{1,9},{5,13},{9,1},{13,5},{2,10},{6,14},... | collective-permute-start | bytes 1572872 | tf_op jit(solution)/shard_map/ppermute | solution.py:221
  9.1 25.9 %collective-permute-start.1 = (bf16[8,128,128]{2,1,0:T(8,128)(2,1)S(1)}, bf16[8,128,128]{2,1,0:T(8,128)(2,1)S(1)}, u32[]{:S(2)}, u32[]{:S(2)}) collective-permute-start(bf16[8,128,128]{2,1,0:T(8,128)(2,1)S(1)} %fusion), channel_id=1, source_target_pairs={{0,4},{1,5},{2,6},{3,7},{16,20},{17,21},{18,22},{19,23}} | collective-permute-start | bytes 786440 | tf_op jit(solution)/shard_map/ppermute | solution.py:266
  9.8 29.7 %collective-permute-start.38 = (bf16[2048,128]{1,0:T(8,128)(2,1)S(1)}, bf16[2048,128]{1,0:T(8,128)(2,1)S(1)}, u32[]{:S(2)}, u32[]{:S(2)}) collective-permute-start(bf16[2048,128]{1,0:T(8,128)(2,1)S(1)} %get-tuple-element.42.refs_0_), channel_id=1, source_target_pairs={{0,1},{1,0},{2,3},{3,2},{4,5},{5,4},{6,7},{7,6},{8,9},{9,8},{10,11... | collective-permute-start | bytes 1572872 | tf_op jit(solution)/shard_map/ppermute | solution.py:217
  10.2 31.4 %collective-permute-start.33 = (bf16[2048,128]{1,0:T(8,128)(2,1)S(1)}, bf16[2048,128]{1,0:T(8,128)(2,1)S(1)}, u32[]{:S(2)}, u32[]{:S(2)}) collective-permute-start(bf16[2048,128]{1,0:T(8,128)(2,1)S(1)} %get-tuple-element.39.refs_0_), channel_id=1, source_target_pairs={{0,1},{1,0},{2,3},{3,2},{4,5},{5,4},{6,7},{7,6},{8,9},{9,8},{10,11... | collective-permute-start | bytes 1572872 | tf_op jit(solution)/shard_map/ppermute | solution.py:217
  10.3 32.1 %collective-permute-start.23 = (bf16[2048,128]{1,0:T(8,128)(2,1)S(1)}, bf16[2048,128]{1,0:T(8,128)(2,1)}, u32[]{:S(2)}, u32[]{:S(2)}) collective-permute-start(bf16[2048,128]{1,0:T(8,128)(2,1)S(1)} %get-tuple-element.42.refs_0_), channel_id=1, source_target_pairs={{0,4},{4,0},{8,12},{12,8},{1,5},{5,1},{9,13},{13,9},{2,6},{6,2},{1... | collective-permute-start | bytes 1572872 | tf_op jit(solution)/shard_map/ppermute | solution.py:221
  32.3 38.0 %collective-permute-start.26 = (bf16[2048,128]{1,0:T(8,128)(2,1)S(1)}, bf16[2048,128]{1,0:T(8,128)(2,1)}, u32[]{:S(2)}, u32[]{:S(2)}) collective-permute-start(bf16[2048,128]{1,0:T(8,128)(2,1)S(1)} %get-tuple-element.42.refs_0_), channel_id=1, source_target_pairs={{0,12},{4,8},{8,4},{12,0},{1,13},{5,9},{9,5},{13,1},{2,14},{6,10},... | collective-permute-start | bytes 1572872 | tf_op jit(solution)/shard_map/ppermute | solution.py:221
  35.0 45.1 %collective-permute-start.16 = (bf16[2048,128]{1,0:T(8,128)(2,1)S(1)}, bf16[2048,128]{1,0:T(8,128)(2,1)S(1)}, u32[]{:S(2)}, u32[]{:S(2)}) collective-permute-start(bf16[2048,128]{1,0:T(8,128)(2,1)S(1)} %get-tuple-element.41.refs_0_), channel_id=1, source_target_pairs={{0,8},{4,12},{8,0},{12,4},{1,9},{5,13},{9,1},{13,5},{2,10},{6,14},... | collective-permute-start | bytes 1572872 | tf_op jit(solution)/shard_map/ppermute | solution.py:221
  39.5 0.8 copy-start.21
  40.3 57.9 %collective-permute-start.2 = (bf16[8,128,128]{2,1,0:T(8,128)(2,1)S(1)}, bf16[8,128,128]{2,1,0:T(8,128)(2,1)S(1)}, u32[]{:S(2)}, u32[]{:S(2)}) collective-permute-start(bf16[8,128,128]{2,1,0:T(8,128)(2,1)S(1)} %add_convert_fusion.1), channel_id=1, source_target_pairs={{4,8},{5,9},{6,10},{7,11},{20,24},{21,25},{22,26},{23,27}} | collective-permute-start | bytes 786440 | tf_op jit(solution)/shard_map/ppermute | solution.py:266
  41.6 0.8 copy-start.19
  42.5 56.0 %collective-permute-start.20 = (bf16[2048,128]{1,0:T(8,128)(2,1)S(1)}, bf16[2048,128]{1,0:T(8,128)(2,1)S(1)}, u32[]{:S(2)}, u32[]{:S(2)}) collective-permute-start(bf16[2048,128]{1,0:T(8,128)(2,1)S(1)} %get-tuple-element.41.refs_0_), channel_id=1, source_target_pairs={{0,1},{1,0},{2,3},{3,2},{4,5},{5,4},{6,7},{7,6},{8,9},{9,8},{10,11... | collective-permute-start | bytes 1572872 | tf_op jit(solution)/shard_map/ppermute | solution.py:217
  42.5 58.3 %collective-permute-start.15 = (bf16[2048,128]{1,0:T(8,128)(2,1)S(1)}, bf16[2048,128]{1,0:T(8,128)(2,1)S(1)}, u32[]{:S(2)}, u32[]{:S(2)}) collective-permute-start(bf16[2048,128]{1,0:T(8,128)(2,1)S(1)} %get-tuple-element.40.refs_0_), channel_id=1, source_target_pairs={{0,1},{1,0},{2,3},{3,2},{4,5},{5,4},{6,7},{7,6},{8,9},{9,8},{10,11... | collective-permute-start | bytes 1572872 | tf_op jit(solution)/shard_map/ppermute | solution.py:217
  70.2 32.8 %collective-permute-start.5 = (bf16[2048,128]{1,0:T(8,128)(2,1)S(1)}, bf16[2048,128]{1,0:T(8,128)(2,1)S(1)}, u32[]{:S(2)}, u32[]{:S(2)}) collective-permute-start(bf16[2048,128]{1,0:T(8,128)(2,1)S(1)} %get-tuple-element.41.refs_0_), channel_id=1, source_target_pairs={{0,4},{4,0},{8,12},{12,8},{1,5},{5,1},{9,13},{13,9},{2,6},{6,2},{1... | collective-permute-start | bytes 1572872 | tf_op jit(solution)/shard_map/ppermute | solution.py:221
  80.1 18.2 %copy-start.13 = (bf16[2048,128]{1,0:T(8,128)(2,1)}, bf16[2048,128]{1,0:T(8,128)(2,1)S(1)}, u32[]{:S(2)}) copy-start(bf16[2048,128]{1,0:T(8,128)(2,1)S(1)} %collective-permute-done.16.refs_2_) | copy-start | bytes 1572868
  80.1 28.8 %collective-permute-start.8 = (bf16[2048,128]{1,0:T(8,128)(2,1)S(1)}, bf16[2048,128]{1,0:T(8,128)(2,1)S(1)}, u32[]{:S(2)}, u32[]{:S(2)}) collective-permute-start(bf16[2048,128]{1,0:T(8,128)(2,1)S(1)} %get-tuple-element.41.refs_0_), channel_id=1, source_target_pairs={{0,12},{4,8},{8,4},{12,0},{1,13},{5,9},{9,5},{13,1},{2,14},{6,10},... | collective-permute-start | bytes 1572872 | tf_op jit(solution)/shard_map/ppermute | solution.py:221
  98.3 12.2 %collective-permute-start.39 = (bf16[2048,128]{1,0:T(8,128)(2,1)}, bf16[2048,128]{1,0:T(8,128)(2,1)S(1)}, u32[]{:S(2)}, u32[]{:S(2)}) collective-permute-start(bf16[2048,128]{1,0:T(8,128)(2,1)} %collective-permute-done.34.refs_2_), channel_id=1, source_target_pairs={{0,1},{1,0},{2,3},{3,2},{4,5},{5,4},{6,7},{7,6},{8,9},{9,8},{10,11... | collective-permute-start | bytes 1572872 | tf_op jit(solution)/shard_map/ppermute | solution.py:217
  98.3 41.0 %copy-start.8 = (f32[2048]{0:T(1024)S(1)}, f32[2048]{0:T(1024)}, u32[]{:S(2)}) copy-start(f32[2048]{0:T(1024)} %param.9) | copy-start | bytes 24580
  99.3 12.0 %collective-permute-start.3 = (bf16[8,128,128]{2,1,0:T(8,128)(2,1)S(1)}, bf16[8,128,128]{2,1,0:T(8,128)(2,1)S(1)}, u32[]{:S(2)}, u32[]{:S(2)}) collective-permute-start(bf16[8,128,128]{2,1,0:T(8,128)(2,1)S(1)} %get-tuple-element.37), channel_id=1, source_target_pairs={{8,12},{9,13},{10,14},{11,15},{24,28},{25,29},{26,30},{27,31}} | collective-permute-start | bytes 786440 | tf_op jit(solution)/shard_map/ppermute | solution.py:266
  101.6 33.5 %collective-permute-start.35 = (bf16[2048,128]{1,0:T(8,128)(2,1)}, bf16[2048,128]{1,0:T(8,128)(2,1)}, u32[]{:S(2)}, u32[]{:S(2)}) collective-permute-start(bf16[2048,128]{1,0:T(8,128)(2,1)} %collective-permute-done.34.refs_2_), channel_id=1, source_target_pairs={{0,16},{16,0},{1,17},{17,1},{2,18},{18,2},{3,19},{19,3},{4,20},{20... | collective-permute-start | bytes 1572872 | tf_op jit(solution)/shard_map/ppermute | solution.py:217
  103.1 8.2 %copy-start.11 = (bf16[2048,128]{1,0:T(8,128)(2,1)}, bf16[2048,128]{1,0:T(8,128)(2,1)S(1)}, u32[]{:S(2)}) copy-start(bf16[2048,128]{1,0:T(8,128)(2,1)S(1)} %collective-permute-done.5.refs_0_) | copy-start | bytes 1572868
  103.1 32.4 %collective-permute-start.30 = (bf16[2048,128]{1,0:T(8,128)(2,1)}, bf16[2048,128]{1,0:T(8,128)(2,1)}, u32[]{:S(2)}, u32[]{:S(2)}) collective-permute-start(bf16[2048,128]{1,0:T(8,128)(2,1)} %collective-permute-done.23.refs_0_), channel_id=1, source_target_pairs={{0,1},{1,0},{2,3},{3,2},{4,5},{5,4},{6,7},{7,6},{8,9},{9,8},{10,11... | collective-permute-start | bytes 1572872 | tf_op jit(solution)/shard_map/ppermute | solution.py:217
  108.9 2.4 copy-start.15
  108.9 27.2 %collective-permute-start.24 = (bf16[2048,128]{1,0:T(8,128)(2,1)}, bf16[2048,128]{1,0:T(8,128)(2,1)}, u32[]{:S(2)}, u32[]{:S(2)}) collective-permute-start(bf16[2048,128]{1,0:T(8,128)(2,1)} %collective-permute-done.23.refs_0_), channel_id=1, source_target_pairs={{0,16},{16,0},{1,17},{17,1},{2,18},{18,2},{3,19},{19,3},{4,20},{20... | collective-permute-start | bytes 1572872 | tf_op jit(solution)/shard_map/ppermute | solution.py:217
  110.4 0.8 copy-start.23
  111.3 24.5 %collective-permute-start.31 = (bf16[2048,128]{1,0:T(8,128)(2,1)}, bf16[2048,128]{1,0:T(8,128)(2,1)}, u32[]{:S(2)}, u32[]{:S(2)}) collective-permute-start(bf16[2048,128]{1,0:T(8,128)(2,1)} %collective-permute-done.26.refs_2_), channel_id=1, source_target_pairs={{0,1},{1,0},{2,3},{3,2},{4,5},{5,4},{6,7},{7,6},{8,9},{9,8},{10,11... | collective-permute-start | bytes 1572872 | tf_op jit(solution)/shard_map/ppermute | solution.py:217
  112.0 26.7 %collective-permute-start.27 = (bf16[2048,128]{1,0:T(8,128)(2,1)}, bf16[2048,128]{1,0:T(8,128)(2,1)}, u32[]{:S(2)}, u32[]{:S(2)}) collective-permute-start(bf16[2048,128]{1,0:T(8,128)(2,1)} %collective-permute-done.26.refs_2_), channel_id=1, source_target_pairs={{0,16},{16,0},{1,17},{17,1},{2,18},{18,2},{3,19},{19,3},{4,20},{20... | collective-permute-start | bytes 1572872 | tf_op jit(solution)/shard_map/ppermute | solution.py:217
  112.5 2.2 copy-start.2
  114.7 2.2 copy-start.5
  116.9 2.2 copy-start.7
  130.7 3.3 %copy-start = (f32[1024,2048]{1,0:T(8,128)}, f32[1024,2048]{1,0:T(8,128)S(1)}, u32[]{:S(2)}) copy-start(f32[1024,2048]{1,0:T(8,128)S(1)} %intra_block.1.a_ref) | copy-start | bytes 25165828
  135.0 3.6 %collective-permute-start.4 = (bf16[8,128,128]{2,1,0:T(8,128)(2,1)S(1)}, bf16[8,128,128]{2,1,0:T(8,128)(2,1)S(1)}, u32[]{:S(2)}, u32[]{:S(2)}) collective-permute-start(bf16[8,128,128]{2,1,0:T(8,128)(2,1)S(1)} %add.185.p_ref), channel_id=1, source_target_pairs={{0,1},{1,0},{2,3},{3,2},{4,5},{5,4},{6,7},{7,6},{8,9},{9,8},{10,11... | collective-permute-start | bytes 786440 | tf_op jit(solution)/shard_map/ppermute | solution.py:217
  135.5 28.2 %collective-permute-start.21 = (bf16[2048,128]{1,0:T(8,128)(2,1)}, bf16[2048,128]{1,0:T(8,128)(2,1)}, u32[]{:S(2)}, u32[]{:S(2)}) collective-permute-start(bf16[2048,128]{1,0:T(8,128)(2,1)} %copy-done.13), channel_id=1, source_target_pairs={{0,1},{1,0},{2,3},{3,2},{4,5},{5,4},{6,7},{7,6},{8,9},{9,8},{10,11... | collective-permute-start | bytes 1572872 | tf_op jit(solution)/shard_map/ppermute | solution.py:217
  135.8 29.5 %collective-permute-start.36 = (bf16[2048,128]{1,0:T(8,128)(2,1)}, bf16[2048,128]{1,0:T(8,128)(2,1)}, u32[]{:S(2)}, u32[]{:S(2)}) collective-permute-start(bf16[2048,128]{1,0:T(8,128)(2,1)} %collective-permute-done.35.refs_2_), channel_id=1, source_target_pairs={{0,1},{1,0},{2,3},{3,2},{4,5},{5,4},{6,7},{7,6},{8,9},{9,8},{10,11... | collective-permute-start | bytes 1572872 | tf_op jit(solution)/shard_map/ppermute | solution.py:217
  136.1 37.9 %collective-permute-start.17 = (bf16[2048,128]{1,0:T(8,128)(2,1)}, bf16[2048,128]{1,0:T(8,128)(2,1)}, u32[]{:S(2)}, u32[]{:S(2)}) collective-permute-start(bf16[2048,128]{1,0:T(8,128)(2,1)} %copy-done.13), channel_id=1, source_target_pairs={{0,16},{16,0},{1,17},{17,1},{2,18},{18,2},{3,19},{19,3},{4,20},{20... | collective-permute-start | bytes 1572872 | tf_op jit(solution)/shard_map/ppermute | solution.py:217
  138.7 35.3 %collective-permute-start.25 = (bf16[2048,128]{1,0:T(8,128)(2,1)}, bf16[2048,128]{1,0:T(8,128)(2,1)}, u32[]{:S(2)}, u32[]{:S(2)}) collective-permute-start(bf16[2048,128]{1,0:T(8,128)(2,1)} %collective-permute-done.24.refs_0_), channel_id=1, source_target_pairs={{0,1},{1,0},{2,3},{3,2},{4,5},{5,4},{6,7},{7,6},{8,9},{9,8},{10,11... | collective-permute-start | bytes 1572872 | tf_op jit(solution)/shard_map/ppermute | solution.py:217
  138.7 35.8 %collective-permute-start.28 = (bf16[2048,128]{1,0:T(8,128)(2,1)}, bf16[2048,128]{1,0:T(8,128)(2,1)}, u32[]{:S(2)}, u32[]{:S(2)}) collective-permute-start(bf16[2048,128]{1,0:T(8,128)(2,1)} %collective-permute-done.27.refs_2_), channel_id=1, source_target_pairs={{0,1},{1,0},{2,3},{3,2},{4,5},{5,4},{6,7},{7,6},{8,9},{9,8},{10,11... | collective-permute-start | bytes 1572872 | tf_op jit(solution)/shard_map/ppermute | solution.py:217
  139.3 3.4 %copy-start.1 = (f32[1024,2048]{1,0:T(8,128)S(1)}, f32[1024,2048]{1,0:T(8,128)}, u32[]{:S(2)}) copy-start(f32[1024,2048]{1,0:T(8,128)} %copy-done) | copy-start | bytes 25165828
  142.6 2.2 copy-start.3
  150.2 5.4 %copy-start.22 = (bf16[2048,128]{1,0:T(8,128)(2,1)S(1)}, bf16[2048,128]{1,0:T(8,128)(2,1)}, u32[]{:S(2)}) copy-start(bf16[2048,128]{1,0:T(8,128)(2,1)} %copy-done.21) | copy-start | bytes 1572868
  150.2 5.4 %copy-start.24 = (bf16[2048,128]{1,0:T(8,128)(2,1)S(1)}, bf16[2048,128]{1,0:T(8,128)(2,1)}, u32[]{:S(2)}) copy-start(bf16[2048,128]{1,0:T(8,128)(2,1)} %copy-done.23) | copy-start | bytes 1572868
  155.6 8.1 %copy-start.16 = (bf16[2048,128]{1,0:T(8,128)(2,1)S(1)}, bf16[2048,128]{1,0:T(8,128)(2,1)}, u32[]{:S(2)}) copy-start(bf16[2048,128]{1,0:T(8,128)(2,1)} %copy-done.15) | copy-start | bytes 1572868
  155.6 9.7 %copy-start.12 = (bf16[2048,128]{1,0:T(8,128)(2,1)S(1)}, bf16[2048,128]{1,0:T(8,128)(2,1)}, u32[]{:S(2)}) copy-start(bf16[2048,128]{1,0:T(8,128)(2,1)} %copy-done.11) | copy-start | bytes 1572868
  155.6 10.2 %copy-start.20 = (bf16[2048,128]{1,0:T(8,128)(2,1)S(1)}, bf16[2048,128]{1,0:T(8,128)(2,1)}, u32[]{:S(2)}) copy-start(bf16[2048,128]{1,0:T(8,128)(2,1)} %copy-done.19) | copy-start | bytes 1572868
  163.7 27.9 %collective-permute-start.9 = (bf16[2048,128]{1,0:T(8,128)(2,1)S(1)}, bf16[2048,128]{1,0:T(8,128)(2,1)S(1)}, u32[]{:S(2)}, u32[]{:S(2)}) collective-permute-start(bf16[2048,128]{1,0:T(8,128)(2,1)S(1)} %copy-done.16), channel_id=1, source_target_pairs={{0,16},{16,0},{1,17},{17,1},{2,18},{18,2},{3,19},{19,3},{4,20},{20... | collective-permute-start | bytes 1572872 | tf_op jit(solution)/shard_map/ppermute | solution.py:217
  165.3 26.8 %collective-permute-start.6 = (bf16[2048,128]{1,0:T(8,128)(2,1)S(1)}, bf16[2048,128]{1,0:T(8,128)(2,1)S(1)}, u32[]{:S(2)}, u32[]{:S(2)}) collective-permute-start(bf16[2048,128]{1,0:T(8,128)(2,1)S(1)} %copy-done.12), channel_id=1, source_target_pairs={{0,16},{16,0},{1,17},{17,1},{2,18},{18,2},{3,19},{19,3},{4,20},{20... | collective-permute-start | bytes 1572872 | tf_op jit(solution)/shard_map/ppermute | solution.py:217
  173.9 26.2 %collective-permute-start.12 = (bf16[2048,128]{1,0:T(8,128)(2,1)S(1)}, bf16[2048,128]{1,0:T(8,128)(2,1)S(1)}, u32[]{:S(2)}, u32[]{:S(2)}) collective-permute-start(bf16[2048,128]{1,0:T(8,128)(2,1)S(1)} %copy-done.12), channel_id=1, source_target_pairs={{0,1},{1,0},{2,3},{3,2},{4,5},{5,4},{6,7},{7,6},{8,9},{9,8},{10,11... | collective-permute-start | bytes 1572872 | tf_op jit(solution)/shard_map/ppermute | solution.py:217
  174.0 27.6 %collective-permute-start.13 = (bf16[2048,128]{1,0:T(8,128)(2,1)S(1)}, bf16[2048,128]{1,0:T(8,128)(2,1)S(1)}, u32[]{:S(2)}, u32[]{:S(2)}) collective-permute-start(bf16[2048,128]{1,0:T(8,128)(2,1)S(1)} %copy-done.16), channel_id=1, source_target_pairs={{0,1},{1,0},{2,3},{3,2},{4,5},{5,4},{6,7},{7,6},{8,9},{9,8},{10,11... | collective-permute-start | bytes 1572872 | tf_op jit(solution)/shard_map/ppermute | solution.py:217
  174.5 27.7 %collective-permute-start.18 = (bf16[2048,128]{1,0:T(8,128)(2,1)}, bf16[2048,128]{1,0:T(8,128)(2,1)S(1)}, u32[]{:S(2)}, u32[]{:S(2)}) collective-permute-start(bf16[2048,128]{1,0:T(8,128)(2,1)} %collective-permute-done.17.refs_2_), channel_id=1, source_target_pairs={{0,1},{1,0},{2,3},{3,2},{4,5},{5,4},{6,7},{7,6},{8,9},{9,8},{10,11... | collective-permute-start | bytes 1572872 | tf_op jit(solution)/shard_map/ppermute | solution.py:217
  183.0 9.2 %copy-start.14 = (bf16[2048,128]{1,0:T(8,128)(2,1)S(1)}, bf16[2048,128]{1,0:T(8,128)(2,1)}, u32[]{:S(2)}) copy-start(bf16[2048,128]{1,0:T(8,128)(2,1)} %copy-done.13) | copy-start | bytes 1572868
  183.0 9.2 %copy-start.18 = (bf16[2048,128]{1,0:T(8,128)(2,1)S(1)}, bf16[2048,128]{1,0:T(8,128)(2,1)}, u32[]{:S(2)}) copy-start(bf16[2048,128]{1,0:T(8,128)(2,1)} %copy-done.17) | copy-start | bytes 1572868
  191.6 12.1 %copy-start.10 = (bf16[2048,128]{1,0:T(8,128)(2,1)S(1)}, bf16[2048,128]{1,0:T(8,128)(2,1)}, u32[]{:S(2)}) copy-start(bf16[2048,128]{1,0:T(8,128)(2,1)} %copy-done.9) | copy-start | bytes 1572868
  191.6 26.9 %collective-permute-start.10 = (bf16[2048,128]{1,0:T(8,128)(2,1)S(1)}, bf16[2048,128]{1,0:T(8,128)(2,1)S(1)}, u32[]{:S(2)}, u32[]{:S(2)}) collective-permute-start(bf16[2048,128]{1,0:T(8,128)(2,1)S(1)} %collective-permute-done.9.refs_2_), channel_id=1, source_target_pairs={{0,1},{1,0},{2,3},{3,2},{4,5},{5,4},{6,7},{7,6},{8,9},{9,8},{10,11... | collective-permute-start | bytes 1572872 | tf_op jit(solution)/shard_map/ppermute | solution.py:217
  192.1 27.1 %collective-permute-start.7 = (bf16[2048,128]{1,0:T(8,128)(2,1)S(1)}, bf16[2048,128]{1,0:T(8,128)(2,1)S(1)}, u32[]{:S(2)}, u32[]{:S(2)}) collective-permute-start(bf16[2048,128]{1,0:T(8,128)(2,1)S(1)} %collective-permute-done.6.refs_0_), channel_id=1, source_target_pairs={{0,1},{1,0},{2,3},{3,2},{4,5},{5,4},{6,7},{7,6},{8,9},{9,8},{10,11... | collective-permute-start | bytes 1572872 | tf_op jit(solution)/shard_map/ppermute | solution.py:217
  200.1 27.4 %collective-permute-start.40 = (bf16[1024,256]{1,0:T(8,128)(2,1)S(1)}, bf16[1024,256]{1,0:T(8,128)(2,1)S(1)}, u32[]{:S(2)}, u32[]{:S(2)}) collective-permute-start(bf16[1024,256]{1,0:T(8,128)(2,1)S(1)} %get-tuple-element.36), channel_id=1, source_target_pairs={{0,2},{2,0},{1,3},{3,1},{4,6},{6,4},{5,7},{7,5},{8,10},{10,8},{9,1... | collective-permute-start | bytes 1572872 | tf_op jit(solution)/shard_map/ppermute | solution.py:221
  201.7 26.5 %collective-permute-start.37 = (bf16[1024,256]{1,0:T(8,128)(2,1)S(1)}, bf16[1024,256]{1,0:T(8,128)(2,1)S(1)}, u32[]{:S(2)}, u32[]{:S(2)}) collective-permute-start(bf16[1024,256]{1,0:T(8,128)(2,1)S(1)} %get-tuple-element.34), channel_id=1, source_target_pairs={{0,2},{2,0},{1,3},{3,1},{4,6},{6,4},{5,7},{7,5},{8,10},{10,8},{9,1... | collective-permute-start | bytes 1572872 | tf_op jit(solution)/shard_map/ppermute | solution.py:221
  202.2 35.2 %collective-permute-start.32 = (bf16[1024,256]{1,0:T(8,128)(2,1)S(1)}, bf16[1024,256]{1,0:T(8,128)(2,1)S(1)}, u32[]{:S(2)}, u32[]{:S(2)}) collective-permute-start(bf16[1024,256]{1,0:T(8,128)(2,1)S(1)} %get-tuple-element.32), channel_id=1, source_target_pairs={{0,2},{2,0},{1,3},{3,1},{4,6},{6,4},{5,7},{7,5},{8,10},{10,8},{9,1... | collective-permute-start | bytes 1572872 | tf_op jit(solution)/shard_map/ppermute | solution.py:221
  218.5 30.1 %collective-permute-start.29 = (bf16[1024,256]{1,0:T(8,128)(2,1)S(1)}, bf16[1024,256]{1,0:T(8,128)(2,1)S(1)}, u32[]{:S(2)}, u32[]{:S(2)}) collective-permute-start(bf16[1024,256]{1,0:T(8,128)(2,1)S(1)} %get-tuple-element.30), channel_id=1, source_target_pairs={{0,2},{2,0},{1,3},{3,1},{4,6},{6,4},{5,7},{7,5},{8,10},{10,8},{9,1... | collective-permute-start | bytes 1572872 | tf_op jit(solution)/shard_map/ppermute | solution.py:221
  219.2 40.7 %collective-permute-start.22 = (bf16[1024,256]{1,0:T(8,128)(2,1)S(1)}, bf16[1024,256]{1,0:T(8,128)(2,1)S(1)}, u32[]{:S(2)}, u32[]{:S(2)}) collective-permute-start(bf16[1024,256]{1,0:T(8,128)(2,1)S(1)} %get-tuple-element.28), channel_id=1, source_target_pairs={{0,2},{2,0},{1,3},{3,1},{4,6},{6,4},{5,7},{7,5},{8,10},{10,8},{9,1... | collective-permute-start | bytes 1572872 | tf_op jit(solution)/shard_map/ppermute | solution.py:221
  227.5 43.6 %collective-permute-start.19 = (bf16[1024,256]{1,0:T(8,128)(2,1)S(1)}, bf16[1024,256]{1,0:T(8,128)(2,1)S(1)}, u32[]{:S(2)}, u32[]{:S(2)}) collective-permute-start(bf16[1024,256]{1,0:T(8,128)(2,1)S(1)} %get-tuple-element.26), channel_id=1, source_target_pairs={{0,2},{2,0},{1,3},{3,1},{4,6},{6,4},{5,7},{7,5},{8,10},{10,8},{9,1... | collective-permute-start | bytes 1572872 | tf_op jit(solution)/shard_map/ppermute | solution.py:221
  228.2 54.2 %collective-permute-start.14 = (bf16[1024,256]{1,0:T(8,128)(2,1)S(1)}, bf16[1024,256]{1,0:T(8,128)(2,1)S(1)}, u32[]{:S(2)}, u32[]{:S(2)}) collective-permute-start(bf16[1024,256]{1,0:T(8,128)(2,1)S(1)} %get-tuple-element.24), channel_id=1, source_target_pairs={{0,2},{2,0},{1,3},{3,1},{4,6},{6,4},{5,7},{7,5},{8,10},{10,8},{9,1... | collective-permute-start | bytes 1572872 | tf_op jit(solution)/shard_map/ppermute | solution.py:221
  237.4 55.7 %collective-permute-start.11 = (bf16[1024,256]{1,0:T(8,128)(2,1)S(1)}, bf16[1024,256]{1,0:T(8,128)(2,1)S(1)}, u32[]{:S(2)}, u32[]{:S(2)}) collective-permute-start(bf16[1024,256]{1,0:T(8,128)(2,1)S(1)} %get-tuple-element.22), channel_id=1, source_target_pairs={{0,2},{2,0},{1,3},{3,1},{4,6},{6,4},{5,7},{7,5},{8,10},{10,8},{9,1... | collective-permute-start | bytes 1572872 | tf_op jit(solution)/shard_map/ppermute | solution.py:221
  (3 other events, 2.3 us)

commit v2 on v0

v2 whole, which is shorter than its diff:
```python
import functools

import jax
import jax.numpy as jnp
from jax import lax
from jax.experimental import pallas as pl
from jax.experimental.pallas import tpu as pltpu
from jax.sharding import PartitionSpec as P

DH = 128
LANES = 128
EPS = 1e-06
F32 = jnp.float32
BF16 = jnp.bfloat16
MIB = 1 << 20
VMEM_MIB = 16
ATTN_MIB = 16
ANY = pl.BlockSpec(memory_space=pl.ANY)
HBM = pl.BlockSpec(memory_space=pltpu.HBM)


def params(mib=VMEM_MIB):
    return pltpu.CompilerParams(vmem_limit_bytes=mib * MIB)


def dot(a, b):
    return lax.dot_general(a, b, (((1,), (0,)), ((), ())), preferred_element_type=F32)


def cost(us):
    return pl.CostEstimate(flops=int(us * 1e9), bytes_accessed=int(us * 3e6), transcendentals=0)


def dot_nt(a, b):
    return lax.dot_general(a, b, (((1,), (1,)), ((), ())), preferred_element_type=F32)


def dot_tn(a, b):
    return lax.dot_general(a, b, (((0,), (0,)), ((), ())), preferred_element_type=F32)


def gate_kernel(*refs):
    pass


def gate(x, *deps):
    return pl.pallas_call(
        gate_kernel,
        in_specs=[ANY] * (1 + len(deps)),
        out_specs=ANY,
        out_shape=jax.ShapeDtypeStruct(x.shape, x.dtype),
        input_output_aliases={0: 0},
        compiler_params=params(),
        cost_estimate=cost(0.01),
        name="gate",
    )(x, *deps)


def pair_up(mats):
    zero = jnp.zeros_like(mats[0])
    return jnp.concatenate(
        [
            jnp.concatenate([m if i == j else zero for j in range(len(mats))], axis=1)
            for i, m in enumerate(mats)
        ],
        axis=0,
    )


def split_dot(a, b):
    high = b.astype(BF16)
    return dot(a, high) + dot(a, (b - high.astype(F32)).astype(BF16))


def heads_of(i, size):
    return slice(i * DH, (i + size) * DH)


def state_kernel(per, size, steps, k_hbm, v_hbm, *refs):
    out_hbm, send_hbm = refs[-2:]

    def body(k_ref, v_ref, out_ref, send_ref):
        for i in range(0, per, size):
            state = dot_tn(k_ref[:, heads_of(i, size)], v_ref[:, heads_of(i, size)])
            for j in range(size):
                own = state[heads_of(j, 1), heads_of(j, 1)]
                out_ref[i + j] = own
                send_ref[i + j] = own.astype(BF16)

    spec = pl.BlockSpec((k_hbm.shape[0], per * DH), lambda i: (0, i))
    state = pl.BlockSpec((per, DH, DH), lambda i: (i, 0, 0))
    pltpu.emit_pipeline(body, grid=(steps,), in_specs=[spec] * 2, out_specs=[state] * 2)(
        k_hbm, v_hbm, out_hbm, send_hbm
    )


def block_states(keys, values, heads, *deps):
    per = 4 if heads % 4 == 0 else 1
    size = 2 if per % 2 == 0 else 1
    return pl.pallas_call(
        functools.partial(state_kernel, per, size, heads // per),
        in_specs=[HBM] * 2 + [ANY] * len(deps),
        out_specs=[ANY] * 2,
        out_shape=[jax.ShapeDtypeStruct((heads, DH, DH), t) for t in (F32, BF16)],
        compiler_params=params(60),
        cost_estimate=cost(1000),
        name="block_states",
    )(keys, values, *deps)


def intra_kernel(size, chunk, steps, first, place, q_hbm, k_hbm, v_hbm, *refs):
    rows = q_hbm.shape[0]
    row_ids = lax.broadcasted_iota(jnp.int32, (chunk, chunk), 0)
    col_ids = lax.broadcasted_iota(jnp.int32, (chunk, chunk), 1)
    causal = col_ids <= row_ids

    def body(q_ref, k_ref, v_ref, out_ref):
        state = None
        for at in range(0, rows, chunk):
            part = slice(at, at + chunk)
            for i in range(size):
                cols = heads_of(i, 1)
                scores = dot_nt(q_ref[part, cols], k_ref[part, cols])
                scores = jnp.where(causal, scores, 0.0).astype(BF16)
                mixed = dot(scores, v_ref[part, cols])
                if state is not None:
                    mixed = mixed + split_dot(q_ref[part, cols], state[i])
                out_ref[part, cols] = mixed
            if at + chunk < rows:
                step = dot_tn(k_ref[part, :], v_ref[part, :])
                step = [step[heads_of(i, 1), heads_of(i, 1)] for i in range(size)]
                state = step if state is None else [a + b for a, b in zip(state, step)]

    start = first(place)
    spec = pl.BlockSpec((rows, size * DH), lambda i: (0, start + i))
    out = pl.BlockSpec((rows, size * DH), lambda i: (0, i))
    pltpu.emit_pipeline(body, grid=(steps,), in_specs=[spec] * 3, out_specs=[out])(
        q_hbm, k_hbm, v_hbm, refs[-2]
    )
    refs[-1][...] = jnp.zeros_like(refs[-1])


def intra_block(place, o, b, n_sub, n_band, queries, keys, values, part, *deps):
    rows = queries.shape[0]
    part //= n_band
    size = 2 if part % 2 == 0 else 1
    steps = part // size
    chunk = 256 if rows % 256 == 0 else rows

    def first(t):
        return (lax.rem(t[3] + (n_sub - o), n_sub) * n_band + b) * steps

    return pl.pallas_call(
        functools.partial(intra_kernel, size, chunk, steps, first),
        grid_spec=pltpu.PrefetchScalarGridSpec(
            num_scalar_prefetch=1,
            grid=(1,),
            in_specs=[HBM] * 3 + [ANY] * len(deps),
            out_specs=[ANY, pl.BlockSpec((8, LANES), lambda i, t: (0, 0))],
        ),
        out_shape=[
            jax.ShapeDtypeStruct((rows, part * DH), F32),
            jax.ShapeDtypeStruct((8, LANES), F32),
        ],
        compiler_params=params(40),
        cost_estimate=cost(4.4),
        name="intra_block",
    )(place, queries, keys, values, *deps)


def norm_kernel(per, size, n_sub, o, place, q_ref, a_ref, p_ref, g_ref, *refs):
    sib_refs, out_ref = refs[: n_sub - 1], refs[-2]
    refs[-1][...] = jnp.zeros_like(refs[-1])
    for i in range(0, per, size):
        mats = []
        for j in range(i, i + size):
            state = p_ref[j].astype(F32)
            for n, sib in enumerate(sib_refs):
                state = state + jnp.where(place[3] >= n + 1, sib[j].astype(F32), 0.0)
            mats.append(state)
        both = a_ref[:, heads_of(i, size)] + split_dot(q_ref[:, heads_of(i, size)], pair_up(mats))
        for j in range(size):
            mixed = both[:, heads_of(j, 1)]
            mean_sq = jnp.mean(mixed * mixed, axis=-1, keepdims=True)
            normed = mixed * lax.rsqrt(mean_sq + EPS) * g_ref[i + j]
            out_ref[:, heads_of(i + j, 1)] = normed.astype(BF16)


def norm_part(place, o, b, n_sub, n_band, queries, intra, prefix, gain, sibs, normed, *deps):
    rows, width = queries.shape
    part = prefix.shape[0] // n_band
    per = 4 if part % 4 == 0 else 1
    size = 2 if per % 2 == 0 else 1
    steps = part // per

    def which(t):
        return (lax.rem(t[3] - o + n_sub, n_sub) * n_band + b) * steps

    cols = pl.BlockSpec((rows, per * DH), lambda i, t: (0, which(t) + i))
    mat = pl.BlockSpec((per, DH, DH), lambda i, t: (which(t) + i, 0, 0))
    in_specs = [
        cols,
        pl.BlockSpec((rows, per * DH), lambda i, t: (0, i)),
        pl.BlockSpec((per, DH, DH), lambda i, t: (b * steps + i, 0, 0)),
        pl.BlockSpec((per, 1, DH), lambda i, t: (which(t) + i, 0, 0)),
    ] + [mat] * len(sibs)
    operands = [queries, intra, prefix, gain, *sibs, *deps]
    in_specs += [ANY] * len(deps)
    aliases = {}
    if normed is not None:
        in_specs.append(ANY)
        operands.append(normed)
        aliases = {len(operands): 0}
    return pl.pallas_call(
        functools.partial(norm_kernel, per, size, n_sub, o),
        grid_spec=pltpu.PrefetchScalarGridSpec(
            num_scalar_prefetch=1,
            grid=(steps,),
            in_specs=in_specs,
            out_specs=[cols, pl.BlockSpec((8, LANES), lambda i, t: (0, 0))],
        ),
        out_shape=[
            jax.ShapeDtypeStruct((rows, width), BF16),
            jax.ShapeDtypeStruct((8, LANES), F32),
        ],
        input_output_aliases=aliases,
        compiler_params=params(ATTN_MIB),
        cost_estimate=cost(1.8),
        name="norm_part",
    )(place, *operands)


class Plan:
    def __init__(self, sizes, cols):
        self.n_group, self.n_ctx, self.n_head, self.n_sub = (
            sizes[a] for a in ("groups", "ctx", "head", "sub")
        )
        self.near = self.n_ctx // self.n_head
        self.split = self.n_group if cols % (self.n_group * LANES) == 0 else 1
        self.rounds = cols // (self.split * LANES)
        self.tiles = self.split * self.rounds
        self.line = self.n_head == 2 and self.near == 2

    def own(self, place):
        return jnp.bitwise_xor(place[1] // self.near, place[2])

    def mine(self, place, step):
        r, _, o, _ = step
        return lax.rem(place[0] + (self.n_group - o), self.split) * self.rounds + r

    def target(self, place, step, j):
        low = jnp.bitwise_xor(lax.rem(place[1], self.near), step[1])
        if self.line:
            far = jnp.where(place[1] < self.near, step[1], self.near - 1 - step[1])
            low = jnp.where(self.own(place) == 0, low, far)
        sub = lax.rem(place[3] + (self.n_sub - j), self.n_sub)
        return (low * self.n_sub + sub) * self.tiles + self.mine(place, step)

    def holder(self, place, step, kh, j):
        low = jnp.bitwise_xor(lax.rem(place[1], self.near), step[1])
        far = jnp.where(place[1] < self.near, step[1], self.near - 1 - step[1])
        half = place[1] // self.near
        ctx = half * self.near + low if kh == 0 else (1 - half) * self.near + far
        group = lax.rem(place[0] + (self.n_group - step[2]), self.split)
        sub = lax.rem(place[3] + (self.n_sub - j), self.n_sub)
        return (group * self.n_ctx + ctx) * self.n_sub + sub


def lanes(i, count):
    return pl.ds(pl.multiple_of(i * LANES, LANES), count * LANES)


def add_up(plan, step, place, stage, keep_hbm, recv_hbm, out_hbm, sems):
    keep, recv, total = stage
    ins = [pltpu.make_async_copy(keep_hbm, keep, sems.at[0])]
    ins += [
        pltpu.make_async_copy(r, recv.at[i], sems.at[1 + i]) for i, r in enumerate(recv_hbm)
    ]
    outs = [
        pltpu.make_async_copy(
            total.at[:, j * step[3] * LANES : (j + 1) * step[3] * LANES],
            out_hbm.at[:, lanes(plan.target(place, step, j), step[3])],
            sems.at[plan.n_head + j],
        )
        for j in range(plan.n_sub)
    ]

    def middle():
        for copy in ins:
            copy.wait()
        value = keep[...]
        for i in range(len(recv_hbm)):
            value = value + recv[i].astype(F32)
        total[...] = value.astype(BF16)
        for copy in outs:
            copy.start()

    def last():
        for copy in outs:
            copy.wait()

    for copy in ins:
        copy.start()
    return middle, last


def project_kernel(plan, step, which, kinds, before, n_deps, place, x_hbm, *refs):
    n_head, n_sub = plan.n_head, plan.n_sub
    refs = list(refs)

    def take(n):
        got = refs[:n]
        del refs[:n]
        return got

    w_hbm = take(len(kinds))
    if before is not None:
        keep_old, recv_old = take(1)[0], take(n_head - 1)
    take(n_deps)
    if before is not None:
        take(1 if before[1] else 0)
    res_hbm = take(len(which))
    if before is not None:
        out_hbm = take(1)[0]
    x, w, keep, send, old_keep, old_recv, total, x_sem, w_sem, res_sem, old_sem = refs
    rows = x.shape[0]
    tiles = [slice(j * step[3] * LANES, (j + 1) * step[3] * LANES) for j in range(n_sub)]
    tile = 256 if rows % 256 == 0 else rows
    own = plan.own(place)
    loads = []
    for i in range(n_head * n_sub):
        if kinds[0] == 3:
            src = w_hbm[0].at[plan.holder(place, step, i // n_sub, i % n_sub)]
        else:
            src = w_hbm[i]
            if kinds[i]:
                src = src.at[:, lanes(plan.mine(place, step), step[3])]
        dst = w.at[i // n_sub, :, tiles[i % n_sub]]
        loads.append(pltpu.make_async_copy(src, dst, w_sem.at[i]))
    parts = [slice(at, at + tile) for at in range(0, rows, tile)]
    rows_in = [
        pltpu.make_async_copy(x_hbm.at[p], x.at[p], x_sem.at[i]) for i, p in enumerate(parts)
    ]
    rows_in[0].start()
    for copy in loads:
        copy.start()
    for copy in rows_in[1:]:
        copy.start()
    if before is not None:
        stage = (old_keep, old_recv, total)
        middle, last = add_up(
            plan, before[0], place, stage, keep_old, recv_old, out_hbm, old_sem
        )
    results = []
    for n, o in enumerate(which):
        slot = jnp.bitwise_xor(own, o)
        for j in range(n_sub):
            dst = w.at[slot, :, tiles[j]]
            pltpu.make_async_copy(dst, dst, w_sem.at[slot * n_sub + j]).wait()
        for i, p in enumerate(parts):
            if n == 0:
                rows_in[i].wait()
            res = dot(x[p], w[slot])
            if o == 0:
                keep[p] = res
            else:
                send[o - 1, p] = res.astype(BF16)
        src = keep if o == 0 else send.at[o - 1]
        results.append(pltpu.make_async_copy(src, res_hbm[n], res_sem.at[o]))
        results[-1].start()
        if before is not None and n == 0:
            middle()
    for o in range(n_head):
        if o not in which:
            slot = jnp.bitwise_xor(own, o)
            for j in range(n_sub):
                dst = w.at[slot, :, tiles[j]]
                pltpu.make_async_copy(dst, dst, w_sem.at[slot * n_sub + j]).wait()
    for copy in results:
        copy.wait()
    if before is not None:
        last()


def project(plan, place, step, which, normed, pieces, before, out, deps):
    rows, depth = normed.shape
    n_head, n_sub = plan.n_head, plan.n_sub
    width = n_sub * step[3] * LANES
    kinds = [3 if p.ndim == 3 else int(p.shape[1] != step[3] * LANES) for p in pieces]
    operands = [normed, *pieces]
    shapes = [jax.ShapeDtypeStruct((rows, width), BF16 if o else F32) for o in which]
    aliases, info = {}, None
    if before is not None:
        operands += [before[1], *before[2]]
        info = (before[0], out is not None)
    operands += deps
    if before is not None:
        shapes.append(jax.ShapeDtypeStruct((rows, n_sub * plan.near * plan.tiles * LANES), BF16))
        if out is not None:
            operands.append(out)
            aliases = {len(operands): len(shapes) - 1}
    tiles = rows // 256 if rows % 256 == 0 else 1
    old = width if before is None else n_sub * before[0][3] * LANES
    dma = pltpu.SemaphoreType.DMA
    return pl.pallas_call(
        functools.partial(project_kernel, plan, step, which, kinds, info, len(deps)),
        grid_spec=pltpu.PrefetchScalarGridSpec(
            num_scalar_prefetch=1,
            grid=(1,),
            in_specs=[ANY] * len(operands),
            out_specs=[ANY] * len(shapes),
            scratch_shapes=[
                pltpu.VMEM((rows, depth), BF16),
                pltpu.VMEM((n_head, depth, width), BF16),
                pltpu.VMEM((rows, width), F32),
                pltpu.VMEM((max(1, n_head - 1), rows, width), BF16),
                pltpu.VMEM((rows, old), F32),
                pltpu.VMEM((max(1, n_head - 1), rows, old), BF16),
                pltpu.VMEM((rows, old), BF16),
                dma((tiles,)),
                dma((n_head * n_sub,)),
                dma((n_head,)),
                dma((n_head + n_sub,)),
            ],
        ),
        out_shape=shapes,
        input_output_aliases=aliases,
        compiler_params=params(32),
        cost_estimate=cost(2.7),
        name="project",
    )(place, *operands)


def combine_kernel(plan, step, n_recv, place, *refs):
    keep_hbm, recv_hbm = refs[0], refs[1 : 1 + n_recv]
    out_hbm, keep, recv, total, sems = refs[-5:]
    middle, last = add_up(
        plan, step, place, (keep, recv, total), keep_hbm, recv_hbm, out_hbm, sems
    )
    middle()
    last()


def combine(plan, place, step, keep, recvs, out):
    rows, width = keep.shape
    operands = [keep, *recvs, out]
    return pl.pallas_call(
        functools.partial(combine_kernel, plan, step, len(recvs)),
        grid_spec=pltpu.PrefetchScalarGridSpec(
            num_scalar_prefetch=1,
            grid=(1,),
            in_specs=[ANY] * len(operands),
            out_specs=ANY,
            scratch_shapes=[
                pltpu.VMEM((rows, width), F32),
                pltpu.VMEM((max(1, len(recvs)), rows, width), BF16),
                pltpu.VMEM((rows, width), BF16),
                pltpu.SemaphoreType.DMA((plan.n_head + plan.n_sub,)),
            ],
        ),
        out_shape=jax.ShapeDtypeStruct(out.shape, BF16),
        input_output_aliases={len(operands): 0},
        compiler_params=params(),
        cost_estimate=cost(0.5),
        name="combine",
    )(place, *operands)


def shift(x, axis, size, o):
    return lax.ppermute(x, axis, [(i, (i + o) % size) for i in range(size)])


def swap(x, axis, size, k):
    return lax.ppermute(x, axis, [(i, i ^ k) for i in range(size)])


def local(sizes, queries, keys, values, out_weight, norm_gain):
    rows, width = queries.shape
    heads = width // DH
    depth, cols = out_weight.shape
    plan = Plan(sizes, cols)
    n_group, n_ctx, n_head, n_sub = plan.n_group, plan.n_ctx, plan.n_head, plan.n_sub
    near, split, rounds = plan.near, plan.split, plan.rounds
    place = jnp.stack([lax.axis_index(a) for a in ("groups", "ctx", "head", "sub")]).astype(jnp.int32)
    s = place[3]

    steps = [(r, kl, o, 1) for r in range(rounds) for kl in range(near) for o in range(split)]
    line = plan.line and rounds == 2 and split == 2

    whole = [out_weight] + [shift(out_weight, "sub", n_sub, j) for j in range(1, n_sub)]

    def cut(r, count):
        at = plan.mine(place, (r, 0, 0, count)) * LANES
        return lax.dynamic_slice(out_weight, (0, at), (depth, count * LANES))

    first = [cut(r, 1) for r in range(rounds)]
    pieces = {(r, 0, o, 1, 0): whole for r in range(rounds) for o in range(split)}
    later = {}
    held = {step: [] for step in steps}

    def cross(piece):
        return [piece] + [shift(piece, "sub", n_sub, j) for j in range(1, n_sub)]

    def hold(n, *arrays):
        held[steps[n]] += arrays

    part = heads // n_sub
    states, sent = block_states(keys, values, heads, first[0])
    sibs = [shift(sent, "sub", n_sub, o) for o in range(1, n_sub)]
    total = sum(
        lax.dynamic_slice_in_dim(x, s * part, part).astype(F32) for x in [states, *sibs]
    )
    ends, middle, out_way = [(0, 1), (1, 0), (2, 3), (3, 2)], [(1, 2), (2, 1)], [(1, 0), (2, 3)]
    prefix = jnp.zeros((part, DH, DH), BF16)
    n_band = 1
    bands = [(o, b) for o in range(n_sub) for b in range(n_band)]
    intra, tokens, hops = {}, [], []
    for i in range(n_ctx - 1):
        hop = (prefix.astype(F32) + total).astype(BF16)
        if i:
            hop = gate(hop, *tokens[i - 1 : i])
        hops.append(hop)
        if i < len(bands):
            deps = [hop] if i == 0 else [hop, *whole[1:]]
            intra[bands[i]], token = intra_block(
                place, *bands[i], n_sub, n_band, queries, keys, values, part, *deps
            )
            tokens.append(token)
        prefix = prefix + lax.ppermute(hop, "ctx", [(i, i + 1)])
    gain = norm_gain.reshape(heads, 1, DH)

    normed, normed_token = None, None
    for o in range(n_sub):
        mat = prefix if o == 0 else shift(prefix, "sub", n_sub, o)
        for b in range(n_band):
            deps = []
            normed, token = norm_part(
                place, o, b, n_sub, n_band, queries, intra[o, b], mat, gain, sibs, normed, *deps
            )
            normed_token = token if normed_token is None else normed_token

    if line:
        inner = (place[1] == 1) | (place[1] == 2)

        def along(x, perm, *deps):
            return lax.ppermute(gate(x, *deps) if deps else x, "ctx", perm)

        def over(x, *deps):
            return shift(gate(x, *deps) if deps else x, "groups", n_group, 1)

        near_a = gate(along(first[0], ends), tokens[0])
        across_a = gate(along(first[0], middle), tokens[0])
        y_near_a = over(near_a)
        outward_a = gate(along(across_a, out_way), tokens[1])
        across_b = gate(along(near_a, middle), tokens[1])
        outward_b = gate(along(across_b, out_way), normed_token)
        far_a = jnp.where(inner, across_a, outward_a)
        far_b = jnp.where(inner, across_b, outward_b)
        across_c = along(first[1], middle, across_b)
        y_far_a = over(far_a, prefix)
        y_far_b = over(far_b, y_far_a, token)
        near_c = along(first[1], ends, outward_b)
        outward_c = along(across_c, out_way, normed_token)
        pieces[0, 0, 0, 1, 1] = cross(far_a)
        pieces[0, 0, 1, 1, 1] = cross(y_far_a)
        pieces[0, 1, 0, 1, 0] = cross(gate(near_a, prefix))
        pieces[0, 1, 0, 1, 1] = cross(far_b)
        pieces[0, 1, 1, 1, 0] = cross(gate(y_near_a, normed_token))
        hold(0, y_near_a, across_c, *pieces[0, 1, 0, 1, 0][1:])
        hold(1, near_c, outward_c, y_far_b, *pieces[0, 1, 0, 1, 1][1:], *pieces[0, 1, 1, 1, 0][1:])

        def after_0(*sent):
            pieces[0, 1, 1, 1, 1] = cross(gate(y_far_b, *sent))
            hold(2, *pieces[0, 1, 1, 1, 1][1:])

        def after_1(*sent):
            far_c = jnp.where(inner, across_c, gate(outward_c, *sent))
            pieces[1, 0, 0, 1, 1] = cross(far_c)
            later["y_far_c"] = over(far_c)
            later["across_d"] = along(near_c, middle, *sent)
            pieces[1, 1, 0, 1, 0] = cross(gate(near_c, *sent))
            hold(3, later["y_far_c"], later["across_d"], *pieces[1, 1, 0, 1, 0][1:])

        def after_2(*sent):
            outward_d = along(later["across_d"], out_way)
            later["y_near_c"] = over(near_c, later["y_far_c"])
            far_d = jnp.where(inner, later["across_d"], outward_d)
            pieces[1, 0, 1, 1, 1] = cross(later["y_far_c"])
            pieces[1, 1, 0, 1, 1] = cross(far_d)
            y_far_d = over(far_d, later["y_near_c"])
            hold(4, outward_d, later["y_near_c"])
            pieces[1, 1, 1, 1, 0] = cross(later["y_near_c"])
            pieces[1, 1, 1, 1, 1] = cross(y_far_d)
            hold(5, *pieces[1, 1, 0, 1, 1][1:])
            hold(6, y_far_d, *pieces[1, 1, 1, 1, 0][1:])

        later = {0: after_0, 1: after_1, 2: after_2}
    else:
        for r in range(rounds):
            for kl in range(near):
                for kh in range(n_head):
                    if kl or kh:
                        piece = swap(first[r], "ctx", n_ctx, kh * near + kl)
                        pieces[r, kl, 0, 1, kh] = cross(piece)
                        for o in range(1, split):
                            pieces[r, kl, o, 1, kh] = cross(shift(piece, "groups", n_group, o))

    out, sent, late = None, [], None
    waiting = []
    others = list(range(1, n_head))
    for n, step in enumerate(steps):
        use = [p for kh in range(n_head) for p in pieces[*step, kh]]
        before = waiting.pop(0) if len(waiting) > 1 else None
        which = others if n == 0 and len(steps) > 1 else others + [0]
        deps = held[step] + sent
        shares = list(project(plan, place, step, which, normed, use, before, out, deps))
        if before is not None:
            out = shares.pop()
        got = dict(zip(which, shares))
        sent = shares[:1]
        if late:
            waiting[0] = late(sent)
            late = None
        recvs = [swap(got[i], "head", n_head, i) for i in others]
        waiting.append((step, got.get(0), recvs))
        if n in later:
            later[n](*sent)
        if 0 not in got:

            def late(deps, step=step, use=use, recvs=recvs):
                return step, project(plan, place, step, [0], normed, use, None, None, deps)[0], recvs

    if out is None:
        out = jnp.zeros((rows, n_sub * near * cols), BF16)
    for step, keep, recvs in waiting:
        out = combine(plan, place, step, keep, recvs, out)
    return out


def solution(mesh):
    return jax.shard_map(
        functools.partial(local, dict(mesh.shape)),
        mesh=mesh,
        in_specs=(
            P(("groups", "ctx", "sub"), "head"),
            P(("groups", "ctx", "sub"), "head"),
            P(("groups", "ctx", "sub"), "head"),
            P("head", ("ctx", "sub")),
            P("head"),
        ),
        out_specs=P(("groups", "ctx", "sub"), "head"),
        check_vma=False,
    )
```

time: 479 us -> 205 us (0.43)
  waiting for transfers between devices: 383 us -> 58.6 us
  Pallas kernels: 0 us -> 83.8 us
  matrix products: 59.5 us -> 0 us
  starting transfers between devices: 0.08 us -> 47.4 us
  between operations: 13.2 us -> 0.83 us
  other arithmetic: 14.1 us -> 4.54 us
    all_gather x2 -> x0, waiting for transfers between devices: 193 us -> none  [the longest x1 136 us: local(): lax.all_gather(out_weight, ('ctx', 'sub'), axis=1, tiled=True)]
    reduce_scatter x1 -> x0, waiting for transfers between devices: 189 us -> none  [local(): lax.psum_scatter(partial_out, 'head', scatter_dimension=1, tiled=True)]
    pallas_call x0 -> x35, Pallas kernels: none -> 83.8 us  [the longest x9 49.8 us: project(): pl.pallas_call(functools.partial(project_kernel, plan, step, which, kinds...]
    dot_general x4 -> x0, matrix products: 59.5 us -> none  [the longest x1 23.7 us: local(): jnp.dot(normed, lax.all_gather(out_weight, ('ctx', 'sub'), axis=1, tiled=...]
    ppermute x0 -> x42, waiting for transfers between devices: none -> 58.6 us  [the longest x8 25.6 us: swap(): return lax.ppermute(x, axis, [(i, i ^ k) for i in range(size)])]
    ppermute x0 -> x42, starting transfers between devices: none -> 47.4 us  [the longest x10 23.4 us: along(): return lax.ppermute(gate(x, *deps) if deps else x, 'ctx', perm)]
    convert_element_type x2 -> x3, other arithmetic: 8.96 us -> 2.09 us  [local(): hop = (prefix.astype(F32) + total).astype(BF16)]
    reshape x1 -> x0, local copies, waits for them, and re-layouts: 6.39 us -> none  [local(): key_blk = keys.reshape(tok_rows, head_count, DH)]
  transfers between devices with their start and end apart: 3 -> 42, of which waited for: 3 -> 13; matrix products, arithmetic and copies ran while one was open for 8% -> 3% of each run, Pallas kernels for 0% -> 40%
where the time goes in v2:
time: 205 us; the launch traced here: 204 us
  Pallas kernels  83.8 us (41%)
  waiting for transfers between devices  58.6 us (29%)
  starting transfers between devices  47.4 us (23%)
  local copies, waits for them, and re-layouts  8.89 us (4%)
  other arithmetic  4.54 us (2%)
    pallas_call x9, Pallas kernels, project(): pl.pallas_call(functools.partial(project_kernel, plan, step, which, kinds...  49.8 us
    ppermute x8, waiting for transfers between devices, swap(): return lax.ppermute(x, axis, [(i, i ^ k) for i in range(size)])  25.6 us
    ppermute x10, starting transfers between devices, along(): return lax.ppermute(gate(x, *deps) if deps else x, 'ctx', perm)  23.4 us
    pallas_call x2, Pallas kernels, intra_block(): pl.pallas_call(functools.partial(intra_kernel, size, chunk, steps, first)...  17.6 us
    ppermute x10, waiting for transfers between devices, along(): return lax.ppermute(gate(x, *deps) if deps else x, 'ctx', perm)  15.4 us
    ppermute x21, waiting for transfers between devices, shift(): return lax.ppermute(x, axis, [(i, (i + o) % size) for i in range(size)])  12.1 us
    ppermute x21, starting transfers between devices, shift(): return lax.ppermute(x, axis, [(i, (i + o) % size) for i in range(size)])  12.1 us
    ppermute x8, starting transfers between devices, swap(): return lax.ppermute(x, axis, [(i, i ^ k) for i in range(size)])  7.69 us
  transfers between devices with their start and end apart: 42, of which 13 were waited for; matrix products, arithmetic and copies ran while one was open for 3% of the time, Pallas kernels for 40%

profile of v2, /device:TPU:16, one launch (start us, length us, event | category | flops | bytes accessed | tf_op | source)
XLA Modules:
  0.0 204.1 jit_solution(12565823281781044604)
XLA Ops:
  0.0 2.3 %constant_dynamic-slice_fusion = (bf16[2048,128]{1,0:T(8,128)(2,1)}, bf16[2048,128]{1,0:T(8,128)(2,1)}) fusion(bf16[2048,512]{1,0:T(8,128)(2,1)} %refs_0_.9, s32[]{:T(128)S(6)} %select_n.32, s32[]{:T(128)S(6)} %select_n.30), kind=kLoop, calls=%fused_computation.8 | loop fusion | bytes 2097160 | tf_op jit(solution)/shard_map/dynamic_slice | solution.py:494
  2.3 6.0 %block_states.1 = (f32[16,128,128]{2,1,0:T(8,128)}, bf16[16,128,128]{2,1,0:T(8,128)(2,1)}) custom-call(bf16[1024,2048]{1,0:T(8,128)(2,1)} %k_hbm.5, bf16[1024,2048]{1,0:T(8,128)(2,1)} %v_hbm.5, bf16[2048,128]{1,0:T(8,128)(2,1)} %get-tuple-element.68.refs_0_), custom_call_target="tpu_custom_call" | custom-call | flops 999999995904 | bytes 3000000000 | tf_op jit(solution)/shard_map/block_states/pallas_call | solution.py:100
  8.8 2.3 %collective-permute-start.12 = (bf16[2048,128]{1,0:T(8,128)(2,1)S(1)}, bf16[2048,128]{1,0:T(8,128)(2,1)}, u32[]{:S(2)}, u32[]{:S(2)}) collective-permute-start(bf16[2048,128]{1,0:T(8,128)(2,1)S(1)} %copy-done.12), channel_id=1, source_target_pairs={{4,8},{8,4},{5,9},{9,5},{6,10},{10,6},{7,11},{11,7},{20,24},{24,20... | collective-permute-start | bytes 1572872 | tf_op jit(solution)/shard_map/ppermute | solution.py:546
  11.1 0.7 collective-permute-start.6
  11.9 1.1 fusion.refs_0_
  13.0 0.7 collective-permute-start.1
  13.7 2.2 %copy-done.1 = bf16[1024,2048]{1,0:T(8,128)(2,1)S(1)} copy-done((bf16[1024,2048]{1,0:T(8,128)(2,1)S(1)}, bf16[1024,2048]{1,0:T(8,128)(2,1)}, u32[]{:S(2)}) %copy-start.1) | copy-done | bytes 4194328
  15.9 2.2 %copy-done.10 = bf16[1024,2048]{1,0:T(8,128)(2,1)S(1)} copy-done((bf16[1024,2048]{1,0:T(8,128)(2,1)S(1)}, bf16[1024,2048]{1,0:T(8,128)(2,1)}, u32[]{:S(2)}) %copy-start.10) | copy-done | bytes 4194328
  18.1 8.8 %intra_block.2 = (f32[1024,1024]{1,0:T(8,128)S(1)}, f32[8,128]{1,0:T(8,128)S(1)}) custom-call(s32[4]{0:T(128)S(1)} %pad_add_fusion.place, bf16[1024,2048]{1,0:T(8,128)(2,1)S(1)} %copy-done.1, bf16[1024,2048]{1,0:T(8,128)(2,1)S(1)} %copy-done.10, bf16[1024,2048]{1,0:T(8,128)(2,1)} %v_hbm.5, bf16[8,128,128]{2,1,0:T(8,128)(2,1)S(1)} %fusion.refs_0_), custom_call_target="tpu_custom_call" | custom-call | flops 4400000000 | bytes 13200000 | tf_op jit(solution)/shard_map/intra_block/pallas_call | solution.py:153
  27.1 1.6 collective-permute-start.3
  28.7 3.7 %collective-permute-start.13 = (bf16[2048,128]{1,0:T(8,128)(2,1)}, bf16[2048,128]{1,0:T(8,128)(2,1)}, u32[]{:S(2)}, u32[]{:S(2)}) collective-permute-start(bf16[2048,128]{1,0:T(8,128)(2,1)} %gate.27), channel_id=1, source_target_pairs={{4,0},{8,12},{5,1},{9,13},{6,2},{10,14},{7,3},{11,15},{20,16},{24,... | collective-permute-start | bytes 1572872 | tf_op jit(solution)/shard_map/ppermute | solution.py:546
  32.3 5.1 %collective-permute-start.7 = (bf16[2048,128]{1,0:T(8,128)(2,1)S(1)}, bf16[2048,128]{1,0:T(8,128)(2,1)S(1)}, u32[]{:S(2)}, u32[]{:S(2)}) collective-permute-start(bf16[2048,128]{1,0:T(8,128)(2,1)S(1)} %gate.21.refs_0_), channel_id=1, source_target_pairs={{4,8},{8,4},{5,9},{9,5},{6,10},{10,6},{7,11},{11,7},{20,24},{24,20... | collective-permute-start | bytes 1572872 | tf_op jit(solution)/shard_map/ppermute | solution.py:546
  37.4 2.8 %collective-permute-done.3 = bf16[8,128,128]{2,1,0:T(8,128)(2,1)S(1)} collective-permute-done((bf16[8,128,128]{2,1,0:T(8,128)(2,1)S(1)}, bf16[8,128,128]{2,1,0:T(8,128)(2,1)S(1)}, u32[]{:S(2)}, u32[]{:S(2)}) %collective-permute-start.3) | collective-permute-done | bytes 262176 | tf_op jit(solution)/shard_map/ppermute | solution.py:529
  40.2 0.9 add_convert_fusion
  41.1 8.8 %intra_block.3 = (f32[1024,1024]{1,0:T(8,128)S(1)}, f32[8,128]{1,0:T(8,128)S(1)}) custom-call(s32[4]{0:T(128)S(1)} %pad_add_fusion.place, bf16[1024,2048]{1,0:T(8,128)(2,1)S(1)} %copy-done.2, bf16[1024,2048]{1,0:T(8,128)(2,1)} %k_hbm.5, bf16[1024,2048]{1,0:T(8,128)(2,1)} %v_hbm.5, bf16[8,128,128]{2,1,0:T(8,128)(2,1)S(1)} %gate.19.refs_0_, ...), custom_call_target="tpu_custom_call" | custom-call | flops 4400000000 | bytes 13200000 | tf_op jit(solution)/shard_map/intra_block/pallas_call | solution.py:153
  49.9 2.0 copy-done.5
  51.9 2.0 collective-permute-start.4
  53.9 1.5 collective-permute-start.18
  55.5 1.6 collective-permute-start.8
  57.1 2.7 %collective-permute-done.4 = bf16[8,128,128]{2,1,0:T(8,128)(2,1)} collective-permute-done((bf16[8,128,128]{2,1,0:T(8,128)(2,1)S(1)}, bf16[8,128,128]{2,1,0:T(8,128)(2,1)}, u32[]{:S(2)}, u32[]{:S(2)}) %collective-permute-start.4) | collective-permute-done | bytes 262176 | tf_op jit(solution)/shard_map/ppermute | solution.py:529
  59.9 1.1 add.40.p_ref.refs_1_
  61.1 1.1 broadcast_select_fusion.3.refs_2_
  62.2 0.6 collective-permute-start.20
  62.8 1.9 collective-permute-start.10
  64.8 3.6 %norm_part.2 = (bf16[1024,2048]{1,0:T(8,128)(2,1)S(1)}, f32[8,128]{1,0:T(8,128)S(1)}) custom-call(s32[4]{0:T(128)S(1)} %pad_add_fusion.place, bf16[1024,2048]{1,0:T(8,128)(2,1)S(1)} %copy-done.3, f32[1024,1024]{1,0:T(8,128)S(1)} %copy-done.8, bf16[8,128,128]{2,1,0:T(8,128)(2,1)S(1)} %add.40.p_ref.refs_1_, f32[16,1,128]{2,1,0:T(1,128)S(1)} %bitcast.5, ...), custom_call_target="tpu_custom_call" | custom-call | flops 1800000000 | bytes 5400000 | tf_op jit(solution)/shard_map/norm_part/pallas_call | solution.py:214
  68.5 1.7 collective-permute-start.14
  70.1 3.6 %norm_part.3 = (bf16[1024,2048]{1,0:T(8,128)(2,1)S(1)}, f32[8,128]{1,0:T(8,128)S(1)}) custom-call(s32[4]{0:T(128)S(1)} %pad_add_fusion.place, bf16[1024,2048]{1,0:T(8,128)(2,1)S(1)} %copy-done.3, f32[1024,1024]{1,0:T(8,128)S(1)} %copy-done.6, bf16[8,128,128]{2,1,0:T(8,128)(2,1)S(1)} %collective-permute-done.5.p_ref, ...), custom_call_target="tpu_custom_call", output_to_operand_aliasing={{0}: (6, {})} | custom-call | flops 1800000000 | bytes 5400000 | tf_op jit(solution)/shard_map/norm_part/pallas_call | solution.py:214
  73.8 1.4 collective-permute-start.9
  75.3 3.2 %collective-permute-done.10.refs_5_ = bf16[2048,128]{1,0:T(8,128)(2,1)S(1)} collective-permute-done((bf16[2048,128]{1,0:T(8,128)(2,1)S(1)}, bf16[2048,128]{1,0:T(8,128)(2,1)S(1)}, u32[]{:S(2)}, u32[]{:S(2)}) %collective-permute-start.10) | collective-permute-done | bytes 524320 | tf_op jit(solution)/shard_map/ppermute | solution.py:546
  78.6 4.3 %collective-permute-done.14.refs_1_.refs_2_ = bf16[2048,128]{1,0:T(8,128)(2,1)S(1)} collective-permute-done((bf16[2048,128]{1,0:T(8,128)(2,1)S(1)}, bf16[2048,128]{1,0:T(8,128)(2,1)S(1)}, u32[]{:S(2)}, u32[]{:S(2)}) %collective-permute-start.14) | collective-permute-done | bytes 524320 | tf_op jit(solution)/shard_map/ppermute | solution.py:470
  82.8 3.5 %collective-permute-start.11 = (bf16[2048,128]{1,0:T(8,128)(2,1)S(1)}, bf16[2048,128]{1,0:T(8,128)(2,1)S(1)}, u32[]{:S(2)}, u32[]{:S(2)}) collective-permute-start(bf16[2048,128]{1,0:T(8,128)(2,1)S(1)} %gate.26), channel_id=1, source_target_pairs={{4,0},{8,12},{5,1},{9,13},{6,2},{10,14},{7,3},{11,15},{20,16},{24,... | collective-permute-start | bytes 1572872 | tf_op jit(solution)/shard_map/ppermute | solution.py:546
  86.3 1.6 collective-permute-start.16
  88.0 4.7 %project.9.refs_9_.refs_1_ = bf16[1024,256]{1,0:T(8,128)(2,1)S(1)} custom-call(s32[4]{0:T(128)S(1)} %pad_add_fusion.place, bf16[1024,2048]{1,0:T(8,128)(2,1)S(1)} %get-tuple-element.42.x_hbm, bf16[2048,512]{1,0:T(8,128)(2,1)S(1)} %copy-done, bf16[2048,512]{1,0:T(8,128)(2,1)} %collective-permute-done.2.refs_1_, ...), custom_call_target="tpu_custom_call" | custom-call | flops 2700000000 | bytes 8100000 | tf_op jit(solution)/shard_map/project/pallas_call | solution.py:405
  92.7 0.6 collective-permute-start.19
  93.3 0.9 collective-permute-start.33
  94.2 3.8 %collective-permute-done.11.refs_5_.refs_0_ = bf16[2048,128]{1,0:T(8,128)(2,1)S(1)} collective-permute-done((bf16[2048,128]{1,0:T(8,128)(2,1)S(1)}, bf16[2048,128]{1,0:T(8,128)(2,1)S(1)}, u32[]{:S(2)}, u32[]{:S(2)}) %collective-permute-start.11) | collective-permute-done | bytes 524320 | tf_op jit(solution)/shard_map/ppermute | solution.py:546
  98.0 1.6 collective-permute-done.16.refs_6_.refs_0_
  99.6 6.0 %project.10 = (bf16[1024,256]{1,0:T(8,128)(2,1)S(1)}, f32[1024,256]{1,0:T(8,128)S(1)}) custom-call(s32[4]{0:T(128)S(1)} %pad_add_fusion.place, bf16[1024,2048]{1,0:T(8,128)(2,1)S(1)} %get-tuple-element.42.x_hbm, bf16[2048,512]{1,0:T(8,128)(2,1)S(1)} %copy-done, bf16[2048,512]{1,0:T(8,128)(2,1)} %collective-permute-done.2.refs_1_, ...), custom_call_target="tpu_custom_call" | custom-call | flops 2700000000 | bytes 8100000 | tf_op jit(solution)/shard_map/project/pallas_call | solution.py:405
  105.7 1.9 collective-permute-start.25
  107.8 1.6 collective-permute-start.22
  109.6 1.8 collective-permute-start.31
  111.4 8.5 %collective-permute-done.25.refs_7_ = bf16[2048,128]{1,0:T(8,128)(2,1)S(1)} collective-permute-done((bf16[2048,128]{1,0:T(8,128)(2,1)S(1)}, bf16[2048,128]{1,0:T(8,128)(2,1)S(1)}, u32[]{:S(2)}, u32[]{:S(2)}) %collective-permute-start.25) | collective-permute-done | bytes 524320 | tf_op jit(solution)/shard_map/ppermute | solution.py:546
  119.9 1.3 collective-permute-start.26
  121.2 4.1 %project.11.refs_4_ = f32[1024,256]{1,0:T(8,128)S(1)} custom-call(s32[4]{0:T(128)S(1)} %pad_add_fusion.place, bf16[1024,2048]{1,0:T(8,128)(2,1)S(1)} %get-tuple-element.42.x_hbm, bf16[2048,512]{1,0:T(8,128)(2,1)S(1)} %copy-done, bf16[2048,512]{1,0:T(8,128)(2,1)} %collective-permute-done.2.refs_1_, bf16[2048,128]{1,0:T(8,128)(2,1)S(1)} %broadcast_select_fusion.3.refs_2_, ...), custom_call_target="tpu_custom_call" | custom-call | flops 2700000000 | bytes 8100000 | tf_op jit(solution)/shard_map/project/pallas_call | solution.py:405
  125.4 5.7 %project.12 = (bf16[1024,256]{1,0:T(8,128)(2,1)S(1)}, f32[1024,256]{1,0:T(8,128)S(1)}, bf16[1024,2048]{1,0:T(8,128)(2,1)}) custom-call(s32[4]{0:T(128)S(1)} %pad_add_fusion.place, bf16[1024,2048]{1,0:T(8,128)(2,1)S(1)} %get-tuple-element.42.x_hbm, bf16[2048,128]{1,0:T(8,128)(2,1)S(1)} %gate.32.refs_0_, ...), custom_call_target="tpu_custom_call" | custom-call | flops 2700000000 | bytes 8100000 | tf_op jit(solution)/shard_map/project/pallas_call | solution.py:405
  131.1 1.6 collective-permute-start.37
  132.7 1.6 collective-permute-start.23
  134.2 5.7 %project.13 = (bf16[1024,256]{1,0:T(8,128)(2,1)S(1)}, f32[1024,256]{1,0:T(8,128)S(1)}, bf16[1024,2048]{1,0:T(8,128)(2,1)}) custom-call(s32[4]{0:T(128)S(1)} %pad_add_fusion.place, bf16[1024,2048]{1,0:T(8,128)(2,1)S(1)} %get-tuple-element.42.x_hbm, bf16[2048,128]{1,0:T(8,128)(2,1)S(1)} %gate.31.refs_0_, ...), custom_call_target="tpu_custom_call", output_to_operand_aliasing={{2}: (12, {})} | custom-call | flops 2700000000 | bytes 8100000 | tf_op jit(solution)/shard_map/project/pallas_call | solution.py:405
  139.9 0.6 collective-permute-start.34
  140.6 6.1 %collective-permute-done.23.refs_1_.refs_7_.refs_0_ = bf16[2048,128]{1,0:T(8,128)(2,1)S(1)} collective-permute-done((bf16[2048,128]{1,0:T(8,128)(2,1)S(1)}, bf16[2048,128]{1,0:T(8,128)(2,1)S(1)}, u32[]{:S(2)}, u32[]{:S(2)}) %collective-permute-start.23) | collective-permute-done | bytes 524320 | tf_op jit(solution)/shard_map/ppermute | solution.py:470
  146.8 1.6 collective-permute-start.27
  148.4 6.1 %project.14 = (bf16[1024,256]{1,0:T(8,128)(2,1)S(1)}, f32[1024,256]{1,0:T(8,128)S(1)}, bf16[1024,2048]{1,0:T(8,128)(2,1)}) custom-call(s32[4]{0:T(128)S(1)} %pad_add_fusion.place, bf16[1024,2048]{1,0:T(8,128)(2,1)S(1)} %get-tuple-element.42.x_hbm, bf16[2048,512]{1,0:T(8,128)(2,1)S(1)} %copy-done, ...), custom_call_target="tpu_custom_call", output_to_operand_aliasing={{2}: (11, {})} | custom-call | flops 2700000000 | bytes 8100000 | tf_op jit(solution)/shard_map/project/pallas_call | solution.py:405
  154.6 2.1 %collective-permute-done.34.refs_5_ = bf16[1024,256]{1,0:T(8,128)(2,1)S(1)} collective-permute-done((bf16[1024,256]{1,0:T(8,128)(2,1)S(1)}, bf16[1024,256]{1,0:T(8,128)(2,1)S(1)}, u32[]{:S(2)}, u32[]{:S(2)}) %collective-permute-start.34) | collective-permute-done | bytes 524320 | tf_op jit(solution)/shard_map/ppermute | solution.py:474
  156.7 6.1 %project.15 = (bf16[1024,256]{1,0:T(8,128)(2,1)S(1)}, f32[1024,256]{1,0:T(8,128)S(1)}, bf16[1024,2048]{1,0:T(8,128)(2,1)}) custom-call(s32[4]{0:T(128)S(1)} %pad_add_fusion.place, bf16[1024,2048]{1,0:T(8,128)(2,1)S(1)} %get-tuple-element.42.x_hbm, bf16[2048,512]{1,0:T(8,128)(2,1)S(1)} %copy-done, ...), custom_call_target="tpu_custom_call", output_to_operand_aliasing={{2}: (10, {})} | custom-call | flops 2700000000 | bytes 8100000 | tf_op jit(solution)/shard_map/project/pallas_call | solution.py:405
  162.8 1.7 collective-permute-start.38
  164.7 4.6 %collective-permute-done.39.refs_5_ = bf16[1024,256]{1,0:T(8,128)(2,1)S(1)} collective-permute-done((bf16[1024,256]{1,0:T(8,128)(2,1)S(1)}, bf16[1024,256]{1,0:T(8,128)(2,1)S(1)}, u32[]{:S(2)}, u32[]{:S(2)}) %collective-permute-start.39) | collective-permute-done | bytes 524320 | tf_op jit(solution)/shard_map/ppermute | solution.py:474
  169.4 5.7 %project.16 = (bf16[1024,256]{1,0:T(8,128)(2,1)S(1)}, f32[1024,256]{1,0:T(8,128)S(1)}, bf16[1024,2048]{1,0:T(8,128)(2,1)}) custom-call(s32[4]{0:T(128)S(1)} %pad_add_fusion.place, bf16[1024,2048]{1,0:T(8,128)(2,1)S(1)} %get-tuple-element.42.x_hbm, bf16[2048,128]{1,0:T(8,128)(2,1)S(1)} %gate.35.refs_0_, ...), custom_call_target="tpu_custom_call", output_to_operand_aliasing={{2}: (11, {})} | custom-call | flops 2700000000 | bytes 8100000 | tf_op jit(solution)/shard_map/project/pallas_call | solution.py:405
  175.6 5.0 %collective-permute-done.38.refs_5_ = bf16[1024,256]{1,0:T(8,128)(2,1)S(1)} collective-permute-done((bf16[1024,256]{1,0:T(8,128)(2,1)S(1)}, bf16[1024,256]{1,0:T(8,128)(2,1)S(1)}, u32[]{:S(2)}, u32[]{:S(2)}) %collective-permute-start.38) | collective-permute-done | bytes 524320 | tf_op jit(solution)/shard_map/ppermute | solution.py:474
  180.6 5.7 %project.17 = (bf16[1024,256]{1,0:T(8,128)(2,1)S(1)}, f32[1024,256]{1,0:T(8,128)S(1)}, bf16[1024,2048]{1,0:T(8,128)(2,1)}) custom-call(s32[4]{0:T(128)S(1)} %pad_add_fusion.place, bf16[1024,2048]{1,0:T(8,128)(2,1)S(1)} %get-tuple-element.42.x_hbm, ...), custom_call_target="tpu_custom_call", output_to_operand_aliasing={{2}: (9, {})} | custom-call | flops 2700000000 | bytes 8100000 | tf_op jit(solution)/shard_map/project/pallas_call | solution.py:405
  186.3 0.6 collective-permute-start.40
  186.8 5.0 %collective-permute-done.41.refs_1_ = bf16[1024,256]{1,0:T(8,128)(2,1)S(1)} collective-permute-done((bf16[1024,256]{1,0:T(8,128)(2,1)S(1)}, bf16[1024,256]{1,0:T(8,128)(2,1)S(1)}, u32[]{:S(2)}, u32[]{:S(2)}) %collective-permute-start.41) | collective-permute-done | bytes 524320 | tf_op jit(solution)/shard_map/ppermute | solution.py:474
  191.8 1.6 combine.2.refs_2_
  193.4 8.9 %collective-permute-done.40.refs_1_ = bf16[1024,256]{1,0:T(8,128)(2,1)S(1)} collective-permute-done((bf16[1024,256]{1,0:T(8,128)(2,1)S(1)}, bf16[1024,256]{1,0:T(8,128)(2,1)S(1)}, u32[]{:S(2)}, u32[]{:S(2)}) %collective-permute-start.40) | collective-permute-done | bytes 524320 | tf_op jit(solution)/shard_map/ppermute | solution.py:474
  202.4 1.6 combine.3
  (97 shorter events, 2.6 us)
Async XLA Ops:
  0.0 41.1 %collective-permute-start.2 = (bf16[2048,512]{1,0:T(8,128)(2,1)}, bf16[2048,512]{1,0:T(8,128)(2,1)}, u32[]{:S(2)}, u32[]{:S(2)}) collective-permute-start(bf16[2048,512]{1,0:T(8,128)(2,1)} %refs_0_.9), channel_id=1, source_target_pairs={{0,1},{1,0},{2,3},{3,2},{4,5},{5,4},{6,7},{7,6},{8,9},{9,8},{10,11... | collective-permute-start | bytes 6291464 | tf_op jit(solution)/shard_map/ppermute | solution.py:470
  2.3 6.5 %copy-start.12 = (bf16[2048,128]{1,0:T(8,128)(2,1)S(1)}, bf16[2048,128]{1,0:T(8,128)(2,1)}, u32[]{:S(2)}) copy-start(bf16[2048,128]{1,0:T(8,128)(2,1)} %get-tuple-element.68.refs_0_) | copy-start | bytes 1572868
  8.3 3.7 %collective-permute-start = (bf16[16,128,128]{2,1,0:T(8,128)(2,1)}, bf16[16,128,128]{2,1,0:T(8,128)(2,1)S(1)}, u32[]{:S(2)}, u32[]{:S(2)}) collective-permute-start(bf16[16,128,128]{2,1,0:T(8,128)(2,1)} %get-tuple-element.36), channel_id=1, source_target_pairs={{0,1},{1,0},{2,3},{3,2},{4,5},{5,4},{6,7},{7,6},{8,9},{9,8},{10,11... | collective-permute-start | bytes 1572872 | tf_op jit(solution)/shard_map/ppermute | solution.py:470
  8.8 19.9 %collective-permute-start.12 = (bf16[2048,128]{1,0:T(8,128)(2,1)S(1)}, bf16[2048,128]{1,0:T(8,128)(2,1)}, u32[]{:S(2)}, u32[]{:S(2)}) collective-permute-start(bf16[2048,128]{1,0:T(8,128)(2,1)S(1)} %copy-done.12), channel_id=1, source_target_pairs={{4,8},{8,4},{5,9},{9,5},{6,10},{10,6},{7,11},{11,7},{20,24},{24,20... | collective-permute-start | bytes 1572872 | tf_op jit(solution)/shard_map/ppermute | solution.py:546
  11.1 21.2 %collective-permute-start.6 = (bf16[2048,128]{1,0:T(8,128)(2,1)S(1)}, bf16[2048,128]{1,0:T(8,128)(2,1)S(1)}, u32[]{:S(2)}, u32[]{:S(2)}) collective-permute-start(bf16[2048,128]{1,0:T(8,128)(2,1)S(1)} %copy-done.12), channel_id=1, source_target_pairs={{0,4},{4,0},{8,12},{12,8},{1,5},{5,1},{9,13},{13,9},{2,6},{6,2},{1... | collective-permute-start | bytes 1572872 | tf_op jit(solution)/shard_map/ppermute | solution.py:546
  13.0 13.9 %collective-permute-start.1 = (bf16[8,128,128]{2,1,0:T(8,128)(2,1)S(1)}, bf16[8,128,128]{2,1,0:T(8,128)(2,1)S(1)}, u32[]{:S(2)}, u32[]{:S(2)}) collective-permute-start(bf16[8,128,128]{2,1,0:T(8,128)(2,1)S(1)} %fusion.refs_0_), channel_id=1, source_target_pairs={{0,4},{1,5},{2,6},{3,7},{16,20},{17,21},{18,22},{19,23}} | collective-permute-start | bytes 786440 | tf_op jit(solution)/shard_map/ppermute | solution.py:529
  13.7 2.2 %copy-start.1 = (bf16[1024,2048]{1,0:T(8,128)(2,1)S(1)}, bf16[1024,2048]{1,0:T(8,128)(2,1)}, u32[]{:S(2)}) copy-start(bf16[1024,2048]{1,0:T(8,128)(2,1)} %q_ref.3) | copy-start | bytes 12582916
  15.9 2.2 %copy-start.10 = (bf16[1024,2048]{1,0:T(8,128)(2,1)S(1)}, bf16[1024,2048]{1,0:T(8,128)(2,1)}, u32[]{:S(2)}) copy-start(bf16[1024,2048]{1,0:T(8,128)(2,1)} %k_hbm.5) | copy-start | bytes 12582916
  18.1 8.9 %copy-start.11 = (f32[16,128,128]{2,1,0:T(8,128)S(1)}, f32[16,128,128]{2,1,0:T(8,128)}, u32[]{:S(2)}) copy-start(f32[16,128,128]{2,1,0:T(8,128)} %get-tuple-element.35) | copy-start | bytes 3145732
  26.9 14.1 %copy-start.7 = (f32[1024,1024]{1,0:T(8,128)}, f32[1024,1024]{1,0:T(8,128)S(1)}, u32[]{:S(2)}) copy-start(f32[1024,1024]{1,0:T(8,128)S(1)} %get-tuple-element.40.a_ref) | copy-start | bytes 12582916
  27.0 14.1 %copy-start.2 = (bf16[1024,2048]{1,0:T(8,128)(2,1)S(1)}, bf16[1024,2048]{1,0:T(8,128)(2,1)}, u32[]{:S(2)}) copy-start(bf16[1024,2048]{1,0:T(8,128)(2,1)} %q_ref.3) | copy-start | bytes 12582916
  27.1 13.1 %collective-permute-start.3 = (bf16[8,128,128]{2,1,0:T(8,128)(2,1)S(1)}, bf16[8,128,128]{2,1,0:T(8,128)(2,1)S(1)}, u32[]{:S(2)}, u32[]{:S(2)}) collective-permute-start(bf16[8,128,128]{2,1,0:T(8,128)(2,1)S(1)} %gate.19.refs_0_), channel_id=1, source_target_pairs={{4,8},{5,9},{6,10},{7,11},{20,24},{21,25},{22,26},{23,27}} | collective-permute-start | bytes 786440 | tf_op jit(solution)/shard_map/ppermute | solution.py:529
  28.7 28.4 %collective-permute-start.13 = (bf16[2048,128]{1,0:T(8,128)(2,1)}, bf16[2048,128]{1,0:T(8,128)(2,1)}, u32[]{:S(2)}, u32[]{:S(2)}) collective-permute-start(bf16[2048,128]{1,0:T(8,128)(2,1)} %gate.27), channel_id=1, source_target_pairs={{4,0},{8,12},{5,1},{9,13},{6,2},{10,14},{7,3},{11,15},{20,16},{24,... | collective-permute-start | bytes 1572872 | tf_op jit(solution)/shard_map/ppermute | solution.py:546
  32.3 23.1 %collective-permute-start.7 = (bf16[2048,128]{1,0:T(8,128)(2,1)S(1)}, bf16[2048,128]{1,0:T(8,128)(2,1)S(1)}, u32[]{:S(2)}, u32[]{:S(2)}) collective-permute-start(bf16[2048,128]{1,0:T(8,128)(2,1)S(1)} %gate.21.refs_0_), channel_id=1, source_target_pairs={{4,8},{8,4},{5,9},{9,5},{6,10},{10,6},{7,11},{11,7},{20,24},{24,20... | collective-permute-start | bytes 1572872 | tf_op jit(solution)/shard_map/ppermute | solution.py:546
  41.1 14.3 %copy-start.4 = (bf16[2048,128]{1,0:T(8,128)(2,1)S(1)}, bf16[2048,128]{1,0:T(8,128)(2,1)}, u32[]{:S(2)}) copy-start(bf16[2048,128]{1,0:T(8,128)(2,1)} %get-tuple-element.67.refs_0_) | copy-start | bytes 1572868
  49.9 2.0 copy-start.5
  51.9 8.0 %collective-permute-start.4 = (bf16[8,128,128]{2,1,0:T(8,128)(2,1)S(1)}, bf16[8,128,128]{2,1,0:T(8,128)(2,1)}, u32[]{:S(2)}, u32[]{:S(2)}) collective-permute-start(bf16[8,128,128]{2,1,0:T(8,128)(2,1)S(1)} %gate.20), channel_id=1, source_target_pairs={{8,12},{9,13},{10,14},{11,15},{24,28},{25,29},{26,30},{27,31}} | collective-permute-start | bytes 786440 | tf_op jit(solution)/shard_map/ppermute | solution.py:529
  53.9 10.8 %collective-permute-start.18 = (bf16[2048,128]{1,0:T(8,128)(2,1)S(1)}, bf16[2048,128]{1,0:T(8,128)(2,1)S(1)}, u32[]{:S(2)}, u32[]{:S(2)}) collective-permute-start(bf16[2048,128]{1,0:T(8,128)(2,1)S(1)} %gate.21.refs_0_), channel_id=1, source_target_pairs={{0,16},{16,0},{1,17},{17,1},{2,18},{18,2},{3,19},{19,3},{4,20},{20... | collective-permute-start | bytes 1572872 | tf_op jit(solution)/shard_map/ppermute | solution.py:470
  55.5 9.3 %copy-start.3 = (bf16[1024,2048]{1,0:T(8,128)(2,1)S(1)}, bf16[1024,2048]{1,0:T(8,128)(2,1)}, u32[]{:S(2)}) copy-start(bf16[1024,2048]{1,0:T(8,128)(2,1)} %q_ref.3) | copy-start | bytes 12582916
  55.5 9.3 %copy-start.8 = (f32[1024,1024]{1,0:T(8,128)S(1)}, f32[1024,1024]{1,0:T(8,128)}, u32[]{:S(2)}) copy-start(f32[1024,1024]{1,0:T(8,128)} %copy-done.7) | copy-start | bytes 12582916
  55.5 9.3 %copy-start.9 = (f32[2048]{0:T(1024)S(1)}, f32[2048]{0:T(1024)}, u32[]{:S(2)}) copy-start(f32[2048]{0:T(1024)} %param.9) | copy-start | bytes 24580
  55.5 18.2 %collective-permute-start.8 = (bf16[2048,128]{1,0:T(8,128)(2,1)S(1)}, bf16[2048,128]{1,0:T(8,128)(2,1)S(1)}, u32[]{:S(2)}, u32[]{:S(2)}) collective-permute-start(bf16[2048,128]{1,0:T(8,128)(2,1)S(1)} %gate.22.refs_1_), channel_id=1, source_target_pairs={{4,0},{8,12},{5,1},{9,13},{6,2},{10,14},{7,3},{11,15},{20,16},{24,... | collective-permute-start | bytes 1572872 | tf_op jit(solution)/shard_map/ppermute | solution.py:546
  61.0 7.5 %collective-permute-start.5 = (bf16[8,128,128]{2,1,0:T(8,128)(2,1)S(1)}, bf16[8,128,128]{2,1,0:T(8,128)(2,1)S(1)}, u32[]{:S(2)}, u32[]{:S(2)}) collective-permute-start(bf16[8,128,128]{2,1,0:T(8,128)(2,1)S(1)} %add.40.p_ref.refs_1_), channel_id=1, source_target_pairs={{0,1},{1,0},{2,3},{3,2},{4,5},{5,4},{6,7},{7,6},{8,9},{9,8},{10,11... | collective-permute-start | bytes 786440 | tf_op jit(solution)/shard_map/ppermute | solution.py:470
  62.2 24.2 %collective-permute-start.20 = (bf16[2048,128]{1,0:T(8,128)(2,1)S(1)}, bf16[2048,128]{1,0:T(8,128)(2,1)S(1)}, u32[]{:S(2)}, u32[]{:S(2)}) collective-permute-start(bf16[2048,128]{1,0:T(8,128)(2,1)S(1)} %broadcast_select_fusion.3.refs_2_), channel_id=1, source_target_pairs={{0,1},{1,0},{2,3},{3,2},{4,5},{5,4},{6,7},{7,6},{8,9},{9,8},{10,11... | collective-permute-start | bytes 1572872 | tf_op jit(solution)/shard_map/ppermute | solution.py:470
  62.8 15.7 %collective-permute-start.10 = (bf16[2048,128]{1,0:T(8,128)(2,1)S(1)}, bf16[2048,128]{1,0:T(8,128)(2,1)S(1)}, u32[]{:S(2)}, u32[]{:S(2)}) collective-permute-start(bf16[2048,128]{1,0:T(8,128)(2,1)S(1)} %gate.25), channel_id=1, source_target_pairs={{4,8},{8,4},{5,9},{9,5},{6,10},{10,6},{7,11},{11,7},{20,24},{24,20... | collective-permute-start | bytes 1572872 | tf_op jit(solution)/shard_map/ppermute | solution.py:546
  64.7 23.3 %collective-permute-start.21 = (bf16[2048,128]{1,0:T(8,128)(2,1)S(1)}, bf16[2048,128]{1,0:T(8,128)(2,1)S(1)}, u32[]{:S(2)}, u32[]{:S(2)}) collective-permute-start(bf16[2048,128]{1,0:T(8,128)(2,1)S(1)} %gate.32.refs_0_), channel_id=1, source_target_pairs={{0,1},{1,0},{2,3},{3,2},{4,5},{5,4},{6,7},{7,6},{8,9},{9,8},{10,11... | collective-permute-start | bytes 1572872 | tf_op jit(solution)/shard_map/ppermute | solution.py:470
  64.8 5.3 %copy-start.6 = (f32[1024,1024]{1,0:T(8,128)S(1)}, f32[1024,1024]{1,0:T(8,128)}, u32[]{:S(2)}) copy-start(f32[1024,1024]{1,0:T(8,128)} %copy-done.5) | copy-start | bytes 12582916
  68.5 14.4 %collective-permute-start.14 = (bf16[2048,128]{1,0:T(8,128)(2,1)S(1)}, bf16[2048,128]{1,0:T(8,128)(2,1)S(1)}, u32[]{:S(2)}, u32[]{:S(2)}) collective-permute-start(bf16[2048,128]{1,0:T(8,128)(2,1)S(1)} %gate.29), channel_id=1, source_target_pairs={{0,16},{16,0},{1,17},{17,1},{2,18},{18,2},{3,19},{19,3},{4,20},{20... | collective-permute-start | bytes 1572872 | tf_op jit(solution)/shard_map/ppermute | solution.py:470
  73.8 14.2 %copy-start = (bf16[2048,512]{1,0:T(8,128)(2,1)S(1)}, bf16[2048,512]{1,0:T(8,128)(2,1)}, u32[]{:S(2)}) copy-start(bf16[2048,512]{1,0:T(8,128)(2,1)} %refs_0_.9) | copy-start | bytes 6291460
  73.8 18.9 %collective-permute-start.9 = (bf16[2048,128]{1,0:T(8,128)(2,1)S(1)}, bf16[2048,128]{1,0:T(8,128)(2,1)S(1)}, u32[]{:S(2)}, u32[]{:S(2)}) collective-permute-start(bf16[2048,128]{1,0:T(8,128)(2,1)S(1)} %gate.24), channel_id=1, source_target_pairs={{0,4},{4,0},{8,12},{12,8},{1,5},{5,1},{9,13},{13,9},{2,6},{6,2},{1... | collective-permute-start | bytes 1572872 | tf_op jit(solution)/shard_map/ppermute | solution.py:546
  78.5 14.8 %collective-permute-start.17 = (bf16[2048,128]{1,0:T(8,128)(2,1)S(1)}, bf16[2048,128]{1,0:T(8,128)(2,1)S(1)}, u32[]{:S(2)}, u32[]{:S(2)}) collective-permute-start(bf16[2048,128]{1,0:T(8,128)(2,1)S(1)} %broadcast_select_fusion.2.refs_2_), channel_id=1, source_target_pairs={{0,1},{1,0},{2,3},{3,2},{4,5},{5,4},{6,7},{7,6},{8,9},{9,8},{10,11... | collective-permute-start | bytes 1572872 | tf_op jit(solution)/shard_map/ppermute | solution.py:470
  82.8 15.2 %collective-permute-start.11 = (bf16[2048,128]{1,0:T(8,128)(2,1)S(1)}, bf16[2048,128]{1,0:T(8,128)(2,1)S(1)}, u32[]{:S(2)}, u32[]{:S(2)}) collective-permute-start(bf16[2048,128]{1,0:T(8,128)(2,1)S(1)} %gate.26), channel_id=1, source_target_pairs={{4,0},{8,12},{5,1},{9,13},{6,2},{10,14},{7,3},{11,15},{20,16},{24,... | collective-permute-start | bytes 1572872 | tf_op jit(solution)/shard_map/ppermute | solution.py:546
  86.3 13.3 %collective-permute-start.16 = (bf16[2048,128]{1,0:T(8,128)(2,1)S(1)}, bf16[2048,128]{1,0:T(8,128)(2,1)S(1)}, u32[]{:S(2)}, u32[]{:S(2)}) collective-permute-start(bf16[2048,128]{1,0:T(8,128)(2,1)S(1)} %gate.30), channel_id=1, source_target_pairs={{0,16},{16,0},{1,17},{17,1},{2,18},{18,2},{3,19},{19,3},{4,20},{20... | collective-permute-start | bytes 1572872 | tf_op jit(solution)/shard_map/ppermute | solution.py:470
  88.0 11.6 %collective-permute-start.15 = (bf16[2048,128]{1,0:T(8,128)(2,1)S(1)}, bf16[2048,128]{1,0:T(8,128)(2,1)S(1)}, u32[]{:S(2)}, u32[]{:S(2)}) collective-permute-start(bf16[2048,128]{1,0:T(8,128)(2,1)S(1)} %collective-permute-done.14.refs_1_.refs_2_), channel_id=1, source_target_pairs={{0,1},{1,0},{2,3},{3,2},{4,5},{5,4},{6,7},{7,6},{8,9},{9,8},{10,11... | collective-permute-start | bytes 1572872 | tf_op jit(solution)/shard_map/ppermute | solution.py:470
  92.7 6.9 %collective-permute-start.19 = (bf16[2048,128]{1,0:T(8,128)(2,1)S(1)}, bf16[2048,128]{1,0:T(8,128)(2,1)S(1)}, u32[]{:S(2)}, u32[]{:S(2)}) collective-permute-start(bf16[2048,128]{1,0:T(8,128)(2,1)S(1)} %gate.31.refs_0_), channel_id=1, source_target_pairs={{0,1},{1,0},{2,3},{3,2},{4,5},{5,4},{6,7},{7,6},{8,9},{9,8},{10,11... | collective-permute-start | bytes 1572872 | tf_op jit(solution)/shard_map/ppermute | solution.py:470
  93.3 16.3 %collective-permute-start.33 = (bf16[1024,256]{1,0:T(8,128)(2,1)S(1)}, bf16[1024,256]{1,0:T(8,128)(2,1)S(1)}, u32[]{:S(2)}, u32[]{:S(2)}) collective-permute-start(bf16[1024,256]{1,0:T(8,128)(2,1)S(1)} %project.9.refs_9_.refs_1_), channel_id=1, source_target_pairs={{0,2},{2,0},{1,3},{3,1},{4,6},{6,4},{5,7},{7,5},{8,10},{10,8},{9,1... | collective-permute-start | bytes 1572872 | tf_op jit(solution)/shard_map/ppermute | solution.py:474
  105.7 14.2 %collective-permute-start.25 = (bf16[2048,128]{1,0:T(8,128)(2,1)S(1)}, bf16[2048,128]{1,0:T(8,128)(2,1)S(1)}, u32[]{:S(2)}, u32[]{:S(2)}) collective-permute-start(bf16[2048,128]{1,0:T(8,128)(2,1)S(1)} %gate.35.refs_0_), channel_id=1, source_target_pairs={{4,8},{8,4},{5,9},{9,5},{6,10},{10,6},{7,11},{11,7},{20,24},{24,20... | collective-permute-start | bytes 1572872 | tf_op jit(solution)/shard_map/ppermute | solution.py:546
  107.6 17.7 %collective-permute-start.30 = (bf16[2048,128]{1,0:T(8,128)(2,1)S(1)}, bf16[2048,128]{1,0:T(8,128)(2,1)S(1)}, u32[]{:S(2)}, u32[]{:S(2)}) collective-permute-start(bf16[2048,128]{1,0:T(8,128)(2,1)S(1)} %gate.37.refs_2_), channel_id=1, source_target_pairs={{0,1},{1,0},{2,3},{3,2},{4,5},{5,4},{6,7},{7,6},{8,9},{9,8},{10,11... | collective-permute-start | bytes 1572872 | tf_op jit(solution)/shard_map/ppermute | solution.py:470
  107.8 23.3 %collective-permute-start.22 = (bf16[2048,128]{1,0:T(8,128)(2,1)S(1)}, bf16[2048,128]{1,0:T(8,128)(2,1)S(1)}, u32[]{:S(2)}, u32[]{:S(2)}) collective-permute-start(bf16[2048,128]{1,0:T(8,128)(2,1)S(1)} %broadcast_select_fusion.1.refs_2_), channel_id=1, source_target_pairs={{0,16},{16,0},{1,17},{17,1},{2,18},{18,2},{3,19},{19,3},{4,20},{20... | collective-permute-start | bytes 1572872 | tf_op jit(solution)/shard_map/ppermute | solution.py:470
  109.4 23.2 %collective-permute-start.32 = (bf16[2048,128]{1,0:T(8,128)(2,1)S(1)}, bf16[2048,128]{1,0:T(8,128)(2,1)S(1)}, u32[]{:S(2)}, u32[]{:S(2)}) collective-permute-start(bf16[2048,128]{1,0:T(8,128)(2,1)S(1)} %gate.35.refs_0_), channel_id=1, source_target_pairs={{0,1},{1,0},{2,3},{3,2},{4,5},{5,4},{6,7},{7,6},{8,9},{9,8},{10,11... | collective-permute-start | bytes 1572872 | tf_op jit(solution)/shard_map/ppermute | solution.py:470
  109.6 24.6 %collective-permute-start.31 = (bf16[1024,256]{1,0:T(8,128)(2,1)S(1)}, bf16[1024,256]{1,0:T(8,128)(2,1)S(1)}, u32[]{:S(2)}, u32[]{:S(2)}) collective-permute-start(bf16[1024,256]{1,0:T(8,128)(2,1)S(1)} %get-tuple-element.45.refs_1_.refs_4_.refs_7_), channel_id=1, source_target_pairs={{0,2},{2,0},{1,3},{3,1},{4,6},{6,4},{5,7},{7,5},{8,10},{10,8},{9,1... | collective-permute-start | bytes 1572872 | tf_op jit(solution)/shard_map/ppermute | solution.py:474
  119.9 20.6 %collective-permute-start.26 = (bf16[2048,128]{1,0:T(8,128)(2,1)S(1)}, bf16[2048,128]{1,0:T(8,128)(2,1)S(1)}, u32[]{:S(2)}, u32[]{:S(2)}) collective-permute-start(bf16[2048,128]{1,0:T(8,128)(2,1)S(1)} %collective-permute-done.25.refs_7_), channel_id=1, source_target_pairs={{4,0},{8,12},{5,1},{9,13},{6,2},{10,14},{7,3},{11,15},{20,16},{24,... | collective-permute-start | bytes 1572872 | tf_op jit(solution)/shard_map/ppermute | solution.py:546
  125.3 21.5 %collective-permute-start.36 = (bf16[2048,128]{1,0:T(8,128)(2,1)S(1)}, bf16[2048,128]{1,0:T(8,128)(2,1)S(1)}, u32[]{:S(2)}, u32[]{:S(2)}) collective-permute-start(bf16[2048,128]{1,0:T(8,128)(2,1)S(1)} %broadcast_select_fusion.1.refs_2_), channel_id=1, source_target_pairs={{0,1},{1,0},{2,3},{3,2},{4,5},{5,4},{6,7},{7,6},{8,9},{9,8},{10,11... | collective-permute-start | bytes 1572872 | tf_op jit(solution)/shard_map/ppermute | solution.py:470
  131.1 17.3 %collective-permute-start.37 = (bf16[1024,256]{1,0:T(8,128)(2,1)S(1)}, bf16[1024,256]{1,0:T(8,128)(2,1)S(1)}, u32[]{:S(2)}, u32[]{:S(2)}) collective-permute-start(bf16[1024,256]{1,0:T(8,128)(2,1)S(1)} %get-tuple-element.47.refs_9_), channel_id=1, source_target_pairs={{0,2},{2,0},{1,3},{3,1},{4,6},{6,4},{5,7},{7,5},{8,10},{10,8},{9,1... | collective-permute-start | bytes 1572872 | tf_op jit(solution)/shard_map/ppermute | solution.py:474
  132.7 14.0 %collective-permute-start.23 = (bf16[2048,128]{1,0:T(8,128)(2,1)S(1)}, bf16[2048,128]{1,0:T(8,128)(2,1)S(1)}, u32[]{:S(2)}, u32[]{:S(2)}) collective-permute-start(bf16[2048,128]{1,0:T(8,128)(2,1)S(1)} %gate.34), channel_id=1, source_target_pairs={{0,16},{16,0},{1,17},{17,1},{2,18},{18,2},{3,19},{19,3},{4,20},{20... | collective-permute-start | bytes 1572872 | tf_op jit(solution)/shard_map/ppermute | solution.py:470
  139.9 16.8 %collective-permute-start.34 = (bf16[1024,256]{1,0:T(8,128)(2,1)S(1)}, bf16[1024,256]{1,0:T(8,128)(2,1)S(1)}, u32[]{:S(2)}, u32[]{:S(2)}) collective-permute-start(bf16[1024,256]{1,0:T(8,128)(2,1)S(1)} %get-tuple-element.50.refs_8_), channel_id=1, source_target_pairs={{0,2},{2,0},{1,3},{3,1},{4,6},{6,4},{5,7},{7,5},{8,10},{10,8},{9,1... | collective-permute-start | bytes 1572872 | tf_op jit(solution)/shard_map/ppermute | solution.py:474
  140.5 16.2 %collective-permute-start.29 = (bf16[2048,128]{1,0:T(8,128)(2,1)S(1)}, bf16[2048,128]{1,0:T(8,128)(2,1)S(1)}, u32[]{:S(2)}, u32[]{:S(2)}) collective-permute-start(bf16[2048,128]{1,0:T(8,128)(2,1)S(1)} %collective-permute-done.22.refs_1_.refs_6_.refs_2_), channel_id=1, source_target_pairs={{0,1},{1,0},{2,3},{3,2},{4,5},{5,4},{6,7},{7,6},{8,9},{9,8},{10,11... | collective-permute-start | bytes 1572872 | tf_op jit(solution)/shard_map/ppermute | solution.py:470
  146.7 10.0 %collective-permute-start.35 = (bf16[2048,128]{1,0:T(8,128)(2,1)S(1)}, bf16[2048,128]{1,0:T(8,128)(2,1)S(1)}, u32[]{:S(2)}, u32[]{:S(2)}) collective-permute-start(bf16[2048,128]{1,0:T(8,128)(2,1)S(1)} %broadcast_select_fusion.refs_2_), channel_id=1, source_target_pairs={{0,1},{1,0},{2,3},{3,2},{4,5},{5,4},{6,7},{7,6},{8,9},{9,8},{10,11... | collective-permute-start | bytes 1572872 | tf_op jit(solution)/shard_map/ppermute | solution.py:470
  146.8 17.8 %collective-permute-start.27 = (bf16[2048,128]{1,0:T(8,128)(2,1)S(1)}, bf16[2048,128]{1,0:T(8,128)(2,1)S(1)}, u32[]{:S(2)}, u32[]{:S(2)}) collective-permute-start(bf16[2048,128]{1,0:T(8,128)(2,1)S(1)} %gate.36), channel_id=1, source_target_pairs={{0,16},{16,0},{1,17},{17,1},{2,18},{18,2},{3,19},{19,3},{4,20},{20... | collective-permute-start | bytes 1572872 | tf_op jit(solution)/shard_map/ppermute | solution.py:470
  154.5 14.8 %collective-permute-start.39 = (bf16[1024,256]{1,0:T(8,128)(2,1)S(1)}, bf16[1024,256]{1,0:T(8,128)(2,1)S(1)}, u32[]{:S(2)}, u32[]{:S(2)}) collective-permute-start(bf16[1024,256]{1,0:T(8,128)(2,1)S(1)} %get-tuple-element.53.refs_7_), channel_id=1, source_target_pairs={{0,2},{2,0},{1,3},{3,1},{4,6},{6,4},{5,7},{7,5},{8,10},{10,8},{9,1... | collective-permute-start | bytes 1572872 | tf_op jit(solution)/shard_map/ppermute | solution.py:474
  156.7 12.7 %collective-permute-start.24 = (bf16[2048,128]{1,0:T(8,128)(2,1)S(1)}, bf16[2048,128]{1,0:T(8,128)(2,1)S(1)}, u32[]{:S(2)}, u32[]{:S(2)}) collective-permute-start(bf16[2048,128]{1,0:T(8,128)(2,1)S(1)} %collective-permute-done.23.refs_1_.refs_7_.refs_0_), channel_id=1, source_target_pairs={{0,1},{1,0},{2,3},{3,2},{4,5},{5,4},{6,7},{7,6},{8,9},{9,8},{10,11... | collective-permute-start | bytes 1572872 | tf_op jit(solution)/shard_map/ppermute | solution.py:470
  162.8 17.7 %collective-permute-start.38 = (bf16[1024,256]{1,0:T(8,128)(2,1)S(1)}, bf16[1024,256]{1,0:T(8,128)(2,1)S(1)}, u32[]{:S(2)}, u32[]{:S(2)}) collective-permute-start(bf16[1024,256]{1,0:T(8,128)(2,1)S(1)} %get-tuple-element.56.refs_8_), channel_id=1, source_target_pairs={{0,2},{2,0},{1,3},{3,1},{4,6},{6,4},{5,7},{7,5},{8,10},{10,8},{9,1... | collective-permute-start | bytes 1572872 | tf_op jit(solution)/shard_map/ppermute | solution.py:474
  164.5 16.1 %collective-permute-start.28 = (bf16[2048,128]{1,0:T(8,128)(2,1)S(1)}, bf16[2048,128]{1,0:T(8,128)(2,1)S(1)}, u32[]{:S(2)}, u32[]{:S(2)}) collective-permute-start(bf16[2048,128]{1,0:T(8,128)(2,1)S(1)} %collective-permute-done.27.refs_6_.refs_2_), channel_id=1, source_target_pairs={{0,1},{1,0},{2,3},{3,2},{4,5},{5,4},{6,7},{7,6},{8,9},{9,8},{10,11... | collective-permute-start | bytes 1572872 | tf_op jit(solution)/shard_map/ppermute | solution.py:470
  175.1 16.8 %collective-permute-start.41 = (bf16[1024,256]{1,0:T(8,128)(2,1)S(1)}, bf16[1024,256]{1,0:T(8,128)(2,1)S(1)}, u32[]{:S(2)}, u32[]{:S(2)}) collective-permute-start(bf16[1024,256]{1,0:T(8,128)(2,1)S(1)} %get-tuple-element.59.refs_6_), channel_id=1, source_target_pairs={{0,2},{2,0},{1,3},{3,1},{4,6},{6,4},{5,7},{7,5},{8,10},{10,8},{9,1... | collective-permute-start | bytes 1572872 | tf_op jit(solution)/shard_map/ppermute | solution.py:474
  186.3 16.1 %collective-permute-start.40 = (bf16[1024,256]{1,0:T(8,128)(2,1)S(1)}, bf16[1024,256]{1,0:T(8,128)(2,1)S(1)}, u32[]{:S(2)}, u32[]{:S(2)}) collective-permute-start(bf16[1024,256]{1,0:T(8,128)(2,1)S(1)} %get-tuple-element.62), channel_id=1, source_target_pairs={{0,2},{2,0},{1,3},{3,1},{4,6},{6,4},{5,7},{7,5},{8,10},{10,8},{9,1... | collective-permute-start | bytes 1572872 | tf_op jit(solution)/shard_map/ppermute | solution.py:474

commit v3 on v2

--- a/solution.py
+++ b/solution.py
@@ -162,7 +162,7 @@
             jax.ShapeDtypeStruct((rows, part * DH), F32),
             jax.ShapeDtypeStruct((8, LANES), F32),
         ],
-        compiler_params=params(40),
+        compiler_params=params(46),
         cost_estimate=cost(4.4),
         name="intra_block",
     )(place, queries, keys, values, *deps)
@@ -304,7 +304,7 @@
     return middle, last
 
 
-def project_kernel(plan, step, which, kinds, before, n_deps, place, x_hbm, *refs):
+def project_kernel(plan, step, which, kinds, before, n_deps, place, x, *refs):
     n_head, n_sub = plan.n_head, plan.n_sub
     refs = list(refs)
 
@@ -322,10 +322,10 @@
     res_hbm = take(len(which))
     if before is not None:
         out_hbm = take(1)[0]
-    x, w, keep, send, old_keep, old_recv, total, x_sem, w_sem, res_sem, old_sem = refs
+    w, keep, send, old_keep, old_recv, total, w_sem, res_sem, old_sem = refs
     rows = x.shape[0]
     tiles = [slice(j * step[3] * LANES, (j + 1) * step[3] * LANES) for j in range(n_sub)]
-    tile = 256 if rows % 256 == 0 else rows
+    tile = 512 if rows % 512 == 0 else rows
     own = plan.own(place)
     loads = []
     for i in range(n_head * n_sub):
@@ -338,13 +338,7 @@
         dst = w.at[i // n_sub, :, tiles[i % n_sub]]
         loads.append(pltpu.make_async_copy(src, dst, w_sem.at[i]))
     parts = [slice(at, at + tile) for at in range(0, rows, tile)]
-    rows_in = [
-        pltpu.make_async_copy(x_hbm.at[p], x.at[p], x_sem.at[i]) for i, p in enumerate(parts)
-    ]
-    rows_in[0].start()
     for copy in loads:
-        copy.start()
-    for copy in rows_in[1:]:
         copy.start()
     if before is not None:
         stage = (old_keep, old_recv, total)
@@ -357,9 +351,7 @@
         for j in range(n_sub):
             dst = w.at[slot, :, tiles[j]]
             pltpu.make_async_copy(dst, dst, w_sem.at[slot * n_sub + j]).wait()
-        for i, p in enumerate(parts):
-            if n == 0:
-                rows_in[i].wait()
+        for p in parts:
             res = dot(x[p], w[slot])
             if o == 0:
                 keep[p] = res
@@ -399,34 +391,31 @@
         if out is not None:
             operands.append(out)
             aliases = {len(operands): len(shapes) - 1}
-    tiles = rows // 256 if rows % 256 == 0 else 1
     old = width if before is None else n_sub * before[0][3] * LANES
     dma = pltpu.SemaphoreType.DMA
     return pl.pallas_call(
         functools.partial(project_kernel, plan, step, which, kinds, info, len(deps)),
-        grid_spec=pltpu.PrefetchScalarGridSpec(
-            num_scalar_prefetch=1,
-            grid=(1,),
-            in_specs=[ANY] * len(operands),
-            out_specs=[ANY] * len(shapes),
-            scratch_shapes=[
-                pltpu.VMEM((rows, depth), BF16),
-                pltpu.VMEM((n_head, depth, width), BF16),
-                pltpu.VMEM((rows, width), F32),
-                pltpu.VMEM((max(1, n_head - 1), rows, width), BF16),
-                pltpu.VMEM((rows, old), F32),
-                pltpu.VMEM((max(1, n_head - 1), rows, old), BF16),
-                pltpu.VMEM((rows, old), BF16),
-                dma((tiles,)),
-                dma((n_head * n_sub,)),
-                dma((n_head,)),
-                dma((n_head + n_sub,)),
-            ],
-        ),
+        in_specs=[
+            pl.BlockSpec(memory_space=pltpu.SMEM),
+            pl.BlockSpec(memory_space=pltpu.VMEM),
+            *[ANY] * (len(operands) - 1),
+        ],
+        out_specs=[ANY] * len(shapes),
+        scratch_shapes=[
+            pltpu.VMEM((n_head, depth, width), BF16),
+            pltpu.VMEM((rows, width), F32),
+            pltpu.VMEM((max(1, n_head - 1), rows, width), BF16),
+            pltpu.VMEM((rows, old), F32),
+            pltpu.VMEM((max(1, n_head - 1), rows, old), BF16),
+            pltpu.VMEM((rows, old), BF16),
+            dma((n_head * n_sub,)),
+            dma((n_head,)),
+            dma((n_head + n_sub,)),
+        ],
         out_shape=shapes,
         input_output_aliases=aliases,
         compiler_params=params(32),
-        cost_estimate=cost(2.7),
+        cost_estimate=cost(4),
         name="project",
     )(place, *operands)
 
@@ -489,11 +478,11 @@
 
     whole = [out_weight] + [shift(out_weight, "sub", n_sub, j) for j in range(1, n_sub)]
 
-    def cut(r, count):
-        at = plan.mine(place, (r, 0, 0, count)) * LANES
-        return lax.dynamic_slice(out_weight, (0, at), (depth, count * LANES))
-
-    first = [cut(r, 1) for r in range(rounds)]
+    def cut(r, where):
+        at = plan.mine(where, (r, 0, 0, 1)) * LANES
+        return lax.dynamic_slice(out_weight, (0, at), (depth, LANES))
+
+    first = [cut(0, place)]
     pieces = {(r, 0, o, 1, 0): whole for r in range(rounds) for o in range(split)}
     later = {}
     held = {step: [] for step in steps}
@@ -514,19 +503,18 @@
     prefix = jnp.zeros((part, DH, DH), BF16)
     n_band = 1
     bands = [(o, b) for o in range(n_sub) for b in range(n_band)]
-    intra, tokens, hops = {}, [], []
+    intra, tokens = {}, []
     for i in range(n_ctx - 1):
         hop = (prefix.astype(F32) + total).astype(BF16)
-        if i:
-            hop = gate(hop, *tokens[i - 1 : i])
-        hops.append(hop)
         if i < len(bands):
             deps = [hop] if i == 0 else [hop, *whole[1:]]
             intra[bands[i]], token = intra_block(
                 place, *bands[i], n_sub, n_band, queries, keys, values, part, *deps
             )
             tokens.append(token)
-        prefix = prefix + lax.ppermute(hop, "ctx", [(i, i + 1)])
+        moved = lax.ppermute(hop, "ctx", [(i, i + 1)])
+        prefix = prefix + (gate(moved, tokens[i]) if i < len(tokens) else moved)
+    first += [cut(r, gate(place, tokens[0])) for r in range(1, rounds)]
     gain = norm_gain.reshape(heads, 1, DH)
 
     normed, normed_token = None, None
@@ -553,46 +541,46 @@
         y_near_a = over(near_a)
         outward_a = gate(along(across_a, out_way), tokens[1])
         across_b = gate(along(near_a, middle), tokens[1])
-        outward_b = gate(along(across_b, out_way), normed_token)
+        outward_b = along(across_b, out_way, prefix)
         far_a = jnp.where(inner, across_a, outward_a)
         far_b = jnp.where(inner, across_b, outward_b)
-        across_c = along(first[1], middle, across_b)
         y_far_a = over(far_a, prefix)
-        y_far_b = over(far_b, y_far_a, token)
-        near_c = along(first[1], ends, outward_b)
-        outward_c = along(across_c, out_way, normed_token)
         pieces[0, 0, 0, 1, 1] = cross(far_a)
         pieces[0, 0, 1, 1, 1] = cross(y_far_a)
-        pieces[0, 1, 0, 1, 0] = cross(gate(near_a, prefix))
-        pieces[0, 1, 0, 1, 1] = cross(far_b)
-        pieces[0, 1, 1, 1, 0] = cross(gate(y_near_a, normed_token))
-        hold(0, y_near_a, across_c, *pieces[0, 1, 0, 1, 0][1:])
-        hold(1, near_c, outward_c, y_far_b, *pieces[0, 1, 0, 1, 1][1:], *pieces[0, 1, 1, 1, 0][1:])
+        hold(1, y_near_a, outward_b)
 
         def after_0(*sent):
-            pieces[0, 1, 1, 1, 1] = cross(gate(y_far_b, *sent))
-            hold(2, *pieces[0, 1, 1, 1, 1][1:])
+            later["across_c"] = along(first[1], middle, *sent)
+            later["near_c"] = along(first[1], ends, *sent)
+            later["y_far_b"] = over(gate(far_b, *sent))
+            pieces[0, 1, 0, 1, 0] = cross(gate(near_a, *sent))
+            pieces[0, 1, 0, 1, 1] = cross(gate(far_b, *sent))
+            hold(2, later["across_c"], later["near_c"], later["y_far_b"])
 
         def after_1(*sent):
-            far_c = jnp.where(inner, across_c, gate(outward_c, *sent))
+            later["outward_c"] = along(later["across_c"], out_way, *sent)
+            later["across_d"] = along(later["near_c"], middle, *sent)
+            later["y_near_c"] = over(later["near_c"], later["y_far_b"])
+            pieces[0, 1, 1, 1, 0] = cross(gate(y_near_a, *sent))
+            pieces[0, 1, 1, 1, 1] = cross(later["y_far_b"])
+            hold(3, later["outward_c"], later["across_d"], later["y_near_c"])
+
+        def after_2(*sent):
+            far_c = jnp.where(inner, later["across_c"], later["outward_c"])
             pieces[1, 0, 0, 1, 1] = cross(far_c)
-            later["y_far_c"] = over(far_c)
-            later["across_d"] = along(near_c, middle, *sent)
-            pieces[1, 1, 0, 1, 0] = cross(gate(near_c, *sent))
-            hold(3, later["y_far_c"], later["across_d"], *pieces[1, 1, 0, 1, 0][1:])
-
-        def after_2(*sent):
+            later["y_far_c"] = over(far_c, later["y_near_c"])
             outward_d = along(later["across_d"], out_way)
-            later["y_near_c"] = over(near_c, later["y_far_c"])
             far_d = jnp.where(inner, later["across_d"], outward_d)
             pieces[1, 0, 1, 1, 1] = cross(later["y_far_c"])
+            y_far_d = over(far_d, later["y_far_c"])
+            hold(4, later["y_far_c"], outward_d)
+            pieces[1, 1, 0, 1, 0] = cross(gate(later["near_c"], *sent))
             pieces[1, 1, 0, 1, 1] = cross(far_d)
-            y_far_d = over(far_d, later["y_near_c"])
-            hold(4, outward_d, later["y_near_c"])
-            pieces[1, 1, 1, 1, 0] = cross(later["y_near_c"])
+            pieces[1, 1, 1, 1, 0] = cross(gate(later["y_near_c"], *sent))
             pieces[1, 1, 1, 1, 1] = cross(y_far_d)
-            hold(5, *pieces[1, 1, 0, 1, 1][1:])
-            hold(6, y_far_d, *pieces[1, 1, 1, 1, 0][1:])
+            hold(4, *pieces[1, 1, 0, 1, 0][1:])
+            hold(5, *pieces[1, 1, 0, 1, 1][1:], *pieces[1, 1, 1, 1, 0][1:])
+            hold(6, y_far_d)
 
         later = {0: after_0, 1: after_1, 2: after_2}
     else:

time: 205 us -> 189 us (0.922); the launches traced: 204 us -> 186 us
  Pallas kernels: 83.8 us -> 69.2 us
  waiting for transfers between devices: 58.6 us -> 72.6 us
  starting transfers between devices: 47.4 us -> 35.2 us
  local copies, waits for them, and re-layouts: 8.89 us -> 4.24 us
    ppermute x8, waiting for transfers between devices: 25.6 us -> 41.8 us  [swap(): return lax.ppermute(x, axis, [(i, i ^ k) for i in range(size)])]
    pallas_call x9, Pallas kernels: 49.8 us -> 34.2 us  [project(): pl.pallas_call(functools.partial(project_kernel, plan, step, which, kinds...]
    ppermute x21, waiting for transfers between devices: 12.1 us -> 6.44 us  [shift(): return lax.ppermute(x, axis, [(i, (i + o) % size) for i in range(size)])]
    unnamed x32 -> x22, local copies, waits for them, and re-layouts: 6.64 us -> 2.29 us
    ppermute x21, starting transfers between devices: 12.1 us -> 8.13 us  [shift(): return lax.ppermute(x, axis, [(i, (i + o) % size) for i in range(size)])]
    ppermute x10, starting transfers between devices: 23.4 us -> 19.6 us  [along(): return lax.ppermute(gate(x, *deps) if deps else x, 'ctx', perm)]
    ppermute x8, starting transfers between devices: 7.69 us -> 3.99 us  [swap(): return lax.ppermute(x, axis, [(i, i ^ k) for i in range(size)])]
    ppermute x10, waiting for transfers between devices: 15.4 us -> 18.3 us  [along(): return lax.ppermute(gate(x, *deps) if deps else x, 'ctx', perm)]
  transfers between devices with their start and end apart: 42 -> 42, of which waited for: 13 -> 17; matrix products, arithmetic and copies ran while one was open for 3% -> 3% of each run, Pallas kernels for 40% -> 36%
where the time goes in v3:
time: 189 us; the launch traced here: 186 us
  waiting for transfers between devices  72.6 us (38%)
  Pallas kernels  69.2 us (37%)
  starting transfers between devices  35.2 us (19%)
  local copies, waits for them, and re-layouts  4.24 us (2%)
  other arithmetic  3.48 us (2%)
    ppermute x8, waiting for transfers between devices, swap(): return lax.ppermute(x, axis, [(i, i ^ k) for i in range(size)])  41.8 us
    pallas_call x9, Pallas kernels, project(): pl.pallas_call(functools.partial(project_kernel, plan, step, which, kinds...  34.2 us
    ppermute x10, starting transfers between devices, along(): return lax.ppermute(gate(x, *deps) if deps else x, 'ctx', perm)  19.6 us
    ppermute x10, waiting for transfers between devices, along(): return lax.ppermute(gate(x, *deps) if deps else x, 'ctx', perm)  18.3 us
    pallas_call x2, Pallas kernels, intra_block(): pl.pallas_call(functools.partial(intra_kernel, size, chunk, steps, first)...  17.4 us
    pallas_call x2, Pallas kernels, norm_part(): pl.pallas_call(functools.partial(norm_kernel, per, size, n_sub, o), grid_...  8.37 us
    ppermute x21, starting transfers between devices, shift(): return lax.ppermute(x, axis, [(i, (i + o) % size) for i in range(size)])  8.13 us
    ppermute x21, waiting for transfers between devices, shift(): return lax.ppermute(x, axis, [(i, (i + o) % size) for i in range(size)])  6.44 us
  transfers between devices with their start and end apart: 42, of which 17 were waited for; matrix products, arithmetic and copies ran while one was open for 3% of the time, Pallas kernels for 36%

profile of v3, /device:TPU:16, one launch (start us, length us, event | category | flops | bytes accessed | tf_op | source)
XLA Modules:
  0.0 185.6 jit_solution(5105689700711409545)
XLA Ops:
  0.0 1.9 %constant_dynamic-slice_fusion.1.refs_0_ = bf16[2048,128]{1,0:T(8,128)(2,1)} fusion(bf16[2048,512]{1,0:T(8,128)(2,1)} %refs_0_.9, s32[]{:T(128)S(6)} %select_n.30), kind=kLoop, calls=%fused_computation.9 | loop fusion | bytes 1048580 | tf_op jit(solution)/shard_map/dynamic_slice | solution.py:483
  1.9 6.0 %block_states.1 = (f32[16,128,128]{2,1,0:T(8,128)}, bf16[16,128,128]{2,1,0:T(8,128)(2,1)}) custom-call(bf16[1024,2048]{1,0:T(8,128)(2,1)} %k_hbm.5, bf16[1024,2048]{1,0:T(8,128)(2,1)} %v_hbm.5, bf16[2048,128]{1,0:T(8,128)(2,1)} %constant_dynamic-slice_fusion.1.refs_0_), custom_call_target="tpu_custom_call" | custom-call | flops 999999995904 | bytes 3000000000 | tf_op jit(solution)/shard_map/block_states/pallas_call | solution.py:100
  7.9 0.5 collective-permute-start
  8.4 2.3 %collective-permute-start.6 = (bf16[2048,128]{1,0:T(8,128)(2,1)S(1)}, bf16[2048,128]{1,0:T(8,128)(2,1)S(1)}, u32[]{:S(2)}, u32[]{:S(2)}) collective-permute-start(bf16[2048,128]{1,0:T(8,128)(2,1)S(1)} %copy-done.6), channel_id=1, source_target_pairs={{4,8},{8,4},{5,9},{9,5},{6,10},{10,6},{7,11},{11,7},{20,24},{24,20... | collective-permute-start | bytes 1572872 | tf_op jit(solution)/shard_map/ppermute | solution.py:534
  10.8 0.1 pad_add_fusion.place
  10.9 1.8 fusion.refs_0_
  12.7 0.7 collective-permute-start.1
  13.4 8.7 %intra_block.2 = (f32[1024,1024]{1,0:T(8,128)S(1)}, f32[8,128]{1,0:T(8,128)S(1)}) custom-call(s32[4]{0:T(128)S(1)} %pad_add_fusion.place, bf16[1024,2048]{1,0:T(8,128)(2,1)} %q_ref.3, bf16[1024,2048]{1,0:T(8,128)(2,1)} %k_hbm.5, bf16[1024,2048]{1,0:T(8,128)(2,1)} %v_hbm.5, bf16[8,128,128]{2,1,0:T(8,128)(2,1)} %fusion.refs_0_), custom_call_target="tpu_custom_call" | custom-call | flops 4400000000 | bytes 13200000 | tf_op jit(solution)/shard_map/intra_block/pallas_call | solution.py:153
  22.1 2.0 %copy-done.2 = f32[1024,1024]{1,0:T(8,128)} copy-done((f32[1024,1024]{1,0:T(8,128)}, f32[1024,1024]{1,0:T(8,128)S(1)}, u32[]{:S(2)}) %copy-start.2) | copy-done | bytes 4194328
  24.1 0.3 collective-permute-done.10.refs_0_
  24.4 4.8 %collective-permute-start.11 = (bf16[2048,128]{1,0:T(8,128)(2,1)S(1)}, bf16[2048,128]{1,0:T(8,128)(2,1)S(1)}, u32[]{:S(2)}, u32[]{:S(2)}) collective-permute-start(bf16[2048,128]{1,0:T(8,128)(2,1)S(1)} %gate.26.refs_0_), channel_id=1, source_target_pairs={{4,8},{8,4},{5,9},{9,5},{6,10},{10,6},{7,11},{11,7},{20,24},{24,20... | collective-permute-start | bytes 1572872 | tf_op jit(solution)/shard_map/ppermute | solution.py:534
  29.1 1.6 collective-permute-start.19
  30.8 1.3 collective-permute-start.7
  32.1 1.2 add_convert_fusion.1.refs_0_
  33.3 1.4 collective-permute-start.3
  34.8 8.7 %intra_block.3 = (f32[1024,1024]{1,0:T(8,128)S(1)}, f32[8,128]{1,0:T(8,128)S(1)}) custom-call(s32[4]{0:T(128)S(1)} %pad_add_fusion.place, bf16[1024,2048]{1,0:T(8,128)(2,1)} %q_ref.3, bf16[1024,2048]{1,0:T(8,128)(2,1)} %k_hbm.5, bf16[1024,2048]{1,0:T(8,128)(2,1)} %v_hbm.5, bf16[8,128,128]{2,1,0:T(8,128)(2,1)S(1)} %add_convert_fusion.1.refs_0_, ...), custom_call_target="tpu_custom_call" | custom-call | flops 4400000000 | bytes 13200000 | tf_op jit(solution)/shard_map/intra_block/pallas_call | solution.py:153
  43.5 2.1 %collective-permute-done.3.refs_0_ = bf16[8,128,128]{2,1,0:T(8,128)(2,1)S(1)} collective-permute-done((bf16[8,128,128]{2,1,0:T(8,128)(2,1)S(1)}, bf16[8,128,128]{2,1,0:T(8,128)(2,1)S(1)}, u32[]{:S(2)}, u32[]{:S(2)}) %collective-permute-start.3) | collective-permute-done | bytes 262176 | tf_op jit(solution)/shard_map/ppermute | solution.py:515
  45.6 0.1 add_convert_fusion
  45.8 1.3 collective-permute-start.4
  47.3 3.9 %collective-permute-done.4 = bf16[8,128,128]{2,1,0:T(8,128)(2,1)S(1)} collective-permute-done((bf16[8,128,128]{2,1,0:T(8,128)(2,1)S(1)}, bf16[8,128,128]{2,1,0:T(8,128)(2,1)S(1)}, u32[]{:S(2)}, u32[]{:S(2)}) %collective-permute-start.4) | collective-permute-done | bytes 262176 | tf_op jit(solution)/shard_map/ppermute | solution.py:515
  51.6 4.4 %collective-permute-start.12 = (bf16[2048,128]{1,0:T(8,128)(2,1)S(1)}, bf16[2048,128]{1,0:T(8,128)(2,1)S(1)}, u32[]{:S(2)}, u32[]{:S(2)}) collective-permute-start(bf16[2048,128]{1,0:T(8,128)(2,1)S(1)} %gate.28), channel_id=1, source_target_pairs={{4,0},{8,12},{5,1},{9,13},{6,2},{10,14},{7,3},{11,15},{20,16},{24,... | collective-permute-start | bytes 1572872 | tf_op jit(solution)/shard_map/ppermute | solution.py:534
  56.0 1.6 collective-permute-start.17
  57.6 4.2 %norm_part.2 = (bf16[1024,2048]{1,0:T(8,128)(2,1)S(1)}, f32[8,128]{1,0:T(8,128)}) custom-call(s32[4]{0:T(128)S(1)} %pad_add_fusion.place, bf16[1024,2048]{1,0:T(8,128)(2,1)S(1)} %copy-done, f32[1024,1024]{1,0:T(8,128)S(1)} %copy-done.3, bf16[8,128,128]{2,1,0:T(8,128)(2,1)S(1)} %add.45.p_ref.refs_1_, f32[16,1,128]{2,1,0:T(1,128)S(1)} %bitcast.7, ...), custom_call_target="tpu_custom_call" | custom-call | flops 1800000000 | bytes 5400000 | tf_op jit(solution)/shard_map/norm_part/pallas_call | solution.py:214
  61.8 4.2 %norm_part.3 = (bf16[1024,2048]{1,0:T(8,128)(2,1)S(1)}, f32[8,128]{1,0:T(8,128)}) custom-call(s32[4]{0:T(128)S(1)} %pad_add_fusion.place, bf16[1024,2048]{1,0:T(8,128)(2,1)S(1)} %copy-done, f32[1024,1024]{1,0:T(8,128)S(1)} %get-tuple-element.36.a_ref, bf16[8,128,128]{2,1,0:T(8,128)(2,1)S(1)} %collective-permute-done.5.p_ref, ...), custom_call_target="tpu_custom_call", output_to_operand_aliasing={{0}: (6, {})} | custom-call | flops 1800000000 | bytes 5400000 | tf_op jit(solution)/shard_map/norm_part/pallas_call | solution.py:214
  66.0 3.1 %project.9.refs_1_.refs_6_ = bf16[1024,256]{1,0:T(8,128)(2,1)S(1)} custom-call(s32[4]{0:T(128)S(1)} %pad_add_fusion.place, bf16[1024,2048]{1,0:T(8,128)(2,1)S(1)} %get-tuple-element.40.x, bf16[2048,512]{1,0:T(8,128)(2,1)S(1)} %copy-done.1, bf16[2048,512]{1,0:T(8,128)(2,1)} %collective-permute-done.2.refs_1_, ...), custom_call_target="tpu_custom_call" | custom-call | flops 4000000000 | bytes 12000000 | tf_op jit(solution)/shard_map/project/pallas_call | solution.py:396
  69.1 2.1 %collective-permute-start.21 = (bf16[2048,128]{1,0:T(8,128)(2,1)S(1)}, bf16[2048,128]{1,0:T(8,128)(2,1)S(1)}, u32[]{:S(2)}, u32[]{:S(2)}) collective-permute-start(bf16[2048,128]{1,0:T(8,128)(2,1)S(1)} %gate.25), channel_id=1, source_target_pairs={{4,8},{8,4},{5,9},{9,5},{6,10},{10,6},{7,11},{11,7},{20,24},{24,20... | collective-permute-start | bytes 1572872 | tf_op jit(solution)/shard_map/ppermute | solution.py:534
  71.4 0.7 collective-permute-start.20
  72.1 0.2 collective-permute-start.15
  72.3 10.6 %collective-permute-done.9.refs_0_.refs_7_ = bf16[2048,128]{1,0:T(8,128)(2,1)S(1)} collective-permute-done((bf16[2048,128]{1,0:T(8,128)(2,1)S(1)}, bf16[2048,128]{1,0:T(8,128)(2,1)S(1)}, u32[]{:S(2)}, u32[]{:S(2)}) %collective-permute-start.9) | collective-permute-done | bytes 524320 | tf_op jit(solution)/shard_map/ppermute | solution.py:534
  82.9 0.5 collective-permute-start.13
  83.5 1.3 collective-permute-done.21.refs_6_
  84.8 4.4 %project.10 = (bf16[1024,256]{1,0:T(8,128)(2,1)S(1)}, f32[1024,256]{1,0:T(8,128)S(1)}) custom-call(s32[4]{0:T(128)S(1)} %pad_add_fusion.place, bf16[1024,2048]{1,0:T(8,128)(2,1)S(1)} %get-tuple-element.40.x, bf16[2048,512]{1,0:T(8,128)(2,1)S(1)} %copy-done.1, bf16[2048,512]{1,0:T(8,128)(2,1)} %collective-permute-done.2.refs_1_, ...), custom_call_target="tpu_custom_call" | custom-call | flops 4000000000 | bytes 12000000 | tf_op jit(solution)/shard_map/project/pallas_call | solution.py:396
  89.2 1.3 collective-permute-start.25
  90.6 1.9 %collective-permute-start.23 = (bf16[2048,128]{1,0:T(8,128)(2,1)S(1)}, bf16[2048,128]{1,0:T(8,128)(2,1)S(1)}, u32[]{:S(2)}, u32[]{:S(2)}) collective-permute-start(bf16[2048,128]{1,0:T(8,128)(2,1)S(1)} %gate.34), channel_id=1, source_target_pairs={{4,8},{8,4},{5,9},{9,5},{6,10},{10,6},{7,11},{11,7},{20,24},{24,20... | collective-permute-start | bytes 1572872 | tf_op jit(solution)/shard_map/ppermute | solution.py:534
  92.5 2.3 %project.11.refs_4_ = f32[1024,256]{1,0:T(8,128)S(1)} custom-call(s32[4]{0:T(128)S(1)} %pad_add_fusion.place, bf16[1024,2048]{1,0:T(8,128)(2,1)S(1)} %get-tuple-element.40.x, bf16[2048,512]{1,0:T(8,128)(2,1)S(1)} %copy-done.1, bf16[2048,512]{1,0:T(8,128)(2,1)} %collective-permute-done.2.refs_1_, bf16[2048,128]{1,0:T(8,128)(2,1)S(1)} %broadcast_select_fusion.3.refs_2_, ...), custom_call_target="tpu_custom_call" | custom-call | flops 4000000000 | bytes 12000000 | tf_op jit(solution)/shard_map/project/pallas_call | solution.py:396
  94.8 1.0 collective-permute-done.13.refs_1_.refs_8_.refs_2_
  95.8 3.8 %project.12 = (bf16[1024,256]{1,0:T(8,128)(2,1)S(1)}, f32[1024,256]{1,0:T(8,128)S(1)}, bf16[1024,2048]{1,0:T(8,128)(2,1)}) custom-call(s32[4]{0:T(128)S(1)} %pad_add_fusion.place, bf16[1024,2048]{1,0:T(8,128)(2,1)S(1)} %get-tuple-element.40.x, bf16[2048,128]{1,0:T(8,128)(2,1)S(1)} %gate.31.refs_0_, bf16[2048,128]{1,0:T(8,128)(2,1)S(1)} %collective-permute-done.15.refs_1_, ...), custom_call_target="tpu_custom_call" | custom-call | flops 4000000000 | bytes 12000000 | tf_op jit(solution)/shard_map/project/pallas_call | solution.py:396
  99.6 0.6 collective-permute-start.14
  100.2 0.5 collective-permute-start.30
  100.7 1.9 %collective-permute-done.25.refs_6_ = bf16[2048,128]{1,0:T(8,128)(2,1)S(1)} collective-permute-done((bf16[2048,128]{1,0:T(8,128)(2,1)S(1)}, bf16[2048,128]{1,0:T(8,128)(2,1)S(1)}, u32[]{:S(2)}, u32[]{:S(2)}) %collective-permute-start.25) | collective-permute-done | bytes 524320 | tf_op jit(solution)/shard_map/ppermute | solution.py:534
  102.7 4.2 %collective-permute-done.23.refs_7_ = bf16[2048,128]{1,0:T(8,128)(2,1)S(1)} collective-permute-done((bf16[2048,128]{1,0:T(8,128)(2,1)S(1)}, bf16[2048,128]{1,0:T(8,128)(2,1)S(1)}, u32[]{:S(2)}, u32[]{:S(2)}) %collective-permute-start.23) | collective-permute-done | bytes 524320 | tf_op jit(solution)/shard_map/ppermute | solution.py:534
  106.8 1.3 collective-permute-start.24
  108.3 4.8 %collective-permute-done.14.refs_0_.refs_1_.refs_8_ = bf16[2048,128]{1,0:T(8,128)(2,1)S(1)} collective-permute-done((bf16[2048,128]{1,0:T(8,128)(2,1)S(1)}, bf16[2048,128]{1,0:T(8,128)(2,1)S(1)}, u32[]{:S(2)}, u32[]{:S(2)}) %collective-permute-start.14) | collective-permute-done | bytes 524320 | tf_op jit(solution)/shard_map/ppermute | solution.py:459
  113.1 1.5 collective-permute-start.36
  114.6 0.5 collective-permute-start.35
  115.1 2.4 %collective-permute-done.32.refs_5_ = bf16[1024,256]{1,0:T(8,128)(2,1)S(1)} collective-permute-done((bf16[1024,256]{1,0:T(8,128)(2,1)S(1)}, bf16[1024,256]{1,0:T(8,128)(2,1)S(1)}, u32[]{:S(2)}, u32[]{:S(2)}) %collective-permute-start.32) | collective-permute-done | bytes 524320 | tf_op jit(solution)/shard_map/ppermute | solution.py:463
  117.5 0.9 collective-permute-start.26
  118.4 4.1 %project.13 = (bf16[1024,256]{1,0:T(8,128)(2,1)S(1)}, f32[1024,256]{1,0:T(8,128)S(1)}, bf16[1024,2048]{1,0:T(8,128)(2,1)}) custom-call(s32[4]{0:T(128)S(1)} %pad_add_fusion.place, bf16[1024,2048]{1,0:T(8,128)(2,1)S(1)} %get-tuple-element.40.x, bf16[2048,128]{1,0:T(8,128)(2,1)S(1)} %gate.38.refs_0_, ...), custom_call_target="tpu_custom_call", output_to_operand_aliasing={{2}: (12, {})} | custom-call | flops 4000000000 | bytes 12000000 | tf_op jit(solution)/shard_map/project/pallas_call | solution.py:396
  122.7 6.0 %collective-permute-done.36.refs_5_ = bf16[1024,256]{1,0:T(8,128)(2,1)S(1)} collective-permute-done((bf16[1024,256]{1,0:T(8,128)(2,1)S(1)}, bf16[1024,256]{1,0:T(8,128)(2,1)S(1)}, u32[]{:S(2)}, u32[]{:S(2)}) %collective-permute-start.36) | collective-permute-done | bytes 524320 | tf_op jit(solution)/shard_map/ppermute | solution.py:463
  128.7 0.6 collective-permute-done.26.refs_1_.refs_6_.refs_2_
  129.4 0.9 collective-permute-start.27
  130.3 4.5 %project.14 = (bf16[1024,256]{1,0:T(8,128)(2,1)S(1)}, f32[1024,256]{1,0:T(8,128)S(1)}, bf16[1024,2048]{1,0:T(8,128)(2,1)}) custom-call(s32[4]{0:T(128)S(1)} %pad_add_fusion.place, bf16[1024,2048]{1,0:T(8,128)(2,1)S(1)} %get-tuple-element.40.x, bf16[2048,512]{1,0:T(8,128)(2,1)S(1)} %copy-done.1, ...), custom_call_target="tpu_custom_call", output_to_operand_aliasing={{2}: (12, {})} | custom-call | flops 4000000000 | bytes 12000000 | tf_op jit(solution)/shard_map/project/pallas_call | solution.py:396
  134.8 5.1 %collective-permute-done.33.refs_5_ = bf16[1024,256]{1,0:T(8,128)(2,1)S(1)} collective-permute-done((bf16[1024,256]{1,0:T(8,128)(2,1)S(1)}, bf16[1024,256]{1,0:T(8,128)(2,1)S(1)}, u32[]{:S(2)}, u32[]{:S(2)}) %collective-permute-start.33) | collective-permute-done | bytes 524320 | tf_op jit(solution)/shard_map/ppermute | solution.py:463
  139.9 4.5 %project.15 = (bf16[1024,256]{1,0:T(8,128)(2,1)S(1)}, f32[1024,256]{1,0:T(8,128)S(1)}, bf16[1024,2048]{1,0:T(8,128)(2,1)}) custom-call(s32[4]{0:T(128)S(1)} %pad_add_fusion.place, bf16[1024,2048]{1,0:T(8,128)(2,1)S(1)} %get-tuple-element.40.x, bf16[2048,512]{1,0:T(8,128)(2,1)S(1)} %copy-done.1, ...), custom_call_target="tpu_custom_call", output_to_operand_aliasing={{2}: (11, {})} | custom-call | flops 4000000000 | bytes 12000000 | tf_op jit(solution)/shard_map/project/pallas_call | solution.py:396
  144.6 6.6 %collective-permute-done.39.refs_5_ = bf16[1024,256]{1,0:T(8,128)(2,1)S(1)} collective-permute-done((bf16[1024,256]{1,0:T(8,128)(2,1)S(1)}, bf16[1024,256]{1,0:T(8,128)(2,1)S(1)}, u32[]{:S(2)}, u32[]{:S(2)}) %collective-permute-start.39) | collective-permute-done | bytes 524320 | tf_op jit(solution)/shard_map/ppermute | solution.py:463
  151.2 3.8 %project.16 = (bf16[1024,256]{1,0:T(8,128)(2,1)S(1)}, f32[1024,256]{1,0:T(8,128)S(1)}, bf16[1024,2048]{1,0:T(8,128)(2,1)}) custom-call(s32[4]{0:T(128)S(1)} %pad_add_fusion.place, bf16[1024,2048]{1,0:T(8,128)(2,1)S(1)} %get-tuple-element.40.x, bf16[2048,128]{1,0:T(8,128)(2,1)S(1)} %gate.39.refs_0_, ...), custom_call_target="tpu_custom_call", output_to_operand_aliasing={{2}: (10, {})} | custom-call | flops 4000000000 | bytes 12000000 | tf_op jit(solution)/shard_map/project/pallas_call | solution.py:396
  155.0 0.8 collective-permute-start.41
  155.8 6.6 %collective-permute-done.38.refs_5_ = bf16[1024,256]{1,0:T(8,128)(2,1)S(1)} collective-permute-done((bf16[1024,256]{1,0:T(8,128)(2,1)S(1)}, bf16[1024,256]{1,0:T(8,128)(2,1)S(1)}, u32[]{:S(2)}, u32[]{:S(2)}) %collective-permute-start.38) | collective-permute-done | bytes 524320 | tf_op jit(solution)/shard_map/ppermute | solution.py:463
  162.4 3.8 %project.17 = (bf16[1024,256]{1,0:T(8,128)(2,1)S(1)}, f32[1024,256]{1,0:T(8,128)S(1)}, bf16[1024,2048]{1,0:T(8,128)(2,1)}) custom-call(s32[4]{0:T(128)S(1)} %pad_add_fusion.place, bf16[1024,2048]{1,0:T(8,128)(2,1)S(1)} %get-tuple-element.40.x, bf16[2048,128]{1,0:T(8,128)(2,1)S(1)} %gate.33.refs_0_, ...), custom_call_target="tpu_custom_call", output_to_operand_aliasing={{2}: (9, {})} | custom-call | flops 4000000000 | bytes 12000000 | tf_op jit(solution)/shard_map/project/pallas_call | solution.py:396
  166.2 0.8 collective-permute-start.40
  167.0 6.6 %collective-permute-done.41.refs_1_ = bf16[1024,256]{1,0:T(8,128)(2,1)S(1)} collective-permute-done((bf16[1024,256]{1,0:T(8,128)(2,1)S(1)}, bf16[1024,256]{1,0:T(8,128)(2,1)S(1)}, u32[]{:S(2)}, u32[]{:S(2)}) %collective-permute-start.41) | collective-permute-done | bytes 524320 | tf_op jit(solution)/shard_map/ppermute | solution.py:463
  173.6 1.6 combine.2.refs_2_
  175.2 8.6 %collective-permute-done.40.refs_1_ = bf16[1024,256]{1,0:T(8,128)(2,1)S(1)} collective-permute-done((bf16[1024,256]{1,0:T(8,128)(2,1)S(1)}, bf16[1024,256]{1,0:T(8,128)(2,1)S(1)}, u32[]{:S(2)}, u32[]{:S(2)}) %collective-permute-start.40) | collective-permute-done | bytes 524320 | tf_op jit(solution)/shard_map/ppermute | solution.py:463
  183.8 1.6 combine.3
  (89 shorter events, 1.5 us)
Async XLA Ops:
  0.0 34.7 %collective-permute-start.2 = (bf16[2048,512]{1,0:T(8,128)(2,1)}, bf16[2048,512]{1,0:T(8,128)(2,1)}, u32[]{:S(2)}, u32[]{:S(2)}) collective-permute-start(bf16[2048,512]{1,0:T(8,128)(2,1)} %refs_0_.9), channel_id=1, source_target_pairs={{0,1},{1,0},{2,3},{3,2},{4,5},{5,4},{6,7},{7,6},{8,9},{9,8},{10,11... | collective-permute-start | bytes 6291464 | tf_op jit(solution)/shard_map/ppermute | solution.py:459
  1.9 6.5 %copy-start.6 = (bf16[2048,128]{1,0:T(8,128)(2,1)S(1)}, bf16[2048,128]{1,0:T(8,128)(2,1)}, u32[]{:S(2)}) copy-start(bf16[2048,128]{1,0:T(8,128)(2,1)} %constant_dynamic-slice_fusion.1.refs_0_) | copy-start | bytes 1572868
  7.9 3.0 %collective-permute-start = (bf16[16,128,128]{2,1,0:T(8,128)(2,1)}, bf16[16,128,128]{2,1,0:T(8,128)(2,1)S(1)}, u32[]{:S(2)}, u32[]{:S(2)}) collective-permute-start(bf16[16,128,128]{2,1,0:T(8,128)(2,1)} %get-tuple-element.34), channel_id=1, source_target_pairs={{0,1},{1,0},{2,3},{3,2},{4,5},{5,4},{6,7},{7,6},{8,9},{9,8},{10,11... | collective-permute-start | bytes 1572872 | tf_op jit(solution)/shard_map/ppermute | solution.py:459
  8.4 22.4 %collective-permute-start.6 = (bf16[2048,128]{1,0:T(8,128)(2,1)S(1)}, bf16[2048,128]{1,0:T(8,128)(2,1)S(1)}, u32[]{:S(2)}, u32[]{:S(2)}) collective-permute-start(bf16[2048,128]{1,0:T(8,128)(2,1)S(1)} %copy-done.6), channel_id=1, source_target_pairs={{4,8},{8,4},{5,9},{9,5},{6,10},{10,6},{7,11},{11,7},{20,24},{24,20... | collective-permute-start | bytes 1572872 | tf_op jit(solution)/shard_map/ppermute | solution.py:534
  10.7 13.6 %collective-permute-start.10 = (bf16[2048,128]{1,0:T(8,128)(2,1)S(1)}, bf16[2048,128]{1,0:T(8,128)(2,1)S(1)}, u32[]{:S(2)}, u32[]{:S(2)}) collective-permute-start(bf16[2048,128]{1,0:T(8,128)(2,1)S(1)} %copy-done.6), channel_id=1, source_target_pairs={{0,4},{4,0},{8,12},{12,8},{1,5},{5,1},{9,13},{13,9},{2,6},{6,2},{1... | collective-permute-start | bytes 1572872 | tf_op jit(solution)/shard_map/ppermute | solution.py:534
  12.7 19.4 %collective-permute-start.1 = (bf16[8,128,128]{2,1,0:T(8,128)(2,1)}, bf16[8,128,128]{2,1,0:T(8,128)(2,1)S(1)}, u32[]{:S(2)}, u32[]{:S(2)}) collective-permute-start(bf16[8,128,128]{2,1,0:T(8,128)(2,1)} %fusion.refs_0_), channel_id=1, source_target_pairs={{0,4},{1,5},{2,6},{3,7},{16,20},{17,21},{18,22},{19,23}} | collective-permute-start | bytes 786440 | tf_op jit(solution)/shard_map/ppermute | solution.py:515
  22.1 2.0 %copy-start.2 = (f32[1024,1024]{1,0:T(8,128)}, f32[1024,1024]{1,0:T(8,128)S(1)}, u32[]{:S(2)}) copy-start(f32[1024,1024]{1,0:T(8,128)S(1)} %get-tuple-element.38.a_ref) | copy-start | bytes 12582916
  24.4 27.1 %collective-permute-start.11 = (bf16[2048,128]{1,0:T(8,128)(2,1)S(1)}, bf16[2048,128]{1,0:T(8,128)(2,1)S(1)}, u32[]{:S(2)}, u32[]{:S(2)}) collective-permute-start(bf16[2048,128]{1,0:T(8,128)(2,1)S(1)} %gate.26.refs_0_), channel_id=1, source_target_pairs={{4,8},{8,4},{5,9},{9,5},{6,10},{10,6},{7,11},{11,7},{20,24},{24,20... | collective-permute-start | bytes 1572872 | tf_op jit(solution)/shard_map/ppermute | solution.py:534
  29.1 42.2 %collective-permute-start.19 = (bf16[2048,128]{1,0:T(8,128)(2,1)S(1)}, bf16[2048,128]{1,0:T(8,128)(2,1)S(1)}, u32[]{:S(2)}, u32[]{:S(2)}) collective-permute-start(bf16[2048,128]{1,0:T(8,128)(2,1)S(1)} %gate.26.refs_0_), channel_id=1, source_target_pairs={{0,16},{16,0},{1,17},{17,1},{2,18},{18,2},{3,19},{19,3},{4,20},{20... | collective-permute-start | bytes 1572872 | tf_op jit(solution)/shard_map/ppermute | solution.py:459
  30.8 16.3 %collective-permute-start.7 = (bf16[2048,128]{1,0:T(8,128)(2,1)S(1)}, bf16[2048,128]{1,0:T(8,128)(2,1)S(1)}, u32[]{:S(2)}, u32[]{:S(2)}) collective-permute-start(bf16[2048,128]{1,0:T(8,128)(2,1)S(1)} %gate.23), channel_id=1, source_target_pairs={{4,0},{8,12},{5,1},{9,13},{6,2},{10,14},{7,3},{11,15},{20,16},{24,... | collective-permute-start | bytes 1572872 | tf_op jit(solution)/shard_map/ppermute | solution.py:534
  33.3 12.3 %copy-start.5 = (f32[16,128,128]{2,1,0:T(8,128)S(1)}, f32[16,128,128]{2,1,0:T(8,128)}, u32[]{:S(2)}) copy-start(f32[16,128,128]{2,1,0:T(8,128)} %get-tuple-element.33) | copy-start | bytes 3145732
  33.3 12.3 %collective-permute-start.3 = (bf16[8,128,128]{2,1,0:T(8,128)(2,1)S(1)}, bf16[8,128,128]{2,1,0:T(8,128)(2,1)S(1)}, u32[]{:S(2)}, u32[]{:S(2)}) collective-permute-start(bf16[8,128,128]{2,1,0:T(8,128)(2,1)S(1)} %add_convert_fusion.1.refs_0_), channel_id=1, source_target_pairs={{4,8},{5,9},{6,10},{7,11},{20,24},{21,25},{22,26},{23,27}} | collective-permute-start | bytes 786440 | tf_op jit(solution)/shard_map/ppermute | solution.py:515
  43.4 7.9 %copy-start.1 = (bf16[2048,512]{1,0:T(8,128)(2,1)S(1)}, bf16[2048,512]{1,0:T(8,128)(2,1)}, u32[]{:S(2)}) copy-start(bf16[2048,512]{1,0:T(8,128)(2,1)} %refs_0_.9) | copy-start | bytes 6291460
  45.8 5.4 %collective-permute-start.4 = (bf16[8,128,128]{2,1,0:T(8,128)(2,1)S(1)}, bf16[8,128,128]{2,1,0:T(8,128)(2,1)S(1)}, u32[]{:S(2)}, u32[]{:S(2)}) collective-permute-start(bf16[8,128,128]{2,1,0:T(8,128)(2,1)S(1)} %get-tuple-element.61), channel_id=1, source_target_pairs={{8,12},{9,13},{10,14},{11,15},{24,28},{25,29},{26,30},{27,31}} | collective-permute-start | bytes 786440 | tf_op jit(solution)/shard_map/ppermute | solution.py:515
  47.1 10.5 %copy-start.3 = (f32[1024,1024]{1,0:T(8,128)S(1)}, f32[1024,1024]{1,0:T(8,128)}, u32[]{:S(2)}) copy-start(f32[1024,1024]{1,0:T(8,128)} %copy-done.2) | copy-start | bytes 12582916
  47.2 10.4 %copy-start = (bf16[1024,2048]{1,0:T(8,128)(2,1)S(1)}, bf16[1024,2048]{1,0:T(8,128)(2,1)}, u32[]{:S(2)}) copy-start(bf16[1024,2048]{1,0:T(8,128)(2,1)} %q_ref.3) | copy-start | bytes 12582916
  47.2 10.4 %copy-start.4 = (f32[2048]{0:T(1024)S(1)}, f32[2048]{0:T(1024)}, u32[]{:S(2)}) copy-start(f32[2048]{0:T(1024)} %param.9) | copy-start | bytes 24580
  47.2 18.8 %collective-permute-start.8 = (bf16[2048,128]{1,0:T(8,128)(2,1)S(1)}, bf16[2048,128]{1,0:T(8,128)(2,1)S(1)}, u32[]{:S(2)}, u32[]{:S(2)}) collective-permute-start(bf16[2048,128]{1,0:T(8,128)(2,1)S(1)} %broadcast_select_fusion.3.refs_2_), channel_id=1, source_target_pairs={{0,1},{1,0},{2,3},{3,2},{4,5},{5,4},{6,7},{7,6},{8,9},{9,8},{10,11... | collective-permute-start | bytes 1572872 | tf_op jit(solution)/shard_map/ppermute | solution.py:459
  51.3 10.5 %collective-permute-start.5 = (bf16[8,128,128]{2,1,0:T(8,128)(2,1)S(1)}, bf16[8,128,128]{2,1,0:T(8,128)(2,1)S(1)}, u32[]{:S(2)}, u32[]{:S(2)}) collective-permute-start(bf16[8,128,128]{2,1,0:T(8,128)(2,1)S(1)} %add.45.p_ref.refs_1_), channel_id=1, source_target_pairs={{0,1},{1,0},{2,3},{3,2},{4,5},{5,4},{6,7},{7,6},{8,9},{9,8},{10,11... | collective-permute-start | bytes 786440 | tf_op jit(solution)/shard_map/ppermute | solution.py:459
  51.6 20.5 %collective-permute-start.12 = (bf16[2048,128]{1,0:T(8,128)(2,1)S(1)}, bf16[2048,128]{1,0:T(8,128)(2,1)S(1)}, u32[]{:S(2)}, u32[]{:S(2)}) collective-permute-start(bf16[2048,128]{1,0:T(8,128)(2,1)S(1)} %gate.28), channel_id=1, source_target_pairs={{4,0},{8,12},{5,1},{9,13},{6,2},{10,14},{7,3},{11,15},{20,16},{24,... | collective-permute-start | bytes 1572872 | tf_op jit(solution)/shard_map/ppermute | solution.py:534
  56.0 15.3 %collective-permute-start.17 = (bf16[2048,128]{1,0:T(8,128)(2,1)S(1)}, bf16[2048,128]{1,0:T(8,128)(2,1)S(1)}, u32[]{:S(2)}, u32[]{:S(2)}) collective-permute-start(bf16[2048,128]{1,0:T(8,128)(2,1)S(1)} %gate.32), channel_id=1, source_target_pairs={{0,16},{16,0},{1,17},{17,1},{2,18},{18,2},{3,19},{19,3},{4,20},{20... | collective-permute-start | bytes 1572872 | tf_op jit(solution)/shard_map/ppermute | solution.py:459
  69.1 13.8 %collective-permute-start.9 = (bf16[2048,128]{1,0:T(8,128)(2,1)S(1)}, bf16[2048,128]{1,0:T(8,128)(2,1)S(1)}, u32[]{:S(2)}, u32[]{:S(2)}) collective-permute-start(bf16[2048,128]{1,0:T(8,128)(2,1)S(1)} %gate.25), channel_id=1, source_target_pairs={{0,4},{4,0},{8,12},{12,8},{1,5},{5,1},{9,13},{13,9},{2,6},{6,2},{1... | collective-permute-start | bytes 1572872 | tf_op jit(solution)/shard_map/ppermute | solution.py:534
  69.1 15.6 %collective-permute-start.21 = (bf16[2048,128]{1,0:T(8,128)(2,1)S(1)}, bf16[2048,128]{1,0:T(8,128)(2,1)S(1)}, u32[]{:S(2)}, u32[]{:S(2)}) collective-permute-start(bf16[2048,128]{1,0:T(8,128)(2,1)S(1)} %gate.25), channel_id=1, source_target_pairs={{4,8},{8,4},{5,9},{9,5},{6,10},{10,6},{7,11},{11,7},{20,24},{24,20... | collective-permute-start | bytes 1572872 | tf_op jit(solution)/shard_map/ppermute | solution.py:534
  71.3 13.6 %collective-permute-start.18 = (bf16[2048,128]{1,0:T(8,128)(2,1)S(1)}, bf16[2048,128]{1,0:T(8,128)(2,1)S(1)}, u32[]{:S(2)}, u32[]{:S(2)}) collective-permute-start(bf16[2048,128]{1,0:T(8,128)(2,1)S(1)} %collective-permute-done.17.refs_2_), channel_id=1, source_target_pairs={{0,1},{1,0},{2,3},{3,2},{4,5},{5,4},{6,7},{7,6},{8,9},{9,8},{10,11... | collective-permute-start | bytes 1572872 | tf_op jit(solution)/shard_map/ppermute | solution.py:459
  71.4 23.4 %collective-permute-start.20 = (bf16[1024,256]{1,0:T(8,128)(2,1)S(1)}, bf16[1024,256]{1,0:T(8,128)(2,1)S(1)}, u32[]{:S(2)}, u32[]{:S(2)}) collective-permute-start(bf16[1024,256]{1,0:T(8,128)(2,1)S(1)} %project.9.refs_1_.refs_6_), channel_id=1, source_target_pairs={{0,2},{2,0},{1,3},{3,1},{4,6},{6,4},{5,7},{7,5},{8,10},{10,8},{9,1... | collective-permute-start | bytes 1572872 | tf_op jit(solution)/shard_map/ppermute | solution.py:463
  72.1 18.5 %collective-permute-start.15 = (bf16[2048,128]{1,0:T(8,128)(2,1)S(1)}, bf16[2048,128]{1,0:T(8,128)(2,1)S(1)}, u32[]{:S(2)}, u32[]{:S(2)}) collective-permute-start(bf16[2048,128]{1,0:T(8,128)(2,1)S(1)} %gate.31.refs_0_), channel_id=1, source_target_pairs={{0,1},{1,0},{2,3},{3,2},{4,5},{5,4},{6,7},{7,6},{8,9},{9,8},{10,11... | collective-permute-start | bytes 1572872 | tf_op jit(solution)/shard_map/ppermute | solution.py:459
  82.9 12.9 %collective-permute-start.13 = (bf16[2048,128]{1,0:T(8,128)(2,1)S(1)}, bf16[2048,128]{1,0:T(8,128)(2,1)S(1)}, u32[]{:S(2)}, u32[]{:S(2)}) collective-permute-start(bf16[2048,128]{1,0:T(8,128)(2,1)S(1)} %gate.29.refs_2_), channel_id=1, source_target_pairs={{0,16},{16,0},{1,17},{17,1},{2,18},{18,2},{3,19},{19,3},{4,20},{20... | collective-permute-start | bytes 1572872 | tf_op jit(solution)/shard_map/ppermute | solution.py:459
  84.8 11.0 %collective-permute-start.16 = (bf16[2048,128]{1,0:T(8,128)(2,1)S(1)}, bf16[2048,128]{1,0:T(8,128)(2,1)S(1)}, u32[]{:S(2)}, u32[]{:S(2)}) collective-permute-start(bf16[2048,128]{1,0:T(8,128)(2,1)S(1)} %gate.29.refs_2_), channel_id=1, source_target_pairs={{0,1},{1,0},{2,3},{3,2},{4,5},{5,4},{6,7},{7,6},{8,9},{9,8},{10,11... | collective-permute-start | bytes 1572872 | tf_op jit(solution)/shard_map/ppermute | solution.py:459
  89.2 13.4 %collective-permute-start.25 = (bf16[2048,128]{1,0:T(8,128)(2,1)S(1)}, bf16[2048,128]{1,0:T(8,128)(2,1)S(1)}, u32[]{:S(2)}, u32[]{:S(2)}) collective-permute-start(bf16[2048,128]{1,0:T(8,128)(2,1)S(1)} %gate.35), channel_id=1, source_target_pairs={{4,0},{8,12},{5,1},{9,13},{6,2},{10,14},{7,3},{11,15},{20,16},{24,... | collective-permute-start | bytes 1572872 | tf_op jit(solution)/shard_map/ppermute | solution.py:534
  90.6 16.2 %collective-permute-start.23 = (bf16[2048,128]{1,0:T(8,128)(2,1)S(1)}, bf16[2048,128]{1,0:T(8,128)(2,1)S(1)}, u32[]{:S(2)}, u32[]{:S(2)}) collective-permute-start(bf16[2048,128]{1,0:T(8,128)(2,1)S(1)} %gate.34), channel_id=1, source_target_pairs={{4,8},{8,4},{5,9},{9,5},{6,10},{10,6},{7,11},{11,7},{20,24},{24,20... | collective-permute-start | bytes 1572872 | tf_op jit(solution)/shard_map/ppermute | solution.py:534
  99.6 13.5 %collective-permute-start.14 = (bf16[2048,128]{1,0:T(8,128)(2,1)S(1)}, bf16[2048,128]{1,0:T(8,128)(2,1)S(1)}, u32[]{:S(2)}, u32[]{:S(2)}) collective-permute-start(bf16[2048,128]{1,0:T(8,128)(2,1)S(1)} %gate.30), channel_id=1, source_target_pairs={{0,16},{16,0},{1,17},{17,1},{2,18},{18,2},{3,19},{19,3},{4,20},{20... | collective-permute-start | bytes 1572872 | tf_op jit(solution)/shard_map/ppermute | solution.py:459
  100.2 14.4 %collective-permute-start.31 = (bf16[2048,128]{1,0:T(8,128)(2,1)S(1)}, bf16[2048,128]{1,0:T(8,128)(2,1)S(1)}, u32[]{:S(2)}, u32[]{:S(2)}) collective-permute-start(bf16[2048,128]{1,0:T(8,128)(2,1)S(1)} %collective-permute-done.13.refs_1_.refs_8_.refs_2_), channel_id=1, source_target_pairs={{0,1},{1,0},{2,3},{3,2},{4,5},{5,4},{6,7},{7,6},{8,9},{9,8},{10,11... | collective-permute-start | bytes 1572872 | tf_op jit(solution)/shard_map/ppermute | solution.py:459
  100.2 14.4 %collective-permute-start.30 = (bf16[2048,128]{1,0:T(8,128)(2,1)S(1)}, bf16[2048,128]{1,0:T(8,128)(2,1)S(1)}, u32[]{:S(2)}, u32[]{:S(2)}) collective-permute-start(bf16[2048,128]{1,0:T(8,128)(2,1)S(1)} %gate.38.refs_0_), channel_id=1, source_target_pairs={{0,1},{1,0},{2,3},{3,2},{4,5},{5,4},{6,7},{7,6},{8,9},{9,8},{10,11... | collective-permute-start | bytes 1572872 | tf_op jit(solution)/shard_map/ppermute | solution.py:459
  102.7 14.8 %collective-permute-start.32 = (bf16[1024,256]{1,0:T(8,128)(2,1)S(1)}, bf16[1024,256]{1,0:T(8,128)(2,1)S(1)}, u32[]{:S(2)}, u32[]{:S(2)}) collective-permute-start(bf16[1024,256]{1,0:T(8,128)(2,1)S(1)} %get-tuple-element.41.refs_4_.refs_9_.refs_1_), channel_id=1, source_target_pairs={{0,2},{2,0},{1,3},{3,1},{4,6},{6,4},{5,7},{7,5},{8,10},{10,8},{9,1... | collective-permute-start | bytes 1572872 | tf_op jit(solution)/shard_map/ppermute | solution.py:463
  106.8 15.6 %collective-permute-start.24 = (bf16[2048,128]{1,0:T(8,128)(2,1)S(1)}, bf16[2048,128]{1,0:T(8,128)(2,1)S(1)}, u32[]{:S(2)}, u32[]{:S(2)}) collective-permute-start(bf16[2048,128]{1,0:T(8,128)(2,1)S(1)} %collective-permute-done.23.refs_7_), channel_id=1, source_target_pairs={{4,0},{8,12},{5,1},{9,13},{6,2},{10,14},{7,3},{11,15},{20,16},{24,... | collective-permute-start | bytes 1572872 | tf_op jit(solution)/shard_map/ppermute | solution.py:534
  113.1 15.6 %collective-permute-start.36 = (bf16[1024,256]{1,0:T(8,128)(2,1)S(1)}, bf16[1024,256]{1,0:T(8,128)(2,1)S(1)}, u32[]{:S(2)}, u32[]{:S(2)}) collective-permute-start(bf16[1024,256]{1,0:T(8,128)(2,1)S(1)} %get-tuple-element.42.refs_1_.refs_9_), channel_id=1, source_target_pairs={{0,2},{2,0},{1,3},{3,1},{4,6},{6,4},{5,7},{7,5},{8,10},{10,8},{9,1... | collective-permute-start | bytes 1572872 | tf_op jit(solution)/shard_map/ppermute | solution.py:463
  114.6 8.0 %collective-permute-start.37 = (bf16[2048,128]{1,0:T(8,128)(2,1)S(1)}, bf16[2048,128]{1,0:T(8,128)(2,1)S(1)}, u32[]{:S(2)}, u32[]{:S(2)}) collective-permute-start(bf16[2048,128]{1,0:T(8,128)(2,1)S(1)} %gate.39.refs_0_), channel_id=1, source_target_pairs={{0,1},{1,0},{2,3},{3,2},{4,5},{5,4},{6,7},{7,6},{8,9},{9,8},{10,11... | collective-permute-start | bytes 1572872 | tf_op jit(solution)/shard_map/ppermute | solution.py:459
  114.6 14.8 %collective-permute-start.35 = (bf16[2048,128]{1,0:T(8,128)(2,1)S(1)}, bf16[2048,128]{1,0:T(8,128)(2,1)S(1)}, u32[]{:S(2)}, u32[]{:S(2)}) collective-permute-start(bf16[2048,128]{1,0:T(8,128)(2,1)S(1)} %broadcast_select_fusion.refs_2_), channel_id=1, source_target_pairs={{0,1},{1,0},{2,3},{3,2},{4,5},{5,4},{6,7},{7,6},{8,9},{9,8},{10,11... | collective-permute-start | bytes 1572872 | tf_op jit(solution)/shard_map/ppermute | solution.py:459
  117.5 11.9 %collective-permute-start.26 = (bf16[2048,128]{1,0:T(8,128)(2,1)S(1)}, bf16[2048,128]{1,0:T(8,128)(2,1)S(1)}, u32[]{:S(2)}, u32[]{:S(2)}) collective-permute-start(bf16[2048,128]{1,0:T(8,128)(2,1)S(1)} %gate.36), channel_id=1, source_target_pairs={{0,16},{16,0},{1,17},{17,1},{2,18},{18,2},{3,19},{19,3},{4,20},{20... | collective-permute-start | bytes 1572872 | tf_op jit(solution)/shard_map/ppermute | solution.py:459
  122.5 12.3 %collective-permute-start.22 = (bf16[2048,128]{1,0:T(8,128)(2,1)S(1)}, bf16[2048,128]{1,0:T(8,128)(2,1)S(1)}, u32[]{:S(2)}, u32[]{:S(2)}) collective-permute-start(bf16[2048,128]{1,0:T(8,128)(2,1)S(1)} %gate.33.refs_0_), channel_id=1, source_target_pairs={{0,1},{1,0},{2,3},{3,2},{4,5},{5,4},{6,7},{7,6},{8,9},{9,8},{10,11... | collective-permute-start | bytes 1572872 | tf_op jit(solution)/shard_map/ppermute | solution.py:459
  122.6 17.3 %collective-permute-start.33 = (bf16[1024,256]{1,0:T(8,128)(2,1)S(1)}, bf16[1024,256]{1,0:T(8,128)(2,1)S(1)}, u32[]{:S(2)}, u32[]{:S(2)}) collective-permute-start(bf16[1024,256]{1,0:T(8,128)(2,1)S(1)} %get-tuple-element.46.refs_9_), channel_id=1, source_target_pairs={{0,2},{2,0},{1,3},{3,1},{4,6},{6,4},{5,7},{7,5},{8,10},{10,8},{9,1... | collective-permute-start | bytes 1572872 | tf_op jit(solution)/shard_map/ppermute | solution.py:463
  128.7 11.2 %collective-permute-start.34 = (bf16[2048,128]{1,0:T(8,128)(2,1)S(1)}, bf16[2048,128]{1,0:T(8,128)(2,1)S(1)}, u32[]{:S(2)}, u32[]{:S(2)}) collective-permute-start(bf16[2048,128]{1,0:T(8,128)(2,1)S(1)} %broadcast_select_fusion.1.refs_2_), channel_id=1, source_target_pairs={{0,1},{1,0},{2,3},{3,2},{4,5},{5,4},{6,7},{7,6},{8,9},{9,8},{10,11... | collective-permute-start | bytes 1572872 | tf_op jit(solution)/shard_map/ppermute | solution.py:459
  129.3 10.6 %collective-permute-start.29 = (bf16[2048,128]{1,0:T(8,128)(2,1)S(1)}, bf16[2048,128]{1,0:T(8,128)(2,1)S(1)}, u32[]{:S(2)}, u32[]{:S(2)}) collective-permute-start(bf16[2048,128]{1,0:T(8,128)(2,1)S(1)} %collective-permute-done.26.refs_1_.refs_6_.refs_2_), channel_id=1, source_target_pairs={{0,1},{1,0},{2,3},{3,2},{4,5},{5,4},{6,7},{7,6},{8,9},{9,8},{10,11... | collective-permute-start | bytes 1572872 | tf_op jit(solution)/shard_map/ppermute | solution.py:459
  129.4 15.1 %collective-permute-start.27 = (bf16[2048,128]{1,0:T(8,128)(2,1)S(1)}, bf16[2048,128]{1,0:T(8,128)(2,1)S(1)}, u32[]{:S(2)}, u32[]{:S(2)}) collective-permute-start(bf16[2048,128]{1,0:T(8,128)(2,1)S(1)} %gate.37), channel_id=1, source_target_pairs={{0,16},{16,0},{1,17},{17,1},{2,18},{18,2},{3,19},{19,3},{4,20},{20... | collective-permute-start | bytes 1572872 | tf_op jit(solution)/shard_map/ppermute | solution.py:459
  134.8 16.4 %collective-permute-start.39 = (bf16[1024,256]{1,0:T(8,128)(2,1)S(1)}, bf16[1024,256]{1,0:T(8,128)(2,1)S(1)}, u32[]{:S(2)}, u32[]{:S(2)}) collective-permute-start(bf16[1024,256]{1,0:T(8,128)(2,1)S(1)} %get-tuple-element.49.refs_8_), channel_id=1, source_target_pairs={{0,2},{2,0},{1,3},{3,1},{4,6},{6,4},{5,7},{7,5},{8,10},{10,8},{9,1... | collective-permute-start | bytes 1572872 | tf_op jit(solution)/shard_map/ppermute | solution.py:463
  144.4 18.0 %collective-permute-start.38 = (bf16[1024,256]{1,0:T(8,128)(2,1)S(1)}, bf16[1024,256]{1,0:T(8,128)(2,1)S(1)}, u32[]{:S(2)}, u32[]{:S(2)}) collective-permute-start(bf16[1024,256]{1,0:T(8,128)(2,1)S(1)} %get-tuple-element.52.refs_7_), channel_id=1, source_target_pairs={{0,2},{2,0},{1,3},{3,1},{4,6},{6,4},{5,7},{7,5},{8,10},{10,8},{9,1... | collective-permute-start | bytes 1572872 | tf_op jit(solution)/shard_map/ppermute | solution.py:463
  144.5 17.9 %collective-permute-start.28 = (bf16[2048,128]{1,0:T(8,128)(2,1)S(1)}, bf16[2048,128]{1,0:T(8,128)(2,1)S(1)}, u32[]{:S(2)}, u32[]{:S(2)}) collective-permute-start(bf16[2048,128]{1,0:T(8,128)(2,1)S(1)} %collective-permute-done.27.refs_6_.refs_2_), channel_id=1, source_target_pairs={{0,1},{1,0},{2,3},{3,2},{4,5},{5,4},{6,7},{7,6},{8,9},{9,8},{10,11... | collective-permute-start | bytes 1572872 | tf_op jit(solution)/shard_map/ppermute | solution.py:459
  155.0 18.6 %collective-permute-start.41 = (bf16[1024,256]{1,0:T(8,128)(2,1)S(1)}, bf16[1024,256]{1,0:T(8,128)(2,1)S(1)}, u32[]{:S(2)}, u32[]{:S(2)}) collective-permute-start(bf16[1024,256]{1,0:T(8,128)(2,1)S(1)} %get-tuple-element.55.refs_6_), channel_id=1, source_target_pairs={{0,2},{2,0},{1,3},{3,1},{4,6},{6,4},{5,7},{7,5},{8,10},{10,8},{9,1... | collective-permute-start | bytes 1572872 | tf_op jit(solution)/shard_map/ppermute | solution.py:463
  166.2 17.6 %collective-permute-start.40 = (bf16[1024,256]{1,0:T(8,128)(2,1)S(1)}, bf16[1024,256]{1,0:T(8,128)(2,1)S(1)}, u32[]{:S(2)}, u32[]{:S(2)}) collective-permute-start(bf16[1024,256]{1,0:T(8,128)(2,1)S(1)} %get-tuple-element.58), channel_id=1, source_target_pairs={{0,2},{2,0},{1,3},{3,1},{4,6},{6,4},{5,7},{7,5},{8,10},{10,8},{9,1... | collective-permute-start | bytes 1572872 | tf_op jit(solution)/shard_map/ppermute | solution.py:463
